TPU v7x, 256 devices: a whole 4x4x8 slice. The times are simulated.
256 devices in a mesh: dp: 4 (over z_hi), pipe: 8 (over x, core), tensor: 8 (over y, z_lo).
Axes of the slice: x: 4, y: 4, z: 8 (z_hi: 4, z_lo: 2; z = z_hi * 2 + z_lo), core: 2. Of those that a mesh axis runs over, the one named last changes fastest.
Arguments:
- activations: bfloat16 [4096, 28672], P('dp', 'tensor'), may hold values from -6 to 6
- down_weight: bfloat16 [28672, 8192], P('tensor', 'pipe'), may hold values from -0.03125 to 0.03125
- output_grads: bfloat16 [4096, 8192], P('dp', ('pipe', 'tensor')), may hold values from -170 to 170
- act_factors: bfloat16 [64, 32, 28672], P('pipe', None, 'tensor'), may hold values from -0.03125 to 0.03125
- grad_factors: bfloat16 [64, 32, 8192], P(None, None, ('pipe', 'tensor')), may hold values from -0.0625 to 0.0625
- rank_weight: float32 [64, 32], P('pipe'), may hold values from 0.05 to 1
Outputs:
- layer_output: bfloat16 [4096, 8192], P('dp', ('pipe', 'tensor'))
- influence: float32 [4096, 64], P('dp', 'pipe')
All inputs are finite; a program needn't handle non-finite values.
Results may differ from a plain program's by a relative error of at most 0.001.
Values sent between devices are 32-bit elements; how exact they have to be, the bound alone decides.
No kernel may reach another device: no remote copies, remote signals or barrier semaphores. Data moves between devices by JAX's collectives and lax.ppermute only.
A program may use at most 128 MiB of HBM per device.

v0:
```python
import math

import jax
import jax.numpy as jnp
from jax import lax
from jax.sharding import PartitionSpec as P


def body(activations, down_weight, output_grads, act_factors, grad_factors, rank_weight):
    tok_rows = activations.shape[0]
    partial_value = jnp.dot(activations, down_weight, preferred_element_type=jnp.float32)
    layer_output = lax.psum_scatter(
        partial_value, "tensor", scatter_dimension=1, tiled=True
    ).astype(jnp.bfloat16)
    local_queries, rank_count, hidden_width = act_factors.shape
    all_queries = grad_factors.shape[0]
    act_local = jnp.einsum(
        "tf,qrf->tqr", activations, act_factors, preferred_element_type=jnp.float32
    )
    grad_local = jnp.einsum(
        "td,qrd->tqr", output_grads, grad_factors, preferred_element_type=jnp.float32
    )
    scale_factor = 1.0 / math.sqrt(rank_count)
    act_flat = act_local.reshape(tok_rows, local_queries * rank_count)
    act_proj = lax.psum(act_flat, "tensor")
    grad_flat = grad_local.reshape(tok_rows, all_queries * rank_count)
    summed_all = lax.psum(grad_flat, ("pipe", "tensor"))
    owned_terms = lax.dynamic_slice_in_dim(
        summed_all,
        lax.axis_index("pipe") * (local_queries * rank_count),
        local_queries * rank_count,
        1,
    )
    product = (act_proj * owned_terms).reshape(tok_rows, local_queries, rank_count)
    raw_scores = jnp.sum(product * rank_weight[None, :, :], axis=2) * scale_factor
    square_sum = lax.psum(jnp.sum(raw_scores * raw_scores, axis=0), "dp")
    spread = square_sum / (tok_rows * lax.axis_size("dp"))
    influence = raw_scores / jnp.sqrt(spread + 1e-06)
    return (layer_output, influence)


def solution(mesh):
    return jax.shard_map(
        body,
        mesh=mesh,
        in_specs=(
            P("dp", "tensor"),
            P("tensor", "pipe"),
            P("dp", ("pipe", "tensor")),
            P("pipe", None, "tensor"),
            P(None, None, ("pipe", "tensor")),
            P("pipe", None),
        ),
        out_specs=(P("dp", ("pipe", "tensor")), P("dp", "pipe")),
        check_vma=False,
    )
```

profile of v0, /device:TPU:2, one launch (start us, length us, event | category | flops | bytes accessed | tf_op | source)
XLA Modules:
  0.0 823.5 jit_solution(15491009013952467567)
XLA Ops:
  7.2 0.0 copy-start
  7.2 0.0 copy-start.1
  7.2 0.0 copy-start.2
  7.2 0.0 all-reduce.3.cloned.1.call-start
  7.2 1.4 copy-done
  8.7 6.2 fusion
  14.9 0.0 all-reduce.3.cloned.1.call-update
  14.9 0.0 all-reduce.5.cloned.1.call-start
  14.9 0.0 copy-done.1
  14.9 0.0 copy-done.2
  14.9 4.5 fusion.2
  19.4 0.0 all-reduce.5.cloned.1.call-update
  19.4 0.0 copy-start.3
  19.4 0.0 reduce-scatter.2.cloned.1.call-start
  19.5 13.5 %fusion.4 = f32[1024,1024]{1,0:T(8,128)} fusion(bf16[1024,3584]{1,0:T(8,128)(2,1)} %param.6, bf16[3584,1024]{1,0:T(8,128)(2,1)} %param.7), kind=kOutput, calls=%fused_computation.9 | convolution fusion | flops 7516192768 | bytes 18874368 | tf_op jit(solution)/shard_map/dot_general | solution.py:11
  33.0 0.0 reduce-scatter.2.cloned.1.call-update
  33.0 70.3 %all-reduce.3.cloned.1.call-done = f32[1024,256]{0,1:T(8,128)} async-done(((f32[1024,256]{0,1:T(8,128)}), f32[1024,256]{0,1:T(8,128)}) %all-reduce.3.cloned.1.call-update) | async-done | bytes 1048592 | tf_op jit(solution)/shard_map/psum | solution.py:25
  103.3 592.9 %all-reduce.5.cloned.1.call-done = f32[1024,2048]{0,1:T(8,128)} async-done(((f32[1024,2048]{0,1:T(8,128)}), f32[1024,2048]{0,1:T(8,128)}) %all-reduce.5.cloned.1.call-update) | async-done | bytes 8388624 | tf_op jit(solution)/shard_map/psum | solution.py:27
  696.2 0.0 copy-done.3
  696.2 1.8 multiply_reduce_fusion
  698.0 0.1 multiply_reduce_fusion.1
  698.1 13.4 %psum.23 = f32[8]{0:T(128)S(1)} all-reduce(f32[8]{0:T(128)S(1)} %multiply_reduce_fusion.1), channel_id=1, replica_groups=mesh['dp'=4,'pipe'=8,'tensor'=8] {'dp'}, use_global_device_ids=true, to_apply=%region_5.0 | all-reduce | flops 8 | bytes 64 | tf_op jit(solution)/shard_map/psum | solution.py:36
  711.5 0.7 multiply_divide_fusion
  712.2 103.0 %reduce-scatter.2.cloned.1.call-done = f32[1024,128]{1,0:T(8,128)} async-done(((f32[1024,1024]{1,0:T(8,128)}), f32[1024,128]{1,0:T(8,128)}) %reduce-scatter.2.cloned.1.call-update) | async-done | bytes 524304 | tf_op jit(solution)/shard_map/reduce_scatter | solution.py:12
  815.2 1.8 convert_element_type.3
  (1 shorter events, 0.0 us)
Async XLA Ops:
  7.2 1.5 copy-start
  7.2 7.7 copy-start.1
  7.2 7.7 copy-start.2
  7.2 96.1 %all-reduce.3.cloned.1.call-start = ((), (), s32[]{:S(2)}) async-start(), calls=%async_computation.2 | async-start | bytes 2097152 | tf_op jit(solution)/shard_map/psum | solution.py:25
  14.9 681.3 %all-reduce.5.cloned.1.call-start = ((), (), s32[]{:S(2)}) async-start(), calls=%async_computation.3 | async-start | bytes 16777216 | tf_op jit(solution)/shard_map/psum | solution.py:27
  19.4 676.7 %copy-start.3 = (f32[8,32]{1,0:T(8,128)S(1)}, f32[8,32]{1,0:T(8,128)}, u32[]{:S(2)}) copy-start(f32[8,32]{1,0:T(8,128)} %param.11) | copy-start | bytes 3076
  19.4 795.8 %reduce-scatter.2.cloned.1.call-start = ((), (), s32[]{:S(2)}) async-start(), calls=%async_computation.1 | async-start | bytes 4718592 | tf_op jit(solution)/shard_map/reduce_scatter | solution.py:12
Sparse Core Ops, SparseCore 0:
  15.0 88.2 all-reduce.2
  106.0 590.1 all-reduce.4
  698.7 116.4 reduce-scatter.1
where the time goes:
time: 824 us
  waiting for transfers between devices  766 us (93%)
  matrix products  24.1 us (3%)
  between operations  13.8 us (2%)
  blocking collectives  13.4 us (2%)
    psum x1, waiting for transfers between devices, body(): summed_all = lax.psum(grad_flat, ('pipe', 'tensor'))  593 us
    reduce_scatter x1, waiting for transfers between devices, body(): lax.psum_scatter(partial_value, 'tensor', scatter_dimension=1, tiled=True)  103 us
    psum x1, waiting for transfers between devices, body(): act_proj = lax.psum(act_flat, 'tensor')  70.3 us
  transfers between devices with their start and end apart: 3, of which 3 were waited for; matrix products, arithmetic and copies ran while one was open for 2% of the time, Pallas kernels for 0%

commit v1 on v0

v1 whole, which is shorter than its diff:
```python
import functools
import math

import jax
import jax.numpy as jnp
from jax import lax
from jax.experimental import pallas as pl
from jax.experimental.pallas import tpu as pltpu
from jax.sharding import PartitionSpec as P

F32 = jnp.float32
MIB = 1 << 20


def x_shift(d):
    return [(p, ((p // 2 + d) % 4) * 2 + p % 2) for p in range(8)]


def core_swap():
    return [(p, p ^ 1) for p in range(8)]


def y_shift(d):
    return [(t, ((t // 2 + d) % 4) * 2 + t % 2) for t in range(8)]


def z_swap():
    return [(t, t ^ 1) for t in range(8)]


def dp_shift(d):
    return [(i, (i + d) % 4) for i in range(4)]


def params(limit):
    return pltpu.CompilerParams(vmem_limit_bytes=limit)


def cost(flops, nbytes):
    return pl.CostEstimate(flops=flops, bytes_accessed=nbytes, transcendentals=0)


def pack_kernel(idx, og, gf, *outs):
    tokens = og.shape[0]
    rows = gf.shape[0] // 4
    for out, d in zip(outs, (1, 3, 2)):
        out[pl.ds(0, tokens), :] = og[...].astype(F32)
        start = pl.multiple_of(lax.rem(idx[0] + d, 4) * rows, rows)
        out[pl.ds(tokens, rows), :] = gf[pl.ds(start, rows), :].astype(F32)


def pack(idx, og, gf):
    tokens, width = og.shape
    rows = tokens + gf.shape[0] // 4
    whole = pl.BlockSpec(memory_space=pltpu.VMEM)
    return pl.pallas_call(
        pack_kernel,
        grid_spec=pltpu.PrefetchScalarGridSpec(
            num_scalar_prefetch=1, grid=(), in_specs=[whole, whole], out_specs=[whole] * 3
        ),
        out_shape=[jax.ShapeDtypeStruct((rows, width), F32)] * 3,
        compiler_params=params(16 * MIB),
        cost_estimate=cost(0, 4 * 3 * rows * width),
        name="pack",
    )(idx, og, gf)


def act_kernel(idx, af, a, *rest):
    *outs, scratch = rest
    scratch[...] = lax.dot_general(
        af[...], a[...], (((1,), (1,)), ((), ())), preferred_element_type=F32
    )
    rows = outs[0].shape[0]
    for j, out in enumerate(outs):
        start = pl.multiple_of(lax.rem(idx[2] + j, 4) * rows, rows)
        out[...] = scratch[pl.ds(start, rows), :]


def act_pieces(idx, af, a):
    qr, hidden = af.shape
    tokens = a.shape[0]
    tile = 256
    return pl.pallas_call(
        act_kernel,
        grid_spec=pltpu.PrefetchScalarGridSpec(
            num_scalar_prefetch=1,
            grid=(tokens // tile,),
            in_specs=[
                pl.BlockSpec((qr, hidden), lambda i, idx: (0, 0)),
                pl.BlockSpec((tile, hidden), lambda i, idx: (i, 0)),
            ],
            out_specs=[pl.BlockSpec((qr // 4, tile), lambda i, idx: (0, i))] * 4,
            scratch_shapes=[pltpu.VMEM((qr, tile), F32)],
        ),
        out_shape=[jax.ShapeDtypeStruct((qr // 4, tokens), F32)] * 4,
        compiler_params=params(24 * MIB),
        cost_estimate=cost(2 * qr * tokens * hidden, 2 * hidden * (qr + tokens)),
        name="act",
    )(idx, af, a)


def layer_z_kernel(idx, a, w, keep, send):
    acc = jnp.dot(a[...], w[...], preferred_element_type=F32)
    half = acc.shape[1] // 2

    @pl.when(idx[3] == 0)
    def _():
        keep[0] = acc[:, :half]
        send[0] = acc[:, half:]

    @pl.when(idx[3] == 1)
    def _():
        keep[0] = acc[:, half:]
        send[0] = acc[:, :half]


def layer_z_first(idx, a, w, block, rows):
    hidden, cols = w.shape
    width = cols // 4
    return pl.pallas_call(
        layer_z_kernel,
        grid_spec=pltpu.PrefetchScalarGridSpec(
            num_scalar_prefetch=1,
            grid=(4,),
            in_specs=[
                pl.BlockSpec((rows, hidden), lambda j, idx: (block, 0)),
                pl.BlockSpec((hidden, width), lambda j, idx: (0, lax.rem(idx[2] + j, 4))),
            ],
            out_specs=[pl.BlockSpec((1, rows, width // 2), lambda j, idx: (j, 0, 0))] * 2,
        ),
        out_shape=[jax.ShapeDtypeStruct((4, rows, width // 2), F32)] * 2,
        compiler_params=params(24 * MIB),
        cost_estimate=cost(2 * rows * hidden * cols, 2 * hidden * (rows + cols)),
        name="layer_z",
    )(idx, a, w)


def layer_y_kernel(idx, a, w, *outs):
    for j, out in enumerate(outs):

        @pl.when(pl.program_id(0) == j)
        def _(out=out):
            out[...] = jnp.dot(a[...], w[...], preferred_element_type=F32)


def layer_y_first(idx, a, w, block, rows):
    hidden, cols = w.shape
    width = cols // 4
    return pl.pallas_call(
        layer_y_kernel,
        grid_spec=pltpu.PrefetchScalarGridSpec(
            num_scalar_prefetch=1,
            grid=(4,),
            in_specs=[
                pl.BlockSpec((rows, hidden), lambda j, idx: (block, 0)),
                pl.BlockSpec((hidden, width), lambda j, idx: (0, lax.rem(idx[2] + j, 4))),
            ],
            out_specs=[pl.BlockSpec((rows, width), lambda j, idx: (0, 0))] * 4,
        ),
        out_shape=[jax.ShapeDtypeStruct((rows, width), F32)] * 4,
        compiler_params=params(24 * MIB),
        cost_estimate=cost(2 * rows * hidden * cols, 2 * hidden * (rows + cols)),
        name="layer_y",
    )(idx, a, w)


def score_kernel(idx, og, gf, a1, b1, a2, b2, a3, b3, mine, other, out, *, ranks):
    bf = jnp.bfloat16
    lhs = jnp.concatenate([gf[...]] + [b[...].astype(bf) for b in (b1, b2, b3)], axis=1)
    rhs = jnp.concatenate([og[...]] + [a[...].astype(bf) for a in (a1, a2, a3)], axis=1)
    grad = lax.dot_general(lhs, rhs, (((1,), (1,)), ((), ())), preferred_element_type=F32)
    rows = mine.shape[1]
    parts = []
    for c in range(2):
        for b in range(4):
            j = lax.rem(b + 4 - idx[2], 4)
            act = jnp.where(idx[1] == c, mine[j], other[j])
            at = (c * 4 + b) * rows
            product = grad[at : at + rows, :] * act
            for q in range(rows // ranks):
                parts.append(
                    jnp.sum(product[q * ranks : (q + 1) * ranks], axis=0, keepdims=True)
                )
    out[...] = jnp.concatenate(parts, axis=0)


def scores(idx, og, gf, moved, mine, other, ranks):
    tokens, width = og.shape
    qr = gf.shape[0] // 4
    tile = 256
    first = tokens // qr
    in_specs = [
        pl.BlockSpec((tile, width), lambda i, idx: (i, 0)),
        pl.BlockSpec((qr, width), lambda i, idx: (idx[0], 0)),
    ]
    args = [og, gf]
    for m in moved:
        in_specs.append(pl.BlockSpec((tile, width), lambda i, idx: (i, 0)))
        in_specs.append(pl.BlockSpec((qr, width), lambda i, idx: (first, 0)))
        args += [m, m]
    for act in (mine, other):
        in_specs.append(pl.BlockSpec((4, act.shape[1], tile), lambda i, idx: (0, 0, i)))
        args.append(act)
    queries = qr // ranks
    return pl.pallas_call(
        functools.partial(score_kernel, ranks=ranks),
        grid_spec=pltpu.PrefetchScalarGridSpec(
            num_scalar_prefetch=1,
            grid=(tokens // tile,),
            in_specs=in_specs,
            out_specs=pl.BlockSpec((queries, tile), lambda i, idx: (0, i)),
        ),
        out_shape=jax.ShapeDtypeStruct((queries, tokens), F32),
        compiler_params=params(24 * MIB),
        cost_estimate=cost(2 * qr * tokens * width * 4, 4 * tokens * (qr + 4 * width)),
        name="scores",
    )(idx, *args)


def body(activations, down_weight, output_grads, act_factors, grad_factors, rank_weight):
    tokens = activations.shape[0]
    queries, ranks, hidden = act_factors.shape
    pipe, tensor = lax.axis_index("pipe"), lax.axis_index("tensor")
    x, core, y, z = pipe // 2, pipe % 2, tensor // 2, tensor % 2
    idx = jnp.stack([x, core, y, z]).astype(jnp.int32)

    gf = grad_factors.reshape(-1, grad_factors.shape[2])
    packed = pack(idx, output_grads, gf)
    moved = [
        lax.ppermute(p, "pipe", x_shift(d)) for p, d in zip(packed, (1, -1, 2))
    ]

    pieces = act_pieces(idx, act_factors.reshape(queries * ranks, hidden), activations)
    got = [lax.ppermute(pieces[j], "tensor", y_shift(j)) for j in (1, 3, 2)]
    own = (pieces[0] + got[2]) + (got[0] + got[1])
    own = own + lax.ppermute(own, "tensor", z_swap())
    weights = (rank_weight * (1.0 / math.sqrt(ranks))).reshape(4, -1)
    own = own * lax.dynamic_index_in_dim(weights, y, 0, keepdims=False)[:, None]
    mine = jnp.stack(
        [own] + [lax.ppermute(own, "tensor", y_shift(-j)) for j in (1, 2, 3)]
    )
    other = lax.ppermute(mine, "pipe", core_swap())

    outputs = []
    for block in range(2):
        keep, send = layer_z_first(idx, activations, down_weight, block, 384)
        total = keep + lax.ppermute(send, "tensor", z_swap())
        got = [lax.ppermute(total[j], "tensor", y_shift(j)) for j in (1, 3, 2)]
        total = (total[0] + got[2]) + (got[0] + got[1])
        outputs.append(total.astype(jnp.bfloat16))
    parts = layer_y_first(idx, activations, down_weight, 3, 256)
    got = [lax.ppermute(parts[j], "tensor", y_shift(j)) for j in (1, 3, 2)]
    total = (parts[0] + got[2]) + (got[0] + got[1])
    half = total.shape[1] // 2
    send = lax.dynamic_slice_in_dim(total, (1 - z) * half, half, 1)
    keep = lax.dynamic_slice_in_dim(total, z * half, half, 1)
    total = keep + lax.ppermute(send, "tensor", z_swap())
    outputs.append(total.astype(jnp.bfloat16))
    layer_output = jnp.concatenate(outputs, axis=0)

    share = scores(idx, output_grads, gf, moved, mine, other, ranks)
    raw = lax.dynamic_slice_in_dim(share, core * queries, queries, 0)
    send = lax.dynamic_slice_in_dim(share, (1 - core) * queries, queries, 0)
    raw = raw + lax.ppermute(send, "pipe", core_swap())
    got = [lax.ppermute(raw, "tensor", y_shift(j)) for j in (1, 3, 2)]
    raw = (raw + got[2]) + (got[0] + got[1])
    raw = raw + lax.ppermute(raw, "tensor", z_swap())

    square = jnp.sum((raw * raw).reshape(queries, -1, 128), axis=1)
    got = [lax.ppermute(square, "dp", dp_shift(j)) for j in (1, 3, 2)]
    square = (square + got[2]) + (got[0] + got[1])
    spread = jnp.sum(square, axis=1, keepdims=True) / (tokens * lax.axis_size("dp"))
    influence = raw / jnp.sqrt(spread + 1e-06)
    return (layer_output, influence.T)


def solution(mesh):
    return jax.shard_map(
        body,
        mesh=mesh,
        in_specs=(
            P("dp", "tensor"),
            P("tensor", "pipe"),
            P("dp", ("pipe", "tensor")),
            P("pipe", None, "tensor"),
            P(None, None, ("pipe", "tensor")),
            P("pipe", None),
        ),
        out_specs=(P("dp", ("pipe", "tensor")), P("dp", "pipe")),
        check_vma=False,
    )
```

time: 824 us -> 172 us (0.21)
  waiting for transfers between devices: 766 us -> 69.2 us
  starting transfers between devices: 0.12 us -> 46.3 us
  Pallas kernels: 0 us -> 24.6 us
  matrix products: 24.1 us -> 0 us
  local copies, waits for them, and re-layouts: 1.45 us -> 21.7 us
  blocking collectives: 13.4 us -> 0 us
  between operations: 13.8 us -> 0.88 us
    psum x2 -> x0, waiting for transfers between devices: 663 us -> none  [the longest x1 593 us: body(): summed_all = lax.psum(grad_flat, ('pipe', 'tensor'))]
    reduce_scatter x1 -> x0, waiting for transfers between devices: 103 us -> none  [body(): lax.psum_scatter(partial_value, 'tensor', scatter_dimension=1, tiled=True)]
    ppermute x0 -> x31, waiting for transfers between devices: none -> 69.2 us  [the longest x1 20.2 us: body(): own = own + lax.ppermute(own, 'tensor', z_swap())]
    ppermute x0 -> x31, starting transfers between devices: none -> 46.3 us  [the longest x3 10.5 us: body(): got = [lax.ppermute(square, 'dp', dp_shift(j)) for j in (1, 3, 2)]]
    pallas_call x0 -> x6, Pallas kernels: none -> 24.6 us  [the longest x2 11.1 us: layer_z_first(): pl.pallas_call(layer_z_kernel, grid_spec=pltpu.PrefetchScalarGridSpec(num...]
    dot_general x3 -> x0, matrix products: 24.1 us -> none  [the longest x1 13.5 us: body(): jnp.dot(activations, down_weight, preferred_element_type=jnp.float32)]
    unnamed x8 -> x30, local copies, waits for them, and re-layouts: 1.45 us -> 21.5 us
    psum x1 -> x0, blocking collectives: 13.4 us -> none  [body(): square_sum = lax.psum(jnp.sum(raw_scores * raw_scores, axis=0), 'dp')]
  transfers between devices with their start and end apart: 3 -> 31, of which waited for: 3 -> 10; matrix products, arithmetic and copies ran while one was open for 2% -> 4% of each run, Pallas kernels for 0% -> 12%
where the time goes in v1:
time: 172 us; the launch traced here: 170 us
  waiting for transfers between devices  69.2 us (40%)
  starting transfers between devices  46.3 us (27%)
  Pallas kernels  24.6 us (14%)
  local copies, waits for them, and re-layouts  21.7 us (13%)
  other arithmetic  6.99 us (4%)
    unnamed x30, local copies, waits for them, and re-layouts  21.5 us
    ppermute x1, waiting for transfers between devices, body(): own = own + lax.ppermute(own, 'tensor', z_swap())  20.2 us
    ppermute x3, waiting for transfers between devices, body(): lax.ppermute(p, 'pipe', x_shift(d))  16.3 us
    pallas_call x2, Pallas kernels, layer_z_first(): pl.pallas_call(layer_z_kernel, grid_spec=pltpu.PrefetchScalarGridSpec(num...  11.1 us
    ppermute x3, starting transfers between devices, body(): got = [lax.ppermute(square, 'dp', dp_shift(j)) for j in (1, 3, 2)]  10.5 us
    ppermute x3, waiting for transfers between devices, body(): total = keep + lax.ppermute(send, 'tensor', z_swap())  10.1 us
    ppermute x3, waiting for transfers between devices, body(): lax.ppermute(own, 'tensor', y_shift(-j))  7.99 us
    ppermute x6, starting transfers between devices, body(): got = [lax.ppermute(total[j], 'tensor', y_shift(j)) for j in (1, 3, 2)]  7.93 us
  transfers between devices with their start and end apart: 31, of which 10 were waited for; matrix products, arithmetic and copies ran while one was open for 4% of the time, Pallas kernels for 12%

profile of v1, /device:TPU:2, one launch (start us, length us, event | category | flops | bytes accessed | tf_op | source)
XLA Modules:
  0.0 169.7 jit_solution(1487987488944154213)
XLA Ops:
  0.7 3.1 %copy-done = bf16[1024,3584]{1,0:T(8,128)(2,1)S(1)} copy-done((bf16[1024,3584]{1,0:T(8,128)(2,1)S(1)}, bf16[1024,3584]{1,0:T(8,128)(2,1)}, u32[]{:S(2)}) %copy-start) | copy-done | bytes 7340056
  3.8 3.1 %copy-done.3 = bf16[3584,1024]{1,0:T(8,128)(2,1)S(1)} copy-done((bf16[3584,1024]{1,0:T(8,128)(2,1)S(1)}, bf16[3584,1024]{1,0:T(8,128)(2,1)}, u32[]{:S(2)}) %copy-start.3) | copy-done | bytes 7340056
  6.9 4.3 %layer_y.1 = (f32[256,256]{1,0:T(8,128)S(1)}, f32[256,256]{1,0:T(8,128)S(1)}, f32[256,256]{1,0:T(8,128)S(1)}, f32[256,256]{1,0:T(8,128)S(1)}) custom-call(s32[4]{0:T(128)S(1)} %pad_add_fusion.idx, bf16[1024,3584]{1,0:T(8,128)(2,1)S(1)} %copy-done, bf16[3584,1024]{1,0:T(8,128)(2,1)S(1)} %copy-done.3), custom_call_target="tpu_custom_call" | custom-call | flops 1879048192 | bytes 9175040 | tf_op jit(solution)/shard_map/layer_y/pallas_call | solution.py:149
  11.2 1.7 collective-permute-start.9
  12.9 1.7 collective-permute-start.10
  14.5 3.6 %act.1 = (f32[64,1024]{1,0:T(8,128)S(1)}, f32[64,1024]{1,0:T(8,128)S(1)}, f32[64,1024]{1,0:T(8,128)S(1)}, f32[64,1024]{1,0:T(8,128)S(1)}) custom-call(s32[4]{0:T(128)S(1)} %pad_add_fusion.idx, bf16[256,3584]{1,0:T(8,128)(2,1)S(1)} %bitcast.46, bf16[1024,3584]{1,0:T(8,128)(2,1)S(1)} %copy-done), custom_call_target="tpu_custom_call" | custom-call | flops 1879048192 | bytes 9175040 | tf_op jit(solution)/shard_map/act/pallas_call | solution.py:83
  18.6 2.9 %collective-permute-start.17 = (f32[64,1024]{1,0:T(8,128)S(1)}, f32[64,1024]{1,0:T(8,128)}, u32[]{:S(2)}, u32[]{:S(2)}) collective-permute-start(f32[64,1024]{1,0:T(8,128)S(1)} %get-tuple-element.31), channel_id=1, source_target_pairs={{0,6},{1,7},{2,0},{3,1},{4,2},{5,3},{6,4},{7,5},{8,14},{9,15},{10,... | collective-permute-start | bytes 786440 | tf_op jit(solution)/shard_map/ppermute | solution.py:234
  21.4 0.8 collective-permute-start.15
  22.2 3.1 %copy-done.1 = bf16[1024,3584]{1,0:T(8,128)(2,1)S(1)} copy-done((bf16[1024,3584]{1,0:T(8,128)(2,1)S(1)}, bf16[1024,3584]{1,0:T(8,128)(2,1)}, u32[]{:S(2)}) %copy-start.1) | copy-done | bytes 7340056
  25.3 3.1 %copy-done.4 = bf16[3584,1024]{1,0:T(8,128)(2,1)S(1)} copy-done((bf16[3584,1024]{1,0:T(8,128)(2,1)S(1)}, bf16[3584,1024]{1,0:T(8,128)(2,1)}, u32[]{:S(2)}) %copy-start.4) | copy-done | bytes 7340056
  28.4 5.2 %layer_z.3 = (f32[4,384,128]{2,1,0:T(8,128)S(1)}, f32[4,384,128]{2,1,0:T(8,128)S(1)}) custom-call(s32[4]{0:T(128)S(1)} %pad_add_fusion.idx, bf16[1024,3584]{1,0:T(8,128)(2,1)S(1)} %copy-done.1, bf16[3584,1024]{1,0:T(8,128)(2,1)S(1)} %copy-done.4), custom_call_target="tpu_custom_call" | custom-call | flops 2818572288 | bytes 10092544 | tf_op jit(solution)/shard_map/layer_z/pallas_call | solution.py:120
  33.6 0.9 copy-done.11
  34.5 2.8 %collective-permute-start.8 = (f32[256,256]{1,0:T(8,128)S(1)}, f32[256,256]{1,0:T(8,128)S(1)}, u32[]{:S(2)}, u32[]{:S(2)}) collective-permute-start(f32[256,256]{1,0:T(8,128)S(1)} %get-tuple-element.22), channel_id=1, source_target_pairs={{0,4},{1,5},{2,6},{3,7},{4,0},{5,1},{6,2},{7,3},{8,12},{9,13},{10,... | collective-permute-start | bytes 786440 | tf_op jit(solution)/shard_map/ppermute | solution.py:252
  37.3 2.0 %collective-permute-start.4 = (f32[4,384,128]{2,1,0:T(8,128)S(1)}, f32[4,384,128]{2,1,0:T(8,128)}, u32[]{:S(2)}, u32[]{:S(2)}) collective-permute-start(f32[4,384,128]{2,1,0:T(8,128)S(1)} %get-tuple-element.20), channel_id=1, source_target_pairs={{0,1},{1,0},{2,3},{3,2},{4,5},{5,4},{6,7},{7,6},{8,9},{9,8},{10,11... | collective-permute-start | bytes 2359304 | tf_op jit(solution)/shard_map/ppermute | solution.py:247
  39.2 1.2 add_add_fusion
  40.6 20.2 %collective-permute-done.18 = f32[64,1024]{1,0:T(8,128)S(1)} collective-permute-done((f32[64,1024]{1,0:T(8,128)S(1)}, f32[64,1024]{1,0:T(8,128)S(1)}, u32[]{:S(2)}, u32[]{:S(2)}) %collective-permute-start.18) | collective-permute-done | bytes 262176 | tf_op jit(solution)/shard_map/ppermute | solution.py:236
  61.0 1.9 %collective-permute-start.20 = (f32[64,1024]{1,0:T(8,128)S(1)}, f32[64,1024]{1,0:T(8,128)S(1)}, u32[]{:S(2)}, u32[]{:S(2)}) collective-permute-start(f32[64,1024]{1,0:T(8,128)S(1)} %add_multiply_fusion), channel_id=1, source_target_pairs={{0,4},{1,5},{2,6},{3,7},{4,0},{5,1},{6,2},{7,3},{8,12},{9,13},{10,... | collective-permute-start | bytes 786440 | tf_op jit(solution)/shard_map/ppermute | solution.py:240
  62.9 1.4 collective-permute-start.19
  64.5 1.8 %collective-permute-start.11 = (f32[256,128]{1,0:T(8,128)S(1)}, f32[256,128]{1,0:T(8,128)S(1)}, u32[]{:S(2)}, u32[]{:S(2)}) collective-permute-start(f32[256,128]{1,0:T(8,128)S(1)} %constant_dynamic-slice_fusion.2), channel_id=1, source_target_pairs={{0,1},{1,0},{2,3},{3,2},{4,5},{5,4},{6,7},{7,6},{8,9},{9,8},{10,11... | collective-permute-start | bytes 393224 | tf_op jit(solution)/shard_map/ppermute | solution.py:257
  66.3 7.4 %collective-permute-done.21 = f32[64,1024]{1,0:T(8,128)S(1)} collective-permute-done((f32[64,1024]{1,0:T(8,128)S(1)}, f32[64,1024]{1,0:T(8,128)S(1)}, u32[]{:S(2)}, u32[]{:S(2)}) %collective-permute-start.21) | collective-permute-done | bytes 262176 | tf_op jit(solution)/shard_map/ppermute | solution.py:240
  74.7 3.1 %copy-done.2 = bf16[1024,3584]{1,0:T(8,128)(2,1)S(1)} copy-done((bf16[1024,3584]{1,0:T(8,128)(2,1)S(1)}, bf16[1024,3584]{1,0:T(8,128)(2,1)}, u32[]{:S(2)}) %copy-start.2) | copy-done | bytes 7340056
  77.8 3.1 %copy-done.5 = bf16[3584,1024]{1,0:T(8,128)(2,1)S(1)} copy-done((bf16[3584,1024]{1,0:T(8,128)(2,1)S(1)}, bf16[3584,1024]{1,0:T(8,128)(2,1)}, u32[]{:S(2)}) %copy-start.5) | copy-done | bytes 7340056
  80.9 5.9 %layer_z.2 = (f32[4,384,128]{2,1,0:T(8,128)S(1)}, f32[4,384,128]{2,1,0:T(8,128)}) custom-call(s32[4]{0:T(128)S(1)} %pad_add_fusion.idx, bf16[1024,3584]{1,0:T(8,128)(2,1)S(1)} %copy-done.2, bf16[3584,1024]{1,0:T(8,128)(2,1)S(1)} %copy-done.5), custom_call_target="tpu_custom_call" | custom-call | flops 2818572288 | bytes 10092544 | tf_op jit(solution)/shard_map/layer_z/pallas_call | solution.py:120
  86.7 1.6 collective-permute-start
  88.3 2.0 %pack.1 = (f32[1536,128]{1,0:T(8,128)}, f32[1536,128]{1,0:T(8,128)}, f32[1536,128]{1,0:T(8,128)}) custom-call(s32[4]{0:T(128)S(1)} %pad_add_fusion.idx, bf16[1024,128]{1,0:T(8,128)(2,1)S(1)} %copy-done.9, bf16[2048,128]{1,0:T(8,128)(2,1)S(1)} %bitcast.44), custom_call_target="tpu_custom_call" | custom-call | bytes 2359296 | tf_op jit(solution)/shard_map/pack/pallas_call | solution.py:56
  90.3 1.5 collective-permute-start.12
  92.4 2.1 %collective-permute-start.14 = (f32[1536,128]{1,0:T(8,128)}, f32[1536,128]{1,0:T(8,128)S(1)}, u32[]{:S(2)}, u32[]{:S(2)}) collective-permute-start(f32[1536,128]{1,0:T(8,128)} %get-tuple-element.27), channel_id=1, source_target_pairs={{0,32},{8,40},{16,48},{24,56},{32,0},{40,8},{48,16},{56,24},{1,33}... | collective-permute-start | bytes 2359304 | tf_op jit(solution)/shard_map/ppermute | solution.py:230
  94.5 0.9 add_convert_fusion
  95.4 1.4 add.111
  96.9 10.1 %collective-permute-done = f32[4,384,128]{2,1,0:T(8,128)} collective-permute-done((f32[4,384,128]{2,1,0:T(8,128)}, f32[4,384,128]{2,1,0:T(8,128)}, u32[]{:S(2)}, u32[]{:S(2)}) %collective-permute-start) | collective-permute-done | bytes 786464 | tf_op jit(solution)/shard_map/ppermute | solution.py:247
  107.0 0.8 collective-permute-start.5
  107.8 1.4 add.107
  109.3 1.6 collective-permute-done.12.a1.b1
  110.9 0.9 collective-permute-start.6
  111.8 2.4 %collective-permute-start.7 = (f32[384,128]{1,0:T(8,128)S(1)}, f32[384,128]{1,0:T(8,128)S(1)}, u32[]{:S(2)}, u32[]{:S(2)}) collective-permute-start(f32[384,128]{1,0:T(8,128)S(1)} %get-tuple-element.37), channel_id=1, source_target_pairs={{0,6},{1,7},{2,0},{3,1},{4,2},{5,3},{6,4},{7,5},{8,14},{9,15},{10,... | collective-permute-start | bytes 589832 | tf_op jit(solution)/shard_map/ppermute | solution.py:248
  114.3 14.6 %collective-permute-done.14.a3.b3 = f32[1536,128]{1,0:T(8,128)S(1)} collective-permute-done((f32[1536,128]{1,0:T(8,128)}, f32[1536,128]{1,0:T(8,128)S(1)}, u32[]{:S(2)}, u32[]{:S(2)}) %collective-permute-start.14) | collective-permute-done | bytes 786464 | tf_op jit(solution)/shard_map/ppermute | solution.py:230
  128.9 1.0 copy-done.7
  130.0 0.9 copy-done.10
  130.9 3.6 %scores.1 = f32[16,1024]{1,0:T(8,128)S(1)} custom-call(s32[4]{0:T(128)S(1)} %pad_add_fusion.idx, bf16[1024,128]{1,0:T(8,128)(2,1)S(1)} %copy-done.10, bf16[2048,128]{1,0:T(8,128)(2,1)S(1)} %bitcast.45, f32[1536,128]{1,0:T(8,128)S(1)} %collective-permute-done.12.a1.b1, f32[1536,128]{1,0:T(8,128)S(1)} %collective-permute-done.12.a1.b1, ...), custom_call_target="tpu_custom_call" | custom-call | flops 536870912 | bytes 4194304 | tf_op jit(solution)/shard_map/scores/pallas_call | solution.py:205
  134.7 0.9 collective-permute-start.1
  135.9 2.2 %collective-permute-start.2 = (f32[384,128]{1,0:T(8,128)S(1)}, f32[384,128]{1,0:T(8,128)S(1)}, u32[]{:S(2)}, u32[]{:S(2)}) collective-permute-start(f32[384,128]{1,0:T(8,128)S(1)} %get-tuple-element.35), channel_id=1, source_target_pairs={{0,2},{1,3},{2,4},{3,5},{4,6},{5,7},{6,0},{7,1},{8,10},{9,11},{10,... | collective-permute-start | bytes 589832 | tf_op jit(solution)/shard_map/ppermute | solution.py:248
  138.4 3.0 %collective-permute-start.26 = (f32[8,1024]{1,0:T(8,128)S(1)}, f32[8,1024]{1,0:T(8,128)S(1)}, u32[]{:S(2)}, u32[]{:S(2)}) collective-permute-start(f32[8,1024]{1,0:T(8,128)S(1)} %dynamic-slice_add_fusion), channel_id=1, source_target_pairs={{0,6},{1,7},{2,0},{3,1},{4,2},{5,3},{6,4},{7,5},{8,14},{9,15},{10,... | collective-permute-start | bytes 98312 | tf_op jit(solution)/shard_map/ppermute | solution.py:265
  141.9 7.0 %collective-permute-done.25 = f32[8,1024]{1,0:T(8,128)S(1)} collective-permute-done((f32[8,1024]{1,0:T(8,128)S(1)}, f32[8,1024]{1,0:T(8,128)S(1)}, u32[]{:S(2)}, u32[]{:S(2)}) %collective-permute-start.25) | collective-permute-done | bytes 32800 | tf_op jit(solution)/shard_map/ppermute | solution.py:265
  150.0 5.6 %collective-permute-done.3 = f32[384,128]{1,0:T(8,128)S(1)} collective-permute-done((f32[384,128]{1,0:T(8,128)S(1)}, f32[384,128]{1,0:T(8,128)S(1)}, u32[]{:S(2)}, u32[]{:S(2)}) %collective-permute-start.3) | collective-permute-done | bytes 196640 | tf_op jit(solution)/shard_map/ppermute | solution.py:248
  155.7 3.4 %collective-permute-start.29 = (f32[8,128]{1,0:T(8,128)S(1)}, f32[8,128]{1,0:T(8,128)S(1)}, u32[]{:S(2)}, u32[]{:S(2)}) collective-permute-start(f32[8,128]{1,0:T(8,128)S(1)} %get-tuple-element.32), channel_id=1, source_target_pairs={{0,64},{64,128},{128,192},{192,0},{1,65},{65,129},{129,193},{193,1... | collective-permute-start | bytes 12296 | tf_op jit(solution)/shard_map/ppermute | solution.py:270
  159.1 2.2 %collective-permute-start.30 = (f32[8,128]{1,0:T(8,128)S(1)}, f32[8,128]{1,0:T(8,128)S(1)}, u32[]{:S(2)}, u32[]{:S(2)}) collective-permute-start(f32[8,128]{1,0:T(8,128)S(1)} %get-tuple-element.32), channel_id=1, source_target_pairs={{0,192},{64,0},{128,64},{192,128},{1,193},{65,1},{129,65},{193,129... | collective-permute-start | bytes 12296 | tf_op jit(solution)/shard_map/ppermute | solution.py:270
  161.3 4.9 %collective-permute-start.28 = (f32[8,128]{1,0:T(8,128)S(1)}, f32[8,128]{1,0:T(8,128)S(1)}, u32[]{:S(2)}, u32[]{:S(2)}) collective-permute-start(f32[8,128]{1,0:T(8,128)S(1)} %get-tuple-element.32), channel_id=1, source_target_pairs={{0,128},{64,192},{128,0},{192,64},{1,129},{65,193},{129,1},{193,65... | collective-permute-start | bytes 12296 | tf_op jit(solution)/shard_map/ppermute | solution.py:270
  167.0 1.9 %collective-permute-done.28 = f32[8,128]{1,0:T(8,128)S(1)} collective-permute-done((f32[8,128]{1,0:T(8,128)S(1)}, f32[8,128]{1,0:T(8,128)S(1)}, u32[]{:S(2)}, u32[]{:S(2)}) %collective-permute-start.28) | collective-permute-done | bytes 4128 | tf_op jit(solution)/shard_map/ppermute | solution.py:270
  (74 shorter events, 6.6 us)
Async XLA Ops:
  0.7 3.1 %copy-start = (bf16[1024,3584]{1,0:T(8,128)(2,1)S(1)}, bf16[1024,3584]{1,0:T(8,128)(2,1)}, u32[]{:S(2)}) copy-start(bf16[1024,3584]{1,0:T(8,128)(2,1)} %a.7) | copy-start | bytes 22020100
  3.8 3.1 %copy-start.3 = (bf16[3584,1024]{1,0:T(8,128)(2,1)S(1)}, bf16[3584,1024]{1,0:T(8,128)(2,1)}, u32[]{:S(2)}) copy-start(bf16[3584,1024]{1,0:T(8,128)(2,1)} %w.5) | copy-start | bytes 22020100
  6.9 7.6 %copy-start.8 = (bf16[8,32,3584]{2,1,0:T(8,128)(2,1)S(1)}, bf16[8,32,3584]{2,1,0:T(8,128)(2,1)}, u32[]{:S(2)}) copy-start(bf16[8,32,3584]{2,1,0:T(8,128)(2,1)} %param.9) | copy-start | bytes 5505028
  11.2 49.8 %collective-permute-start.9 = (f32[256,256]{1,0:T(8,128)S(1)}, f32[256,256]{1,0:T(8,128)S(1)}, u32[]{:S(2)}, u32[]{:S(2)}) collective-permute-start(f32[256,256]{1,0:T(8,128)S(1)} %get-tuple-element.23), channel_id=1, source_target_pairs={{0,2},{1,3},{2,4},{3,5},{4,6},{5,7},{6,0},{7,1},{8,10},{9,11},{10,... | collective-permute-start | bytes 786440 | tf_op jit(solution)/shard_map/ppermute | solution.py:252
  12.9 50.1 %collective-permute-start.10 = (f32[256,256]{1,0:T(8,128)S(1)}, f32[256,256]{1,0:T(8,128)S(1)}, u32[]{:S(2)}, u32[]{:S(2)}) collective-permute-start(f32[256,256]{1,0:T(8,128)S(1)} %get-tuple-element.24), channel_id=1, source_target_pairs={{0,6},{1,7},{2,0},{3,1},{4,2},{5,3},{6,4},{7,5},{8,14},{9,15},{10,... | collective-permute-start | bytes 786440 | tf_op jit(solution)/shard_map/ppermute | solution.py:252
  18.1 16.4 %collective-permute-start.16 = (f32[64,1024]{1,0:T(8,128)S(1)}, f32[64,1024]{1,0:T(8,128)}, u32[]{:S(2)}, u32[]{:S(2)}) collective-permute-start(f32[64,1024]{1,0:T(8,128)S(1)} %get-tuple-element.30), channel_id=1, source_target_pairs={{0,2},{1,3},{2,4},{3,5},{4,6},{5,7},{6,0},{7,1},{8,10},{9,11},{10,... | collective-permute-start | bytes 786440 | tf_op jit(solution)/shard_map/ppermute | solution.py:234
  18.6 18.7 %collective-permute-start.17 = (f32[64,1024]{1,0:T(8,128)S(1)}, f32[64,1024]{1,0:T(8,128)}, u32[]{:S(2)}, u32[]{:S(2)}) collective-permute-start(f32[64,1024]{1,0:T(8,128)S(1)} %get-tuple-element.31), channel_id=1, source_target_pairs={{0,6},{1,7},{2,0},{3,1},{4,2},{5,3},{6,4},{7,5},{8,14},{9,15},{10,... | collective-permute-start | bytes 786440 | tf_op jit(solution)/shard_map/ppermute | solution.py:234
  21.4 17.8 %collective-permute-start.15 = (f32[64,1024]{1,0:T(8,128)S(1)}, f32[64,1024]{1,0:T(8,128)}, u32[]{:S(2)}, u32[]{:S(2)}) collective-permute-start(f32[64,1024]{1,0:T(8,128)S(1)} %get-tuple-element.29), channel_id=1, source_target_pairs={{0,4},{1,5},{2,6},{3,7},{4,0},{5,1},{6,2},{7,3},{8,12},{9,13},{10,... | collective-permute-start | bytes 786440 | tf_op jit(solution)/shard_map/ppermute | solution.py:234
  22.2 3.1 %copy-start.1 = (bf16[1024,3584]{1,0:T(8,128)(2,1)S(1)}, bf16[1024,3584]{1,0:T(8,128)(2,1)}, u32[]{:S(2)}) copy-start(bf16[1024,3584]{1,0:T(8,128)(2,1)} %a.7) | copy-start | bytes 22020100
  25.3 3.1 %copy-start.4 = (bf16[3584,1024]{1,0:T(8,128)(2,1)S(1)}, bf16[3584,1024]{1,0:T(8,128)(2,1)}, u32[]{:S(2)}) copy-start(bf16[3584,1024]{1,0:T(8,128)(2,1)} %w.5) | copy-start | bytes 22020100
  28.4 12.1 %copy-start.14 = (f32[8,32]{1,0:T(8,128)S(1)}, f32[8,32]{1,0:T(8,128)}, u32[]{:S(2)}) copy-start(f32[8,32]{1,0:T(8,128)} %param.11) | copy-start | bytes 3076
  33.6 0.9 copy-start.11
  34.5 29.8 %collective-permute-start.8 = (f32[256,256]{1,0:T(8,128)S(1)}, f32[256,256]{1,0:T(8,128)S(1)}, u32[]{:S(2)}, u32[]{:S(2)}) collective-permute-start(f32[256,256]{1,0:T(8,128)S(1)} %get-tuple-element.22), channel_id=1, source_target_pairs={{0,4},{1,5},{2,6},{3,7},{4,0},{5,1},{6,2},{7,3},{8,12},{9,13},{10,... | collective-permute-start | bytes 786440 | tf_op jit(solution)/shard_map/ppermute | solution.py:252
  37.3 55.1 %collective-permute-start.4 = (f32[4,384,128]{2,1,0:T(8,128)S(1)}, f32[4,384,128]{2,1,0:T(8,128)}, u32[]{:S(2)}, u32[]{:S(2)}) collective-permute-start(f32[4,384,128]{2,1,0:T(8,128)S(1)} %get-tuple-element.20), channel_id=1, source_target_pairs={{0,1},{1,0},{2,3},{3,2},{4,5},{5,4},{6,7},{7,6},{8,9},{9,8},{10,11... | collective-permute-start | bytes 2359304 | tf_op jit(solution)/shard_map/ppermute | solution.py:247
  40.4 20.5 %collective-permute-start.18 = (f32[64,1024]{1,0:T(8,128)S(1)}, f32[64,1024]{1,0:T(8,128)S(1)}, u32[]{:S(2)}, u32[]{:S(2)}) collective-permute-start(f32[64,1024]{1,0:T(8,128)S(1)} %add_add_fusion), channel_id=1, source_target_pairs={{0,1},{1,0},{2,3},{3,2},{4,5},{5,4},{6,7},{7,6},{8,9},{9,8},{10,11... | collective-permute-start | bytes 786440 | tf_op jit(solution)/shard_map/ppermute | solution.py:236
  60.9 12.7 %collective-permute-start.21 = (f32[64,1024]{1,0:T(8,128)S(1)}, f32[64,1024]{1,0:T(8,128)S(1)}, u32[]{:S(2)}, u32[]{:S(2)}) collective-permute-start(f32[64,1024]{1,0:T(8,128)S(1)} %add_multiply_fusion), channel_id=1, source_target_pairs={{0,2},{1,3},{2,4},{3,5},{4,6},{5,7},{6,0},{7,1},{8,10},{9,11},{10,... | collective-permute-start | bytes 786440 | tf_op jit(solution)/shard_map/ppermute | solution.py:240
  61.0 12.6 %collective-permute-start.20 = (f32[64,1024]{1,0:T(8,128)S(1)}, f32[64,1024]{1,0:T(8,128)S(1)}, u32[]{:S(2)}, u32[]{:S(2)}) collective-permute-start(f32[64,1024]{1,0:T(8,128)S(1)} %add_multiply_fusion), channel_id=1, source_target_pairs={{0,4},{1,5},{2,6},{3,7},{4,0},{5,1},{6,2},{7,3},{8,12},{9,13},{10,... | collective-permute-start | bytes 786440 | tf_op jit(solution)/shard_map/ppermute | solution.py:240
  62.9 11.4 %collective-permute-start.19 = (f32[64,1024]{1,0:T(8,128)S(1)}, f32[64,1024]{1,0:T(8,128)S(1)}, u32[]{:S(2)}, u32[]{:S(2)}) collective-permute-start(f32[64,1024]{1,0:T(8,128)S(1)} %add_multiply_fusion), channel_id=1, source_target_pairs={{0,6},{1,7},{2,0},{3,1},{4,2},{5,3},{6,4},{7,5},{8,14},{9,15},{10,... | collective-permute-start | bytes 786440 | tf_op jit(solution)/shard_map/ppermute | solution.py:240
  64.4 9.9 %copy-start.13 = (f32[256,256]{1,0:T(8,128)}, f32[256,256]{1,0:T(8,128)S(1)}, u32[]{:S(2)}) copy-start(f32[256,256]{1,0:T(8,128)S(1)} %add_add_fusion.1) | copy-start | bytes 786436
  64.5 27.4 %collective-permute-start.11 = (f32[256,128]{1,0:T(8,128)S(1)}, f32[256,128]{1,0:T(8,128)S(1)}, u32[]{:S(2)}, u32[]{:S(2)}) collective-permute-start(f32[256,128]{1,0:T(8,128)S(1)} %constant_dynamic-slice_fusion.2), channel_id=1, source_target_pairs={{0,1},{1,0},{2,3},{3,2},{4,5},{5,4},{6,7},{7,6},{8,9},{9,8},{10,11... | collective-permute-start | bytes 393224 | tf_op jit(solution)/shard_map/ppermute | solution.py:257
  74.4 54.5 %collective-permute-start.22 = (f32[4,64,1024]{2,1,0:T(8,128)S(1)}, f32[4,64,1024]{2,1,0:T(8,128)}, u32[]{:S(2)}, u32[]{:S(2)}) collective-permute-start(f32[4,64,1024]{2,1,0:T(8,128)S(1)} %pad_maximum_fusion.mine), channel_id=1, source_target_pairs={{0,8},{8,0},{16,24},{24,16},{32,40},{40,32},{48,56},{56,48},{1,9},... | collective-permute-start | bytes 3145736 | tf_op jit(solution)/shard_map/ppermute | solution.py:242
  74.7 3.1 %copy-start.2 = (bf16[1024,3584]{1,0:T(8,128)(2,1)S(1)}, bf16[1024,3584]{1,0:T(8,128)(2,1)}, u32[]{:S(2)}) copy-start(bf16[1024,3584]{1,0:T(8,128)(2,1)} %a.7) | copy-start | bytes 22020100
  77.8 3.1 %copy-start.5 = (bf16[3584,1024]{1,0:T(8,128)(2,1)S(1)}, bf16[3584,1024]{1,0:T(8,128)(2,1)}, u32[]{:S(2)}) copy-start(bf16[3584,1024]{1,0:T(8,128)(2,1)} %w.5) | copy-start | bytes 22020100
  80.9 7.5 %copy-start.6 = (bf16[64,32,128]{2,1,0:T(8,128)(2,1)S(1)}, bf16[64,32,128]{2,1,0:T(8,128)(2,1)}, u32[]{:S(2)}) copy-start(bf16[64,32,128]{2,1,0:T(8,128)(2,1)} %param.10) | copy-start | bytes 1572868
  80.9 7.5 %copy-start.9 = (bf16[1024,128]{1,0:T(8,128)(2,1)S(1)}, bf16[1024,128]{1,0:T(8,128)(2,1)}, u32[]{:S(2)}) copy-start(bf16[1024,128]{1,0:T(8,128)(2,1)} %og.3) | copy-start | bytes 786436
  86.7 5.6 %copy-start.12 = (f32[4,384,128]{2,1,0:T(8,128)}, f32[4,384,128]{2,1,0:T(8,128)S(1)}, u32[]{:S(2)}) copy-start(f32[4,384,128]{2,1,0:T(8,128)S(1)} %get-tuple-element.17) | copy-start | bytes 2359300
  86.7 20.3 %collective-permute-start = (f32[4,384,128]{2,1,0:T(8,128)}, f32[4,384,128]{2,1,0:T(8,128)}, u32[]{:S(2)}, u32[]{:S(2)}) collective-permute-start(f32[4,384,128]{2,1,0:T(8,128)} %get-tuple-element.18), channel_id=1, source_target_pairs={{0,1},{1,0},{2,3},{3,2},{4,5},{5,4},{6,7},{7,6},{8,9},{9,8},{10,11... | collective-permute-start | bytes 2359304 | tf_op jit(solution)/shard_map/ppermute | solution.py:247
  90.3 20.6 %collective-permute-start.12 = (f32[1536,128]{1,0:T(8,128)}, f32[1536,128]{1,0:T(8,128)S(1)}, u32[]{:S(2)}, u32[]{:S(2)}) collective-permute-start(f32[1536,128]{1,0:T(8,128)} %get-tuple-element.25), channel_id=1, source_target_pairs={{0,16},{8,24},{16,32},{24,40},{32,48},{40,56},{48,0},{56,8},{1,17}... | collective-permute-start | bytes 2359304 | tf_op jit(solution)/shard_map/ppermute | solution.py:230
  91.8 20.0 %collective-permute-start.13 = (f32[1536,128]{1,0:T(8,128)}, f32[1536,128]{1,0:T(8,128)S(1)}, u32[]{:S(2)}, u32[]{:S(2)}) collective-permute-start(f32[1536,128]{1,0:T(8,128)} %get-tuple-element.26), channel_id=1, source_target_pairs={{0,48},{8,56},{16,0},{24,8},{32,16},{40,24},{48,32},{56,40},{1,49}... | collective-permute-start | bytes 2359304 | tf_op jit(solution)/shard_map/ppermute | solution.py:230
  92.4 36.5 %collective-permute-start.14 = (f32[1536,128]{1,0:T(8,128)}, f32[1536,128]{1,0:T(8,128)S(1)}, u32[]{:S(2)}, u32[]{:S(2)}) collective-permute-start(f32[1536,128]{1,0:T(8,128)} %get-tuple-element.27), channel_id=1, source_target_pairs={{0,32},{8,40},{16,48},{24,56},{32,0},{40,8},{48,16},{56,24},{1,33}... | collective-permute-start | bytes 2359304 | tf_op jit(solution)/shard_map/ppermute | solution.py:230
  107.0 31.1 %collective-permute-start.5 = (f32[384,128]{1,0:T(8,128)S(1)}, f32[384,128]{1,0:T(8,128)S(1)}, u32[]{:S(2)}, u32[]{:S(2)}) collective-permute-start(f32[384,128]{1,0:T(8,128)S(1)} %get-tuple-element.39), channel_id=1, source_target_pairs={{0,4},{1,5},{2,6},{3,7},{4,0},{5,1},{6,2},{7,3},{8,12},{9,13},{10,... | collective-permute-start | bytes 589832 | tf_op jit(solution)/shard_map/ppermute | solution.py:248
  110.9 27.5 %collective-permute-start.6 = (f32[384,128]{1,0:T(8,128)S(1)}, f32[384,128]{1,0:T(8,128)S(1)}, u32[]{:S(2)}, u32[]{:S(2)}) collective-permute-start(f32[384,128]{1,0:T(8,128)S(1)} %get-tuple-element.38), channel_id=1, source_target_pairs={{0,2},{1,3},{2,4},{3,5},{4,6},{5,7},{6,0},{7,1},{8,10},{9,11},{10,... | collective-permute-start | bytes 589832 | tf_op jit(solution)/shard_map/ppermute | solution.py:248
  111.8 29.6 %collective-permute-start.7 = (f32[384,128]{1,0:T(8,128)S(1)}, f32[384,128]{1,0:T(8,128)S(1)}, u32[]{:S(2)}, u32[]{:S(2)}) collective-permute-start(f32[384,128]{1,0:T(8,128)S(1)} %get-tuple-element.37), channel_id=1, source_target_pairs={{0,6},{1,7},{2,0},{3,1},{4,2},{5,3},{6,4},{7,5},{8,14},{9,15},{10,... | collective-permute-start | bytes 589832 | tf_op jit(solution)/shard_map/ppermute | solution.py:248
  128.9 1.0 copy-start.7
  129.9 0.9 copy-start.10
  134.6 1.3 collective-permute-start.23
  134.7 15.3 %collective-permute-start.1 = (f32[384,128]{1,0:T(8,128)S(1)}, f32[384,128]{1,0:T(8,128)S(1)}, u32[]{:S(2)}, u32[]{:S(2)}) collective-permute-start(f32[384,128]{1,0:T(8,128)S(1)} %get-tuple-element.36), channel_id=1, source_target_pairs={{0,4},{1,5},{2,6},{3,7},{4,0},{5,1},{6,2},{7,3},{8,12},{9,13},{10,... | collective-permute-start | bytes 589832 | tf_op jit(solution)/shard_map/ppermute | solution.py:248
  135.9 14.2 %collective-permute-start.2 = (f32[384,128]{1,0:T(8,128)S(1)}, f32[384,128]{1,0:T(8,128)S(1)}, u32[]{:S(2)}, u32[]{:S(2)}) collective-permute-start(f32[384,128]{1,0:T(8,128)S(1)} %get-tuple-element.35), channel_id=1, source_target_pairs={{0,2},{1,3},{2,4},{3,5},{4,6},{5,7},{6,0},{7,1},{8,10},{9,11},{10,... | collective-permute-start | bytes 589832 | tf_op jit(solution)/shard_map/ppermute | solution.py:248
  138.1 10.8 %collective-permute-start.25 = (f32[8,1024]{1,0:T(8,128)S(1)}, f32[8,1024]{1,0:T(8,128)S(1)}, u32[]{:S(2)}, u32[]{:S(2)}) collective-permute-start(f32[8,1024]{1,0:T(8,128)S(1)} %dynamic-slice_add_fusion), channel_id=1, source_target_pairs={{0,2},{1,3},{2,4},{3,5},{4,6},{5,7},{6,0},{7,1},{8,10},{9,11},{10,... | collective-permute-start | bytes 98312 | tf_op jit(solution)/shard_map/ppermute | solution.py:265
  138.4 11.1 %collective-permute-start.26 = (f32[8,1024]{1,0:T(8,128)S(1)}, f32[8,1024]{1,0:T(8,128)S(1)}, u32[]{:S(2)}, u32[]{:S(2)}) collective-permute-start(f32[8,1024]{1,0:T(8,128)S(1)} %dynamic-slice_add_fusion), channel_id=1, source_target_pairs={{0,6},{1,7},{2,0},{3,1},{4,2},{5,3},{6,4},{7,5},{8,14},{9,15},{10,... | collective-permute-start | bytes 98312 | tf_op jit(solution)/shard_map/ppermute | solution.py:265
  141.4 8.1 %collective-permute-start.24 = (f32[8,1024]{1,0:T(8,128)S(1)}, f32[8,1024]{1,0:T(8,128)S(1)}, u32[]{:S(2)}, u32[]{:S(2)}) collective-permute-start(f32[8,1024]{1,0:T(8,128)S(1)} %dynamic-slice_add_fusion), channel_id=1, source_target_pairs={{0,4},{1,5},{2,6},{3,7},{4,0},{5,1},{6,2},{7,3},{8,12},{9,13},{10,... | collective-permute-start | bytes 98312 | tf_op jit(solution)/shard_map/ppermute | solution.py:265
  148.9 6.8 %collective-permute-start.3 = (f32[384,128]{1,0:T(8,128)S(1)}, f32[384,128]{1,0:T(8,128)S(1)}, u32[]{:S(2)}, u32[]{:S(2)}) collective-permute-start(f32[384,128]{1,0:T(8,128)S(1)} %get-tuple-element.34), channel_id=1, source_target_pairs={{0,6},{1,7},{2,0},{3,1},{4,2},{5,3},{6,4},{7,5},{8,14},{9,15},{10,... | collective-permute-start | bytes 589832 | tf_op jit(solution)/shard_map/ppermute | solution.py:248
  149.5 6.2 %collective-permute-start.27 = (f32[8,1024]{1,0:T(8,128)S(1)}, f32[8,1024]{1,0:T(8,128)S(1)}, u32[]{:S(2)}, u32[]{:S(2)}) collective-permute-start(f32[8,1024]{1,0:T(8,128)S(1)} %add_add_fusion.2), channel_id=1, source_target_pairs={{0,1},{1,0},{2,3},{3,2},{4,5},{5,4},{6,7},{7,6},{8,9},{9,8},{10,11... | collective-permute-start | bytes 98312 | tf_op jit(solution)/shard_map/ppermute | solution.py:267
  155.7 11.2 %collective-permute-start.29 = (f32[8,128]{1,0:T(8,128)S(1)}, f32[8,128]{1,0:T(8,128)S(1)}, u32[]{:S(2)}, u32[]{:S(2)}) collective-permute-start(f32[8,128]{1,0:T(8,128)S(1)} %get-tuple-element.32), channel_id=1, source_target_pairs={{0,64},{64,128},{128,192},{192,0},{1,65},{65,129},{129,193},{193,1... | collective-permute-start | bytes 12296 | tf_op jit(solution)/shard_map/ppermute | solution.py:270
  159.1 7.9 %collective-permute-start.30 = (f32[8,128]{1,0:T(8,128)S(1)}, f32[8,128]{1,0:T(8,128)S(1)}, u32[]{:S(2)}, u32[]{:S(2)}) collective-permute-start(f32[8,128]{1,0:T(8,128)S(1)} %get-tuple-element.32), channel_id=1, source_target_pairs={{0,192},{64,0},{128,64},{192,128},{1,193},{65,1},{129,65},{193,129... | collective-permute-start | bytes 12296 | tf_op jit(solution)/shard_map/ppermute | solution.py:270
  161.3 7.5 %collective-permute-start.28 = (f32[8,128]{1,0:T(8,128)S(1)}, f32[8,128]{1,0:T(8,128)S(1)}, u32[]{:S(2)}, u32[]{:S(2)}) collective-permute-start(f32[8,128]{1,0:T(8,128)S(1)} %get-tuple-element.32), channel_id=1, source_target_pairs={{0,128},{64,192},{128,0},{192,64},{1,129},{65,193},{129,1},{193,65... | collective-permute-start | bytes 12296 | tf_op jit(solution)/shard_map/ppermute | solution.py:270

commit v2 on v1

--- a/solution.py
+++ b/solution.py
@@ -36,31 +36,42 @@
     return pltpu.CompilerParams(vmem_limit_bytes=limit)
 
 
-def cost(flops, nbytes):
-    return pl.CostEstimate(flops=flops, bytes_accessed=nbytes, transcendentals=0)
-
-
-def pack_kernel(idx, og, gf, *outs):
-    tokens = og.shape[0]
+def cost():
+    return pl.CostEstimate(flops=0, bytes_accessed=0, transcendentals=0)
+
+
+def after(value, *others):
+    return lax.optimization_barrier((value, *others))[0]
+
+
+def pack_kernel(idx, og, gf, fwd, bwd):
+    half = og.shape[0] // 2
     rows = gf.shape[0] // 4
-    for out, d in zip(outs, (1, 3, 2)):
-        out[pl.ds(0, tokens), :] = og[...].astype(F32)
-        start = pl.multiple_of(lax.rem(idx[0] + d, 4) * rows, rows)
-        out[pl.ds(tokens, rows), :] = gf[pl.ds(start, rows), :].astype(F32)
+
+    def gf_rows(d, first, count):
+        start = lax.rem(idx[0] + d, 4) * rows + first
+        return gf[pl.ds(pl.multiple_of(start, count), count), :].astype(F32)
+
+    low, high = og[:half, :].astype(F32), og[half:, :].astype(F32)
+    for out, d, ahead, behind, part in ((fwd, 1, high, low, 0), (bwd, 3, low, high, 1)):
+        out[:half, :] = ahead
+        out[half : half + rows, :] = gf_rows(d, 0, rows)
+        out[half + rows : 2 * half + rows, :] = behind
+        out[2 * half + rows :, :] = gf_rows(2, part * (rows // 2), rows // 2)
 
 
 def pack(idx, og, gf):
     tokens, width = og.shape
-    rows = tokens + gf.shape[0] // 4
+    rows = tokens + gf.shape[0] // 4 * 3 // 2
     whole = pl.BlockSpec(memory_space=pltpu.VMEM)
     return pl.pallas_call(
         pack_kernel,
         grid_spec=pltpu.PrefetchScalarGridSpec(
-            num_scalar_prefetch=1, grid=(), in_specs=[whole, whole], out_specs=[whole] * 3
-        ),
-        out_shape=[jax.ShapeDtypeStruct((rows, width), F32)] * 3,
+            num_scalar_prefetch=1, grid=(), in_specs=[whole, whole], out_specs=[whole] * 2
+        ),
+        out_shape=[jax.ShapeDtypeStruct((rows, width), F32)] * 2,
         compiler_params=params(16 * MIB),
-        cost_estimate=cost(0, 4 * 3 * rows * width),
+        cost_estimate=cost(),
         name="pack",
     )(idx, og, gf)
 
@@ -94,7 +105,7 @@
         ),
         out_shape=[jax.ShapeDtypeStruct((qr // 4, tokens), F32)] * 4,
         compiler_params=params(24 * MIB),
-        cost_estimate=cost(2 * qr * tokens * hidden, 2 * hidden * (qr + tokens)),
+        cost_estimate=cost(),
         name="act",
     )(idx, af, a)
 
@@ -130,7 +141,7 @@
         ),
         out_shape=[jax.ShapeDtypeStruct((4, rows, width // 2), F32)] * 2,
         compiler_params=params(24 * MIB),
-        cost_estimate=cost(2 * rows * hidden * cols, 2 * hidden * (rows + cols)),
+        cost_estimate=cost(),
         name="layer_z",
     )(idx, a, w)
 
@@ -159,15 +170,21 @@
         ),
         out_shape=[jax.ShapeDtypeStruct((rows, width), F32)] * 4,
         compiler_params=params(24 * MIB),
-        cost_estimate=cost(2 * rows * hidden * cols, 2 * hidden * (rows + cols)),
+        cost_estimate=cost(),
         name="layer_y",
     )(idx, a, w)
 
 
-def score_kernel(idx, og, gf, a1, b1, a2, b2, a3, b3, mine, other, out, *, ranks):
+def score_kernel(
+    idx, og, gf, a1, b1, a3, b3, a2, b2, a2_, b2_, mine, other, out, *, ranks
+):
     bf = jnp.bfloat16
-    lhs = jnp.concatenate([gf[...]] + [b[...].astype(bf) for b in (b1, b2, b3)], axis=1)
-    rhs = jnp.concatenate([og[...]] + [a[...].astype(bf) for a in (a1, a2, a3)], axis=1)
+    far = jnp.where(pl.program_id(0) < pl.num_programs(0) // 2, a2[...], a2_[...])
+    far_rows = jnp.concatenate([b2[...], b2_[...]], axis=0)
+    lhs = jnp.concatenate(
+        [gf[...]] + [b.astype(bf) for b in (b1[...], b3[...], far_rows)], axis=1
+    )
+    rhs = jnp.concatenate([og[...]] + [a.astype(bf) for a in (a1[...], a3[...], far)], axis=1)
     grad = lax.dot_general(lhs, rhs, (((1,), (1,)), ((), ())), preferred_element_type=F32)
     rows = mine.shape[1]
     parts = []
@@ -184,20 +201,27 @@
     out[...] = jnp.concatenate(parts, axis=0)
 
 
-def scores(idx, og, gf, moved, mine, other, ranks):
+def scores(idx, og, gf, near, far, mine, other, ranks):
     tokens, width = og.shape
     qr = gf.shape[0] // 4
-    tile = 256
-    first = tokens // qr
+    steps = 4
+    tile = tokens // steps
+    mid = steps // 2
+    assert tokens == 2 * qr
+    spec = lambda rows, at: pl.BlockSpec((rows, width), lambda i, idx: (at(i, idx), 0))
     in_specs = [
-        pl.BlockSpec((tile, width), lambda i, idx: (i, 0)),
-        pl.BlockSpec((qr, width), lambda i, idx: (idx[0], 0)),
+        spec(tile, lambda i, idx: i),
+        spec(qr, lambda i, idx: idx[0]),
+        spec(tile, lambda i, idx: jnp.where(i < mid, i + 2 * mid, i - mid)),
+        spec(qr, lambda i, idx: 1),
+        spec(tile, lambda i, idx: jnp.where(i < mid, i, i + mid)),
+        spec(qr, lambda i, idx: 1),
+        spec(tile, lambda i, idx: jnp.minimum(i, mid - 1)),
+        spec(qr // 2, lambda i, idx: 2),
+        spec(tile, lambda i, idx: jnp.maximum(i - mid, 0)),
+        spec(qr // 2, lambda i, idx: 2),
     ]
-    args = [og, gf]
-    for m in moved:
-        in_specs.append(pl.BlockSpec((tile, width), lambda i, idx: (i, 0)))
-        in_specs.append(pl.BlockSpec((qr, width), lambda i, idx: (first, 0)))
-        args += [m, m]
+    args = [og, gf, near[0], near[0], near[1], near[1], far[0], far[0], far[1], far[1]]
     for act in (mine, other):
         in_specs.append(pl.BlockSpec((4, act.shape[1], tile), lambda i, idx: (0, 0, i)))
         args.append(act)
@@ -206,15 +230,20 @@
         functools.partial(score_kernel, ranks=ranks),
         grid_spec=pltpu.PrefetchScalarGridSpec(
             num_scalar_prefetch=1,
-            grid=(tokens // tile,),
+            grid=(steps,),
             in_specs=in_specs,
             out_specs=pl.BlockSpec((queries, tile), lambda i, idx: (0, i)),
         ),
         out_shape=jax.ShapeDtypeStruct((queries, tokens), F32),
         compiler_params=params(24 * MIB),
-        cost_estimate=cost(2 * qr * tokens * width * 4, 4 * tokens * (qr + 4 * width)),
+        cost_estimate=cost(),
         name="scores",
     )(idx, *args)
+
+
+def along_y(parts, shifts=(1, 3, 2)):
+    got = [lax.ppermute(parts[j], "tensor", y_shift(j)) for j in shifts]
+    return (parts[0] + got[2]) + (got[0] + got[1])
 
 
 def body(activations, down_weight, output_grads, act_factors, grad_factors, rank_weight):
@@ -223,47 +252,59 @@
     pipe, tensor = lax.axis_index("pipe"), lax.axis_index("tensor")
     x, core, y, z = pipe // 2, pipe % 2, tensor // 2, tensor % 2
     idx = jnp.stack([x, core, y, z]).astype(jnp.int32)
+    act_factors = act_factors.reshape(queries * ranks, hidden)
+    activations, down_weight, act_factors = (
+        pltpu.with_memory_space_constraint(v, pltpu.HBM)
+        for v in (activations, down_weight, act_factors)
+    )
 
     gf = grad_factors.reshape(-1, grad_factors.shape[2])
-    packed = pack(idx, output_grads, gf)
-    moved = [
-        lax.ppermute(p, "pipe", x_shift(d)) for p, d in zip(packed, (1, -1, 2))
+    fwd, bwd = pack(idx, output_grads, gf)
+    near = [lax.ppermute(fwd, "pipe", x_shift(1)), lax.ppermute(bwd, "pipe", x_shift(-1))]
+
+    at = after(idx, fwd)
+    pieces = act_pieces(at, act_factors, activations)
+    own = along_y(pieces)
+
+    at = after(idx, pieces[0])
+    keep0, send0 = layer_z_first(at, activations, down_weight, 0, 384)
+    got0 = lax.ppermute(send0, "tensor", z_swap())
+    at = after(idx, keep0)
+    parts = layer_y_first(at, activations, down_weight, 3, 256)
+    wide = along_y(parts)
+    at = after(idx, parts[0])
+    keep1, send1 = layer_z_first(at, activations, down_weight, 1, 384)
+
+    own, near[0], near[1] = lax.optimization_barrier((own, near[0], near[1]))
+    at = near[0].shape[0] - tokens // 2 - gf.shape[0] // 8
+    far = [
+        lax.ppermute(near[0][at:], "pipe", x_shift(1)),
+        lax.ppermute(near[1][at:], "pipe", x_shift(-1)),
     ]
-
-    pieces = act_pieces(idx, act_factors.reshape(queries * ranks, hidden), activations)
-    got = [lax.ppermute(pieces[j], "tensor", y_shift(j)) for j in (1, 3, 2)]
-    own = (pieces[0] + got[2]) + (got[0] + got[1])
     own = own + lax.ppermute(own, "tensor", z_swap())
+    got1 = lax.ppermute(send1, "tensor", z_swap())
     weights = (rank_weight * (1.0 / math.sqrt(ranks))).reshape(4, -1)
     own = own * lax.dynamic_index_in_dim(weights, y, 0, keepdims=False)[:, None]
+
+    own, got0, wide, keep1 = lax.optimization_barrier((own, got0, wide, keep1))
     mine = jnp.stack(
         [own] + [lax.ppermute(own, "tensor", y_shift(-j)) for j in (1, 2, 3)]
     )
+    mine, far[0], far[1], got1 = lax.optimization_barrier((mine, far[0], far[1], got1))
     other = lax.ppermute(mine, "pipe", core_swap())
 
-    outputs = []
-    for block in range(2):
-        keep, send = layer_z_first(idx, activations, down_weight, block, 384)
-        total = keep + lax.ppermute(send, "tensor", z_swap())
-        got = [lax.ppermute(total[j], "tensor", y_shift(j)) for j in (1, 3, 2)]
-        total = (total[0] + got[2]) + (got[0] + got[1])
-        outputs.append(total.astype(jnp.bfloat16))
-    parts = layer_y_first(idx, activations, down_weight, 3, 256)
-    got = [lax.ppermute(parts[j], "tensor", y_shift(j)) for j in (1, 3, 2)]
-    total = (parts[0] + got[2]) + (got[0] + got[1])
-    half = total.shape[1] // 2
-    send = lax.dynamic_slice_in_dim(total, (1 - z) * half, half, 1)
-    keep = lax.dynamic_slice_in_dim(total, z * half, half, 1)
-    total = keep + lax.ppermute(send, "tensor", z_swap())
-    outputs.append(total.astype(jnp.bfloat16))
-    layer_output = jnp.concatenate(outputs, axis=0)
-
-    share = scores(idx, output_grads, gf, moved, mine, other, ranks)
+    half = wide.shape[1] // 2
+    send = lax.dynamic_slice_in_dim(wide, (1 - z) * half, half, 1)
+    keep = lax.dynamic_slice_in_dim(wide, z * half, half, 1)
+    out2 = (keep + lax.ppermute(send, "tensor", z_swap())).astype(jnp.bfloat16)
+    out0 = along_y(keep0 + got0).astype(jnp.bfloat16)
+    out1 = along_y(keep1 + got1).astype(jnp.bfloat16)
+
+    share = scores(idx, output_grads, gf, near, far, mine, other, ranks)
     raw = lax.dynamic_slice_in_dim(share, core * queries, queries, 0)
     send = lax.dynamic_slice_in_dim(share, (1 - core) * queries, queries, 0)
     raw = raw + lax.ppermute(send, "pipe", core_swap())
-    got = [lax.ppermute(raw, "tensor", y_shift(j)) for j in (1, 3, 2)]
-    raw = (raw + got[2]) + (got[0] + got[1])
+    raw = along_y([raw] * 4)
     raw = raw + lax.ppermute(raw, "tensor", z_swap())
 
     square = jnp.sum((raw * raw).reshape(queries, -1, 128), axis=1)
@@ -271,7 +312,7 @@
     square = (square + got[2]) + (got[0] + got[1])
     spread = jnp.sum(square, axis=1, keepdims=True) / (tokens * lax.axis_size("dp"))
     influence = raw / jnp.sqrt(spread + 1e-06)
-    return (layer_output, influence.T)
+    return (jnp.concatenate([out0, out1, out2], axis=0), influence.T)
 
 
 def solution(mesh):

time: 172 us -> 132 us (0.77)
  waiting for transfers between devices: 69.2 us -> 33.3 us
  local copies, waits for them, and re-layouts: 21.7 us -> 8.52 us
  Pallas kernels: 24.6 us -> 35 us
    ppermute x21 -> x22, waiting for transfers between devices: 38.9 us -> 15 us  [the longest x15 7.64 us: along_y(): got = [lax.ppermute(parts[j], 'tensor', y_shift(j)) for j in shifts]]
    unnamed x30, local copies, waits for them, and re-layouts: 21.5 us -> 7.37 us
    ppermute x1, waiting for transfers between devices: 20.2 us -> 9.29 us  [body(): own = own + lax.ppermute(own, 'tensor', z_swap())]
    pallas_call x1, Pallas kernels: 3.6 us -> 7.74 us  [act_pieces(): pl.pallas_call(act_kernel, grid_spec=pltpu.PrefetchScalarGridSpec(num_sca...]
    pallas_call x2, Pallas kernels: 11.1 us -> 14.5 us  [layer_z_first(): pl.pallas_call(layer_z_kernel, grid_spec=pltpu.PrefetchScalarGridSpec(num...]
    pallas_call x1, Pallas kernels: 4.25 us -> 7.12 us  [layer_y_first(): pl.pallas_call(layer_y_kernel, grid_spec=pltpu.PrefetchScalarGridSpec(num...]
    ppermute x3, waiting for transfers between devices: 7.99 us -> 5.74 us  [body(): lax.ppermute(own, 'tensor', y_shift(-j))]
    ppermute x21 -> x22, starting transfers between devices: 31.4 us -> 30.4 us  [the longest x15 19.3 us: along_y(): got = [lax.ppermute(parts[j], 'tensor', y_shift(j)) for j in shifts]]
  transfers between devices with their start and end apart: 31 -> 32, of which waited for: 10 -> 11; matrix products, arithmetic and copies ran while one was open for 4% -> 5% of each run, Pallas kernels for 12% -> 25%
where the time goes in v2:
time: 132 us; the launch traced here: 130 us
  starting transfers between devices  45.8 us (35%)
  Pallas kernels  35 us (27%)
  waiting for transfers between devices  33.3 us (25%)
  local copies, waits for them, and re-layouts  8.52 us (6%)
  other arithmetic  6.43 us (5%)
    ppermute x15, starting transfers between devices, along_y(): got = [lax.ppermute(parts[j], 'tensor', y_shift(j)) for j in shifts]  19.3 us
    pallas_call x2, Pallas kernels, layer_z_first(): pl.pallas_call(layer_z_kernel, grid_spec=pltpu.PrefetchScalarGridSpec(num...  14.5 us
    ppermute x3, starting transfers between devices, body(): got = [lax.ppermute(square, 'dp', dp_shift(j)) for j in (1, 3, 2)]  9.99 us
    ppermute x1, waiting for transfers between devices, body(): own = own + lax.ppermute(own, 'tensor', z_swap())  9.29 us
    pallas_call x1, Pallas kernels, act_pieces(): pl.pallas_call(act_kernel, grid_spec=pltpu.PrefetchScalarGridSpec(num_sca...  7.74 us
    ppermute x15, waiting for transfers between devices, along_y(): got = [lax.ppermute(parts[j], 'tensor', y_shift(j)) for j in shifts]  7.64 us
    unnamed x30, local copies, waits for them, and re-layouts  7.37 us
    pallas_call x1, Pallas kernels, layer_y_first(): pl.pallas_call(layer_y_kernel, grid_spec=pltpu.PrefetchScalarGridSpec(num...  7.12 us
  transfers between devices with their start and end apart: 32, of which 11 were waited for; matrix products, arithmetic and copies ran while one was open for 5% of the time, Pallas kernels for 25%

profile of v2, /device:TPU:2, one launch (start us, length us, event | category | flops | bytes accessed | tf_op | source)
XLA Modules:
  0.0 130.0 jit_solution(9207135173901661382)
XLA Ops:
  0.8 1.0 copy-done
  1.8 0.9 copy-done.6
  2.7 1.9 %pack.1 = (f32[1792,128]{1,0:T(8,128)}, f32[1792,128]{1,0:T(8,128)}) custom-call(s32[4]{0:T(128)S(1)} %pad_add_fusion.idx, bf16[1024,128]{1,0:T(8,128)(2,1)S(1)} %copy-done.6, bf16[2048,128]{1,0:T(8,128)(2,1)S(1)} %bitcast.44), custom_call_target="tpu_custom_call" | custom-call | tf_op jit(solution)/shard_map/pack/pallas_call | solution.py:67
  4.7 2.3 %collective-permute-start.4 = (f32[1792,128]{1,0:T(8,128)}, f32[1792,128]{1,0:T(8,128)S(1)}, u32[]{:S(2)}, u32[]{:S(2)}) collective-permute-start(f32[1792,128]{1,0:T(8,128)} %get-tuple-element.39), channel_id=1, source_target_pairs={{0,48},{8,56},{16,0},{24,8},{32,16},{40,24},{48,32},{56,40},{1,49}... | collective-permute-start | bytes 2752520 | tf_op jit(solution)/shard_map/ppermute | solution.py:263
  6.9 7.7 %act.1 = (f32[64,1024]{1,0:T(8,128)S(1)}, f32[64,1024]{1,0:T(8,128)}, f32[64,1024]{1,0:T(8,128)}, f32[64,1024]{1,0:T(8,128)S(1)}) custom-call(s32[4]{0:T(128)S(1)} %pad_add_fusion.idx, bf16[256,3584]{1,0:T(8,128)(2,1)} %bitcast.46, bf16[1024,3584]{1,0:T(8,128)(2,1)} %a.7), custom_call_target="tpu_custom_call" | custom-call | tf_op jit(solution)/shard_map/act/pallas_call | solution.py:94
  14.7 2.9 %collective-permute-start = (f32[64,1024]{1,0:T(8,128)}, f32[64,1024]{1,0:T(8,128)}, u32[]{:S(2)}, u32[]{:S(2)}) collective-permute-start(f32[64,1024]{1,0:T(8,128)} %get-tuple-element.36), channel_id=1, source_target_pairs={{0,4},{1,5},{2,6},{3,7},{4,0},{5,1},{6,2},{7,3},{8,12},{9,13},{10,... | collective-permute-start | bytes 786440 | tf_op jit(solution)/shard_map/ppermute | solution.py:245
  18.3 2.6 %collective-permute-start.2 = (f32[64,1024]{1,0:T(8,128)S(1)}, f32[64,1024]{1,0:T(8,128)}, u32[]{:S(2)}, u32[]{:S(2)}) collective-permute-start(f32[64,1024]{1,0:T(8,128)S(1)} %get-tuple-element.38), channel_id=1, source_target_pairs={{0,6},{1,7},{2,0},{3,1},{4,2},{5,3},{6,4},{7,5},{8,14},{9,15},{10,... | collective-permute-start | bytes 786440 | tf_op jit(solution)/shard_map/ppermute | solution.py:245
  20.9 7.3 %layer_z.2 = (f32[4,384,128]{2,1,0:T(8,128)S(1)}, f32[4,384,128]{2,1,0:T(8,128)S(1)}) custom-call(s32[4]{0:T(128)S(1)} %pad_add_fusion.idx, bf16[1024,3584]{1,0:T(8,128)(2,1)} %a.7, bf16[3584,1024]{1,0:T(8,128)(2,1)} %w.5), custom_call_target="tpu_custom_call" | custom-call | tf_op jit(solution)/shard_map/layer_z/pallas_call | solution.py:131
  28.2 0.9 copy-done.10
  29.1 7.1 %layer_y.1 = (f32[256,256]{1,0:T(8,128)S(1)}, f32[256,256]{1,0:T(8,128)}, f32[256,256]{1,0:T(8,128)}, f32[256,256]{1,0:T(8,128)}) custom-call(s32[4]{0:T(128)S(1)} %pad_add_fusion.idx, bf16[1024,3584]{1,0:T(8,128)(2,1)} %a.7, bf16[3584,1024]{1,0:T(8,128)(2,1)} %w.5), custom_call_target="tpu_custom_call" | custom-call | tf_op jit(solution)/shard_map/layer_y/pallas_call | solution.py:160
  36.2 2.0 %collective-permute-start.6 = (f32[4,384,128]{2,1,0:T(8,128)S(1)}, f32[4,384,128]{2,1,0:T(8,128)S(1)}, u32[]{:S(2)}, u32[]{:S(2)}) collective-permute-start(f32[4,384,128]{2,1,0:T(8,128)S(1)} %get-tuple-element.41), channel_id=1, source_target_pairs={{0,1},{1,0},{2,3},{3,2},{4,5},{5,4},{6,7},{7,6},{8,9},{9,8},{10,11... | collective-permute-start | bytes 2359304 | tf_op jit(solution)/shard_map/ppermute | solution.py:271
  38.2 0.9 collective-permute-start.8
  39.1 2.5 %collective-permute-start.9 = (f32[256,256]{1,0:T(8,128)}, f32[256,256]{1,0:T(8,128)S(1)}, u32[]{:S(2)}, u32[]{:S(2)}) collective-permute-start(f32[256,256]{1,0:T(8,128)} %get-tuple-element.46), channel_id=1, source_target_pairs={{0,6},{1,7},{2,0},{3,1},{4,2},{5,3},{6,4},{7,5},{8,14},{9,15},{10,... | collective-permute-start | bytes 786440 | tf_op jit(solution)/shard_map/ppermute | solution.py:245
  41.5 1.2 add_add_fusion.1
  42.9 7.3 %layer_z.3 = (f32[4,384,128]{2,1,0:T(8,128)S(1)}, f32[4,384,128]{2,1,0:T(8,128)S(1)}) custom-call(s32[4]{0:T(128)S(1)} %pad_add_fusion.idx, bf16[1024,3584]{1,0:T(8,128)(2,1)} %a.7, bf16[3584,1024]{1,0:T(8,128)(2,1)} %w.5), custom_call_target="tpu_custom_call" | custom-call | tf_op jit(solution)/shard_map/layer_z/pallas_call | solution.py:131
  50.2 2.0 %collective-permute-start.18 = (f32[4,384,128]{2,1,0:T(8,128)S(1)}, f32[4,384,128]{2,1,0:T(8,128)S(1)}, u32[]{:S(2)}, u32[]{:S(2)}) collective-permute-start(f32[4,384,128]{2,1,0:T(8,128)S(1)} %get-tuple-element.54), channel_id=1, source_target_pairs={{0,1},{1,0},{2,3},{3,2},{4,5},{5,4},{6,7},{7,6},{8,9},{9,8},{10,11... | collective-permute-start | bytes 2359304 | tf_op jit(solution)/shard_map/ppermute | solution.py:285
  53.0 9.3 %collective-permute-done.5 = f32[64,1024]{1,0:T(8,128)S(1)} collective-permute-done((f32[64,1024]{1,0:T(8,128)S(1)}, f32[64,1024]{1,0:T(8,128)S(1)}, u32[]{:S(2)}, u32[]{:S(2)}) %collective-permute-start.5) | collective-permute-done | bytes 262176 | tf_op jit(solution)/shard_map/ppermute | solution.py:284
  62.5 1.5 %collective-permute-start.14 = (f32[64,1024]{1,0:T(8,128)S(1)}, f32[64,1024]{1,0:T(8,128)S(1)}, u32[]{:S(2)}, u32[]{:S(2)}) collective-permute-start(f32[64,1024]{1,0:T(8,128)S(1)} %add_multiply_fusion), channel_id=1, source_target_pairs={{0,4},{1,5},{2,6},{3,7},{4,0},{5,1},{6,2},{7,3},{8,12},{9,13},{10,... | collective-permute-start | bytes 786440 | tf_op jit(solution)/shard_map/ppermute | solution.py:291
  64.0 1.8 %collective-permute-start.13 = (f32[64,1024]{1,0:T(8,128)S(1)}, f32[64,1024]{1,0:T(8,128)S(1)}, u32[]{:S(2)}, u32[]{:S(2)}) collective-permute-start(f32[64,1024]{1,0:T(8,128)S(1)} %add_multiply_fusion), channel_id=1, source_target_pairs={{0,6},{1,7},{2,0},{3,1},{4,2},{5,3},{6,4},{7,5},{8,14},{9,15},{10,... | collective-permute-start | bytes 786440 | tf_op jit(solution)/shard_map/ppermute | solution.py:291
  65.8 1.4 %collective-permute-start.17 = (f32[768,128]{1,0:T(8,128)S(1)}, f32[768,128]{1,0:T(8,128)S(1)}, u32[]{:S(2)}, u32[]{:S(2)}) collective-permute-start(f32[768,128]{1,0:T(8,128)S(1)} %slice.35), channel_id=1, source_target_pairs={{0,48},{8,56},{16,0},{24,8},{32,16},{40,24},{48,32},{56,40},{1,49}... | collective-permute-start | bytes 1179656 | tf_op jit(solution)/shard_map/ppermute | solution.py:282
  67.2 5.7 %collective-permute-done.15 = f32[64,1024]{1,0:T(8,128)S(1)} collective-permute-done((f32[64,1024]{1,0:T(8,128)S(1)}, f32[64,1024]{1,0:T(8,128)S(1)}, u32[]{:S(2)}, u32[]{:S(2)}) %collective-permute-start.15) | collective-permute-done | bytes 262176 | tf_op jit(solution)/shard_map/ppermute | solution.py:291
  72.9 1.5 %collective-permute-start.16 = (f32[768,128]{1,0:T(8,128)S(1)}, f32[768,128]{1,0:T(8,128)S(1)}, u32[]{:S(2)}, u32[]{:S(2)}) collective-permute-start(f32[768,128]{1,0:T(8,128)S(1)} %slice.34), channel_id=1, source_target_pairs={{0,16},{8,24},{16,32},{24,40},{32,48},{40,56},{48,0},{56,8},{1,17}... | collective-permute-start | bytes 1179656 | tf_op jit(solution)/shard_map/ppermute | solution.py:281
  74.5 2.3 %collective-permute-done.18 = f32[4,384,128]{2,1,0:T(8,128)S(1)} collective-permute-done((f32[4,384,128]{2,1,0:T(8,128)S(1)}, f32[4,384,128]{2,1,0:T(8,128)S(1)}, u32[]{:S(2)}, u32[]{:S(2)}) %collective-permute-start.18) | collective-permute-done | bytes 786464 | tf_op jit(solution)/shard_map/ppermute | solution.py:285
  76.8 0.8 copy-done.2
  77.6 3.1 %collective-permute-done.16.a2.b2 = f32[768,128]{1,0:T(8,128)S(1)} collective-permute-done((f32[768,128]{1,0:T(8,128)S(1)}, f32[768,128]{1,0:T(8,128)S(1)}, u32[]{:S(2)}, u32[]{:S(2)}) %collective-permute-start.16) | collective-permute-done | bytes 393248 | tf_op jit(solution)/shard_map/ppermute | solution.py:281
  81.4 1.6 %add.115 = f32[4,384,128]{2,1,0:T(8,128)S(1)} add(f32[4,384,128]{2,1,0:T(8,128)} %copy-done.10, f32[4,384,128]{2,1,0:T(8,128)} %copy-done.13) | non-fusion elementwise | flops 196608 | bytes 2359296 | tf_op jit(solution)/shard_map/add | solution.py:300
  83.0 0.9 constant_dynamic-slice_fusion.1
  83.9 2.0 %collective-permute-start.22 = (f32[256,128]{1,0:T(8,128)S(1)}, f32[256,128]{1,0:T(8,128)S(1)}, u32[]{:S(2)}, u32[]{:S(2)}) collective-permute-start(f32[256,128]{1,0:T(8,128)S(1)} %constant_dynamic-slice_fusion.1), channel_id=1, source_target_pairs={{0,1},{1,0},{2,3},{3,2},{4,5},{5,4},{6,7},{7,6},{8,9},{9,8},{10,11... | collective-permute-start | bytes 393224 | tf_op jit(solution)/shard_map/ppermute | solution.py:299
  86.1 2.0 %collective-permute-start.11 = (f32[384,128]{1,0:T(8,128)S(1)}, f32[384,128]{1,0:T(8,128)S(1)}, u32[]{:S(2)}, u32[]{:S(2)}) collective-permute-start(f32[384,128]{1,0:T(8,128)S(1)} %get-tuple-element.63), channel_id=1, source_target_pairs={{0,2},{1,3},{2,4},{3,5},{4,6},{5,7},{6,0},{7,1},{8,10},{9,11},{10,... | collective-permute-start | bytes 589832 | tf_op jit(solution)/shard_map/ppermute | solution.py:245
  88.1 2.0 %collective-permute-done.22 = f32[256,128]{1,0:T(8,128)S(1)} collective-permute-done((f32[256,128]{1,0:T(8,128)S(1)}, f32[256,128]{1,0:T(8,128)S(1)}, u32[]{:S(2)}, u32[]{:S(2)}) %collective-permute-start.22) | collective-permute-done | bytes 131104 | tf_op jit(solution)/shard_map/ppermute | solution.py:299
  90.2 0.9 add_convert_fusion
  91.1 1.0 copy-done.3
  92.1 1.0 copy-done.5
  93.1 0.9 copy-done.7
  94.0 3.7 %scores.1 = f32[16,1024]{1,0:T(8,128)S(1)} custom-call(s32[4]{0:T(128)S(1)} %pad_add_fusion.idx, bf16[1024,128]{1,0:T(8,128)(2,1)S(1)} %copy-done.7, bf16[2048,128]{1,0:T(8,128)(2,1)S(1)} %bitcast.45, f32[1792,128]{1,0:T(8,128)S(1)} %collective-permute-done.3.a1.b1, f32[1792,128]{1,0:T(8,128)S(1)} %collective-permute-done.3.a1.b1, ...), custom_call_target="tpu_custom_call" | custom-call | tf_op jit(solution)/shard_map/scores/pallas_call | solution.py:229
  97.9 0.8 collective-permute-done.11
  99.0 1.2 collective-permute-start.27
  101.1 1.8 %collective-permute-start.25 = (f32[8,1024]{1,0:T(8,128)S(1)}, f32[8,1024]{1,0:T(8,128)S(1)}, u32[]{:S(2)}, u32[]{:S(2)}) collective-permute-start(f32[8,1024]{1,0:T(8,128)S(1)} %dynamic-slice_add_fusion), channel_id=1, source_target_pairs={{0,4},{1,5},{2,6},{3,7},{4,0},{5,1},{6,2},{7,3},{8,12},{9,13},{10,... | collective-permute-start | bytes 98312 | tf_op jit(solution)/shard_map/ppermute | solution.py:245
  102.9 1.1 collective-permute-start.21
  104.0 1.0 collective-permute-start.20
  105.0 1.7 %collective-permute-start.19 = (f32[384,128]{1,0:T(8,128)S(1)}, f32[384,128]{1,0:T(8,128)S(1)}, u32[]{:S(2)}, u32[]{:S(2)}) collective-permute-start(f32[384,128]{1,0:T(8,128)S(1)} %get-tuple-element.67), channel_id=1, source_target_pairs={{0,4},{1,5},{2,6},{3,7},{4,0},{5,1},{6,2},{7,3},{8,12},{9,13},{10,... | collective-permute-start | bytes 589832 | tf_op jit(solution)/shard_map/ppermute | solution.py:245
  106.8 1.8 %collective-permute-start.28 = (f32[8,1024]{1,0:T(8,128)S(1)}, f32[8,1024]{1,0:T(8,128)S(1)}, u32[]{:S(2)}, u32[]{:S(2)}) collective-permute-start(f32[8,1024]{1,0:T(8,128)S(1)} %add_add_fusion.2), channel_id=1, source_target_pairs={{0,1},{1,0},{2,3},{3,2},{4,5},{5,4},{6,7},{7,6},{8,9},{9,8},{10,11... | collective-permute-start | bytes 98312 | tf_op jit(solution)/shard_map/ppermute | solution.py:308
  108.6 2.1 %collective-permute-done.21 = f32[384,128]{1,0:T(8,128)S(1)} collective-permute-done((f32[384,128]{1,0:T(8,128)S(1)}, f32[384,128]{1,0:T(8,128)S(1)}, u32[]{:S(2)}, u32[]{:S(2)}) %collective-permute-start.21) | collective-permute-done | bytes 196640 | tf_op jit(solution)/shard_map/ppermute | solution.py:245
  110.7 4.7 %collective-permute-done.20 = f32[384,128]{1,0:T(8,128)S(1)} collective-permute-done((f32[384,128]{1,0:T(8,128)S(1)}, f32[384,128]{1,0:T(8,128)S(1)}, u32[]{:S(2)}, u32[]{:S(2)}) %collective-permute-start.20) | collective-permute-done | bytes 196640 | tf_op jit(solution)/shard_map/ppermute | solution.py:245
  115.5 6.2 %collective-permute-start.31 = (f32[8,128]{1,0:T(8,128)S(1)}, f32[8,128]{1,0:T(8,128)S(1)}, u32[]{:S(2)}, u32[]{:S(2)}) collective-permute-start(f32[8,128]{1,0:T(8,128)S(1)} %get-tuple-element.60), channel_id=1, source_target_pairs={{0,192},{64,0},{128,64},{192,128},{1,193},{65,1},{129,65},{193,129... | collective-permute-start | bytes 12296 | tf_op jit(solution)/shard_map/ppermute | solution.py:311
  121.7 3.8 %collective-permute-start.29 = (f32[8,128]{1,0:T(8,128)S(1)}, f32[8,128]{1,0:T(8,128)S(1)}, u32[]{:S(2)}, u32[]{:S(2)}) collective-permute-start(f32[8,128]{1,0:T(8,128)S(1)} %get-tuple-element.60), channel_id=1, source_target_pairs={{0,128},{64,192},{128,0},{192,64},{1,129},{65,193},{129,1},{193,65... | collective-permute-start | bytes 12296 | tf_op jit(solution)/shard_map/ppermute | solution.py:311
  126.2 1.2 collective-permute-done.30
  127.4 1.8 %collective-permute-done.29 = f32[8,128]{1,0:T(8,128)S(1)} collective-permute-done((f32[8,128]{1,0:T(8,128)S(1)}, f32[8,128]{1,0:T(8,128)S(1)}, u32[]{:S(2)}, u32[]{:S(2)}) %collective-permute-start.29) | collective-permute-done | bytes 4128 | tf_op jit(solution)/shard_map/ppermute | solution.py:311
  (78 shorter events, 6.0 us)
Async XLA Ops:
  0.6 20.2 %copy-start.14 = (f32[8,32]{1,0:T(8,128)S(1)}, f32[8,32]{1,0:T(8,128)}, u32[]{:S(2)}) copy-start(f32[8,32]{1,0:T(8,128)} %param.11) | copy-start | bytes 3076
  0.8 1.0 copy-start
  1.8 0.9 copy-start.6
  4.7 34.4 %collective-permute-start.4 = (f32[1792,128]{1,0:T(8,128)}, f32[1792,128]{1,0:T(8,128)S(1)}, u32[]{:S(2)}, u32[]{:S(2)}) collective-permute-start(f32[1792,128]{1,0:T(8,128)} %get-tuple-element.39), channel_id=1, source_target_pairs={{0,48},{8,56},{16,0},{24,8},{32,16},{40,24},{48,32},{56,40},{1,49}... | collective-permute-start | bytes 2752520 | tf_op jit(solution)/shard_map/ppermute | solution.py:263
  6.9 35.8 %collective-permute-start.3 = (f32[1792,128]{1,0:T(8,128)}, f32[1792,128]{1,0:T(8,128)S(1)}, u32[]{:S(2)}, u32[]{:S(2)}) collective-permute-start(f32[1792,128]{1,0:T(8,128)} %get-tuple-element.31), channel_id=1, source_target_pairs={{0,16},{8,24},{16,32},{24,40},{32,48},{40,56},{48,0},{56,8},{1,17}... | collective-permute-start | bytes 2752520 | tf_op jit(solution)/shard_map/ppermute | solution.py:263
  14.7 21.6 %collective-permute-start = (f32[64,1024]{1,0:T(8,128)}, f32[64,1024]{1,0:T(8,128)}, u32[]{:S(2)}, u32[]{:S(2)}) collective-permute-start(f32[64,1024]{1,0:T(8,128)} %get-tuple-element.36), channel_id=1, source_target_pairs={{0,4},{1,5},{2,6},{3,7},{4,0},{5,1},{6,2},{7,3},{8,12},{9,13},{10,... | collective-permute-start | bytes 786440 | tf_op jit(solution)/shard_map/ppermute | solution.py:245
  17.6 20.6 %collective-permute-start.1 = (f32[64,1024]{1,0:T(8,128)}, f32[64,1024]{1,0:T(8,128)}, u32[]{:S(2)}, u32[]{:S(2)}) collective-permute-start(f32[64,1024]{1,0:T(8,128)} %get-tuple-element.37), channel_id=1, source_target_pairs={{0,2},{1,3},{2,4},{3,5},{4,6},{5,7},{6,0},{7,1},{8,10},{9,11},{10,... | collective-permute-start | bytes 786440 | tf_op jit(solution)/shard_map/ppermute | solution.py:245
  18.3 19.9 %collective-permute-start.2 = (f32[64,1024]{1,0:T(8,128)S(1)}, f32[64,1024]{1,0:T(8,128)}, u32[]{:S(2)}, u32[]{:S(2)}) collective-permute-start(f32[64,1024]{1,0:T(8,128)S(1)} %get-tuple-element.38), channel_id=1, source_target_pairs={{0,6},{1,7},{2,0},{3,1},{4,2},{5,3},{6,4},{7,5},{8,14},{9,15},{10,... | collective-permute-start | bytes 786440 | tf_op jit(solution)/shard_map/ppermute | solution.py:245
  28.2 0.9 copy-start.10
  36.2 26.2 %collective-permute-start.6 = (f32[4,384,128]{2,1,0:T(8,128)S(1)}, f32[4,384,128]{2,1,0:T(8,128)S(1)}, u32[]{:S(2)}, u32[]{:S(2)}) collective-permute-start(f32[4,384,128]{2,1,0:T(8,128)S(1)} %get-tuple-element.41), channel_id=1, source_target_pairs={{0,1},{1,0},{2,3},{3,2},{4,5},{5,4},{6,7},{7,6},{8,9},{9,8},{10,11... | collective-permute-start | bytes 2359304 | tf_op jit(solution)/shard_map/ppermute | solution.py:271
  38.2 12.0 %collective-permute-start.7 = (f32[256,256]{1,0:T(8,128)}, f32[256,256]{1,0:T(8,128)S(1)}, u32[]{:S(2)}, u32[]{:S(2)}) collective-permute-start(f32[256,256]{1,0:T(8,128)} %get-tuple-element.44), channel_id=1, source_target_pairs={{0,4},{1,5},{2,6},{3,7},{4,0},{5,1},{6,2},{7,3},{8,12},{9,13},{10,... | collective-permute-start | bytes 786440 | tf_op jit(solution)/shard_map/ppermute | solution.py:245
  38.2 14.1 %collective-permute-start.8 = (f32[256,256]{1,0:T(8,128)}, f32[256,256]{1,0:T(8,128)S(1)}, u32[]{:S(2)}, u32[]{:S(2)}) collective-permute-start(f32[256,256]{1,0:T(8,128)} %get-tuple-element.45), channel_id=1, source_target_pairs={{0,2},{1,3},{2,4},{3,5},{4,6},{5,7},{6,0},{7,1},{8,10},{9,11},{10,... | collective-permute-start | bytes 786440 | tf_op jit(solution)/shard_map/ppermute | solution.py:245
  39.1 13.2 %collective-permute-start.9 = (f32[256,256]{1,0:T(8,128)}, f32[256,256]{1,0:T(8,128)S(1)}, u32[]{:S(2)}, u32[]{:S(2)}) collective-permute-start(f32[256,256]{1,0:T(8,128)} %get-tuple-element.46), channel_id=1, source_target_pairs={{0,6},{1,7},{2,0},{3,1},{4,2},{5,3},{6,4},{7,5},{8,14},{9,15},{10,... | collective-permute-start | bytes 786440 | tf_op jit(solution)/shard_map/ppermute | solution.py:245
  42.7 19.6 %collective-permute-start.5 = (f32[64,1024]{1,0:T(8,128)S(1)}, f32[64,1024]{1,0:T(8,128)S(1)}, u32[]{:S(2)}, u32[]{:S(2)}) collective-permute-start(f32[64,1024]{1,0:T(8,128)S(1)} %add_add_fusion.1), channel_id=1, source_target_pairs={{0,1},{1,0},{2,3},{3,2},{4,5},{5,4},{6,7},{7,6},{8,9},{9,8},{10,11... | collective-permute-start | bytes 786440 | tf_op jit(solution)/shard_map/ppermute | solution.py:284
  50.2 30.5 %copy-start.8 = (f32[4,384,128]{2,1,0:T(8,128)}, f32[4,384,128]{2,1,0:T(8,128)S(1)}, u32[]{:S(2)}) copy-start(f32[4,384,128]{2,1,0:T(8,128)S(1)} %get-tuple-element.50) | copy-start | bytes 2359300
  50.2 40.9 %copy-start.1 = (bf16[64,32,128]{2,1,0:T(8,128)(2,1)S(1)}, bf16[64,32,128]{2,1,0:T(8,128)(2,1)}, u32[]{:S(2)}) copy-start(bf16[64,32,128]{2,1,0:T(8,128)(2,1)} %param.10) | copy-start | bytes 1572868
  50.2 26.6 %collective-permute-start.18 = (f32[4,384,128]{2,1,0:T(8,128)S(1)}, f32[4,384,128]{2,1,0:T(8,128)S(1)}, u32[]{:S(2)}, u32[]{:S(2)}) collective-permute-start(f32[4,384,128]{2,1,0:T(8,128)S(1)} %get-tuple-element.54), channel_id=1, source_target_pairs={{0,1},{1,0},{2,3},{3,2},{4,5},{5,4},{6,7},{7,6},{8,9},{9,8},{10,11... | collective-permute-start | bytes 2359304 | tf_op jit(solution)/shard_map/ppermute | solution.py:285
  62.4 18.3 %copy-start.13 = (f32[4,384,128]{2,1,0:T(8,128)}, f32[4,384,128]{2,1,0:T(8,128)S(1)}, u32[]{:S(2)}) copy-start(f32[4,384,128]{2,1,0:T(8,128)S(1)} %collective-permute-done.6) | copy-start | bytes 2359300
  62.4 10.5 %collective-permute-start.15 = (f32[64,1024]{1,0:T(8,128)S(1)}, f32[64,1024]{1,0:T(8,128)S(1)}, u32[]{:S(2)}, u32[]{:S(2)}) collective-permute-start(f32[64,1024]{1,0:T(8,128)S(1)} %add_multiply_fusion), channel_id=1, source_target_pairs={{0,2},{1,3},{2,4},{3,5},{4,6},{5,7},{6,0},{7,1},{8,10},{9,11},{10,... | collective-permute-start | bytes 786440 | tf_op jit(solution)/shard_map/ppermute | solution.py:291
  62.5 11.9 %collective-permute-start.14 = (f32[64,1024]{1,0:T(8,128)S(1)}, f32[64,1024]{1,0:T(8,128)S(1)}, u32[]{:S(2)}, u32[]{:S(2)}) collective-permute-start(f32[64,1024]{1,0:T(8,128)S(1)} %add_multiply_fusion), channel_id=1, source_target_pairs={{0,4},{1,5},{2,6},{3,7},{4,0},{5,1},{6,2},{7,3},{8,12},{9,13},{10,... | collective-permute-start | bytes 786440 | tf_op jit(solution)/shard_map/ppermute | solution.py:291
  64.0 10.4 %collective-permute-start.13 = (f32[64,1024]{1,0:T(8,128)S(1)}, f32[64,1024]{1,0:T(8,128)S(1)}, u32[]{:S(2)}, u32[]{:S(2)}) collective-permute-start(f32[64,1024]{1,0:T(8,128)S(1)} %add_multiply_fusion), channel_id=1, source_target_pairs={{0,6},{1,7},{2,0},{3,1},{4,2},{5,3},{6,4},{7,5},{8,14},{9,15},{10,... | collective-permute-start | bytes 786440 | tf_op jit(solution)/shard_map/ppermute | solution.py:291
  65.8 11.0 %collective-permute-start.17 = (f32[768,128]{1,0:T(8,128)S(1)}, f32[768,128]{1,0:T(8,128)S(1)}, u32[]{:S(2)}, u32[]{:S(2)}) collective-permute-start(f32[768,128]{1,0:T(8,128)S(1)} %slice.35), channel_id=1, source_target_pairs={{0,48},{8,56},{16,0},{24,8},{32,16},{40,24},{48,32},{56,40},{1,49}... | collective-permute-start | bytes 1179656 | tf_op jit(solution)/shard_map/ppermute | solution.py:282
  72.9 7.8 %collective-permute-start.16 = (f32[768,128]{1,0:T(8,128)S(1)}, f32[768,128]{1,0:T(8,128)S(1)}, u32[]{:S(2)}, u32[]{:S(2)}) collective-permute-start(f32[768,128]{1,0:T(8,128)S(1)} %slice.34), channel_id=1, source_target_pairs={{0,16},{8,24},{16,32},{24,40},{32,48},{40,56},{48,0},{56,8},{1,17}... | collective-permute-start | bytes 1179656 | tf_op jit(solution)/shard_map/ppermute | solution.py:281
  76.8 3.9 %copy-start.11 = (f32[4,384,128]{2,1,0:T(8,128)}, f32[4,384,128]{2,1,0:T(8,128)S(1)}, u32[]{:S(2)}) copy-start(f32[4,384,128]{2,1,0:T(8,128)S(1)} %collective-permute-done.18) | copy-start | bytes 2359300
  76.8 0.8 copy-start.2
  80.7 0.7 copy-start.4
  81.4 9.6 %collective-permute-start.23 = (f32[4,64,1024]{2,1,0:T(8,128)S(1)}, f32[4,64,1024]{2,1,0:T(8,128)}, u32[]{:S(2)}, u32[]{:S(2)}) collective-permute-start(f32[4,64,1024]{2,1,0:T(8,128)S(1)} %pad_maximum_fusion.mine), channel_id=1, source_target_pairs={{0,8},{8,0},{16,24},{24,16},{32,40},{40,32},{48,56},{56,48},{1,9},... | collective-permute-start | bytes 3145736 | tf_op jit(solution)/shard_map/ppermute | solution.py:294
  81.4 17.3 %copy-start.9 = (f32[4,384,128]{2,1,0:T(8,128)S(1)}, f32[4,384,128]{2,1,0:T(8,128)}, u32[]{:S(2)}) copy-start(f32[4,384,128]{2,1,0:T(8,128)} %copy-done.8) | copy-start | bytes 2359300
  81.4 17.3 %copy-start.12 = (f32[4,384,128]{2,1,0:T(8,128)S(1)}, f32[4,384,128]{2,1,0:T(8,128)}, u32[]{:S(2)}) copy-start(f32[4,384,128]{2,1,0:T(8,128)} %copy-done.11) | copy-start | bytes 2359300
  83.9 6.2 %collective-permute-start.22 = (f32[256,128]{1,0:T(8,128)S(1)}, f32[256,128]{1,0:T(8,128)S(1)}, u32[]{:S(2)}, u32[]{:S(2)}) collective-permute-start(f32[256,128]{1,0:T(8,128)S(1)} %constant_dynamic-slice_fusion.1), channel_id=1, source_target_pairs={{0,1},{1,0},{2,3},{3,2},{4,5},{5,4},{6,7},{7,6},{8,9},{9,8},{10,11... | collective-permute-start | bytes 393224 | tf_op jit(solution)/shard_map/ppermute | solution.py:299
  86.0 11.8 %collective-permute-start.12 = (f32[384,128]{1,0:T(8,128)S(1)}, f32[384,128]{1,0:T(8,128)S(1)}, u32[]{:S(2)}, u32[]{:S(2)}) collective-permute-start(f32[384,128]{1,0:T(8,128)S(1)} %get-tuple-element.62), channel_id=1, source_target_pairs={{0,6},{1,7},{2,0},{3,1},{4,2},{5,3},{6,4},{7,5},{8,14},{9,15},{10,... | collective-permute-start | bytes 589832 | tf_op jit(solution)/shard_map/ppermute | solution.py:245
  86.1 12.5 %collective-permute-start.11 = (f32[384,128]{1,0:T(8,128)S(1)}, f32[384,128]{1,0:T(8,128)S(1)}, u32[]{:S(2)}, u32[]{:S(2)}) collective-permute-start(f32[384,128]{1,0:T(8,128)S(1)} %get-tuple-element.63), channel_id=1, source_target_pairs={{0,2},{1,3},{2,4},{3,5},{4,6},{5,7},{6,0},{7,1},{8,10},{9,11},{10,... | collective-permute-start | bytes 589832 | tf_op jit(solution)/shard_map/ppermute | solution.py:245
  88.1 10.5 %collective-permute-start.10 = (f32[384,128]{1,0:T(8,128)S(1)}, f32[384,128]{1,0:T(8,128)S(1)}, u32[]{:S(2)}, u32[]{:S(2)}) collective-permute-start(f32[384,128]{1,0:T(8,128)S(1)} %get-tuple-element.64), channel_id=1, source_target_pairs={{0,4},{1,5},{2,6},{3,7},{4,0},{5,1},{6,2},{7,3},{8,12},{9,13},{10,... | collective-permute-start | bytes 589832 | tf_op jit(solution)/shard_map/ppermute | solution.py:245
  91.1 1.0 copy-start.3
  92.1 1.0 copy-start.5
  93.1 0.9 copy-start.7
  97.7 1.3 collective-permute-start.24
  99.0 6.0 %collective-permute-start.27 = (f32[8,1024]{1,0:T(8,128)S(1)}, f32[8,1024]{1,0:T(8,128)S(1)}, u32[]{:S(2)}, u32[]{:S(2)}) collective-permute-start(f32[8,1024]{1,0:T(8,128)S(1)} %dynamic-slice_add_fusion), channel_id=1, source_target_pairs={{0,6},{1,7},{2,0},{3,1},{4,2},{5,3},{6,4},{7,5},{8,14},{9,15},{10,... | collective-permute-start | bytes 98312 | tf_op jit(solution)/shard_map/ppermute | solution.py:245
  100.3 6.5 %collective-permute-start.26 = (f32[8,1024]{1,0:T(8,128)S(1)}, f32[8,1024]{1,0:T(8,128)S(1)}, u32[]{:S(2)}, u32[]{:S(2)}) collective-permute-start(f32[8,1024]{1,0:T(8,128)S(1)} %dynamic-slice_add_fusion), channel_id=1, source_target_pairs={{0,2},{1,3},{2,4},{3,5},{4,6},{5,7},{6,0},{7,1},{8,10},{9,11},{10,... | collective-permute-start | bytes 98312 | tf_op jit(solution)/shard_map/ppermute | solution.py:245
  101.1 5.7 %collective-permute-start.25 = (f32[8,1024]{1,0:T(8,128)S(1)}, f32[8,1024]{1,0:T(8,128)S(1)}, u32[]{:S(2)}, u32[]{:S(2)}) collective-permute-start(f32[8,1024]{1,0:T(8,128)S(1)} %dynamic-slice_add_fusion), channel_id=1, source_target_pairs={{0,4},{1,5},{2,6},{3,7},{4,0},{5,1},{6,2},{7,3},{8,12},{9,13},{10,... | collective-permute-start | bytes 98312 | tf_op jit(solution)/shard_map/ppermute | solution.py:245
  102.9 7.8 %collective-permute-start.21 = (f32[384,128]{1,0:T(8,128)S(1)}, f32[384,128]{1,0:T(8,128)S(1)}, u32[]{:S(2)}, u32[]{:S(2)}) collective-permute-start(f32[384,128]{1,0:T(8,128)S(1)} %get-tuple-element.65), channel_id=1, source_target_pairs={{0,6},{1,7},{2,0},{3,1},{4,2},{5,3},{6,4},{7,5},{8,14},{9,15},{10,... | collective-permute-start | bytes 589832 | tf_op jit(solution)/shard_map/ppermute | solution.py:245
  104.0 11.4 %collective-permute-start.20 = (f32[384,128]{1,0:T(8,128)S(1)}, f32[384,128]{1,0:T(8,128)S(1)}, u32[]{:S(2)}, u32[]{:S(2)}) collective-permute-start(f32[384,128]{1,0:T(8,128)S(1)} %get-tuple-element.66), channel_id=1, source_target_pairs={{0,2},{1,3},{2,4},{3,5},{4,6},{5,7},{6,0},{7,1},{8,10},{9,11},{10,... | collective-permute-start | bytes 589832 | tf_op jit(solution)/shard_map/ppermute | solution.py:245
  105.0 10.4 %collective-permute-start.19 = (f32[384,128]{1,0:T(8,128)S(1)}, f32[384,128]{1,0:T(8,128)S(1)}, u32[]{:S(2)}, u32[]{:S(2)}) collective-permute-start(f32[384,128]{1,0:T(8,128)S(1)} %get-tuple-element.67), channel_id=1, source_target_pairs={{0,4},{1,5},{2,6},{3,7},{4,0},{5,1},{6,2},{7,3},{8,12},{9,13},{10,... | collective-permute-start | bytes 589832 | tf_op jit(solution)/shard_map/ppermute | solution.py:245
  106.8 8.7 %collective-permute-start.28 = (f32[8,1024]{1,0:T(8,128)S(1)}, f32[8,1024]{1,0:T(8,128)S(1)}, u32[]{:S(2)}, u32[]{:S(2)}) collective-permute-start(f32[8,1024]{1,0:T(8,128)S(1)} %add_add_fusion.2), channel_id=1, source_target_pairs={{0,1},{1,0},{2,3},{3,2},{4,5},{5,4},{6,7},{7,6},{8,9},{9,8},{10,11... | collective-permute-start | bytes 98312 | tf_op jit(solution)/shard_map/ppermute | solution.py:308
  115.5 10.7 %collective-permute-start.31 = (f32[8,128]{1,0:T(8,128)S(1)}, f32[8,128]{1,0:T(8,128)S(1)}, u32[]{:S(2)}, u32[]{:S(2)}) collective-permute-start(f32[8,128]{1,0:T(8,128)S(1)} %get-tuple-element.60), channel_id=1, source_target_pairs={{0,192},{64,0},{128,64},{192,128},{1,193},{65,1},{129,65},{193,129... | collective-permute-start | bytes 12296 | tf_op jit(solution)/shard_map/ppermute | solution.py:311
  121.7 5.7 %collective-permute-start.30 = (f32[8,128]{1,0:T(8,128)S(1)}, f32[8,128]{1,0:T(8,128)S(1)}, u32[]{:S(2)}, u32[]{:S(2)}) collective-permute-start(f32[8,128]{1,0:T(8,128)S(1)} %get-tuple-element.60), channel_id=1, source_target_pairs={{0,64},{64,128},{128,192},{192,0},{1,65},{65,129},{129,193},{193,1... | collective-permute-start | bytes 12296 | tf_op jit(solution)/shard_map/ppermute | solution.py:311
  121.7 7.5 %collective-permute-start.29 = (f32[8,128]{1,0:T(8,128)S(1)}, f32[8,128]{1,0:T(8,128)S(1)}, u32[]{:S(2)}, u32[]{:S(2)}) collective-permute-start(f32[8,128]{1,0:T(8,128)S(1)} %get-tuple-element.60), channel_id=1, source_target_pairs={{0,128},{64,192},{128,0},{192,64},{1,129},{65,193},{129,1},{193,65... | collective-permute-start | bytes 12296 | tf_op jit(solution)/shard_map/ppermute | solution.py:311

commit v3 on v0

v3 whole, which is shorter than its diff:
```python
import functools
import math

import jax
import jax.numpy as jnp
from jax import lax
from jax.experimental import pallas as pl
from jax.experimental.pallas import tpu as pltpu
from jax.sharding import PartitionSpec as P

F32 = jnp.float32
MIB = 1 << 20
WHOLE = pl.BlockSpec(memory_space=pltpu.VMEM)


def x_ring():
    return [(p, ((p // 2 + 1 - 2 * (p % 2)) % 4) * 2 + p % 2) for p in range(8)]


def core_swap():
    return [(p, p ^ 1) for p in range(8)]


def y_shift(d):
    return [(t, ((t // 2 + d) % 4) * 2 + t % 2) for t in range(8)]


def z_swap():
    return [(t, t ^ 1) for t in range(8)]


def dp_shift(d):
    return [(i, (i + d) % 4) for i in range(4)]


def params(limit):
    return pltpu.CompilerParams(vmem_limit_bytes=limit)


def cost():
    return pl.CostEstimate(flops=0, bytes_accessed=0, transcendentals=0)


def in_hbm(value):
    return pltpu.with_memory_space_constraint(value, pltpu.HBM)


def in_vmem(value):
    return pltpu.with_memory_space_constraint(value, pltpu.VMEM)


def after(value, *others):
    return lax.optimization_barrier((value, *others))[0]


def pack_kernel(idx, og_hbm, gf_hbm, mine, other, og, gf, sems):
    copies = [
        pltpu.make_async_copy(src, dst, sems.at[i])
        for i, (src, dst) in enumerate(((og_hbm, og), (gf_hbm, gf)))
    ]
    for copy in copies:
        copy.start()
    tokens = og.shape[0]
    rows = gf.shape[0] // 4

    def gf_rows(distance):
        start = lax.rem(idx[0] + distance, 4) * rows
        return gf[pl.ds(pl.multiple_of(start, rows), rows), :].astype(F32)

    copies[0].wait()
    wide = og[...].astype(F32)
    other[rows : rows + tokens, :] = wide
    mine[rows : rows + tokens, :] = wide
    copies[1].wait()
    other[:rows, :] = gf_rows(3 - 2 * idx[1])
    mine[:rows, :] = gf_rows(1 + 2 * idx[1])
    mine[rows + tokens :, :] = gf_rows(2)


def pack(idx, og, gf):
    tokens, width = og.shape
    rows = gf.shape[0] // 4
    return pl.pallas_call(
        pack_kernel,
        grid_spec=pltpu.PrefetchScalarGridSpec(
            num_scalar_prefetch=1,
            grid=(),
            in_specs=[pl.BlockSpec(memory_space=pltpu.HBM)] * 2,
            out_specs=[WHOLE] * 2,
            scratch_shapes=[
                pltpu.VMEM(og.shape, og.dtype),
                pltpu.VMEM(gf.shape, gf.dtype),
                pltpu.SemaphoreType.DMA((2,)),
            ],
        ),
        out_shape=[
            jax.ShapeDtypeStruct((r, width), F32) for r in (tokens + 2 * rows, tokens + rows)
        ],
        compiler_params=params(16 * MIB),
        cost_estimate=cost(),
        name="pack",
    )(idx, in_hbm(og), in_hbm(gf))


def act_kernel(idx, af_hbm, a_hbm, out0, out1, out2, out3, a, af, scratch, sems):
    outs = (out0, out1, out2, out3)
    rows = out0.shape[0]
    tile = scratch.shape[1]
    steps = a.shape[0] // tile

    def rows_of(i):
        return pl.ds(i * tile, tile)

    copies = [pltpu.make_async_copy(af_hbm, af, sems.at[steps])] + [
        pltpu.make_async_copy(a_hbm.at[rows_of(i), :], a.at[rows_of(i), :], sems.at[i])
        for i in range(steps)
    ]
    for copy in copies:
        copy.start()
    copies[0].wait()
    for i in range(steps):
        copies[1 + i].wait()
        scratch[...] = lax.dot_general(
            af[...], a[rows_of(i), :], (((1,), (1,)), ((), ())), preferred_element_type=F32
        )
        for j, out in enumerate(outs):
            start = pl.multiple_of(lax.rem(idx[2] + j, 4) * rows, rows)
            out[:, rows_of(i)] = scratch[pl.ds(start, rows), :]


def act_pieces(idx, af, a):
    qr, tokens = af.shape[0], a.shape[0]
    steps = 4
    return pl.pallas_call(
        act_kernel,
        grid_spec=pltpu.PrefetchScalarGridSpec(
            num_scalar_prefetch=1,
            grid=(),
            in_specs=[pl.BlockSpec(memory_space=pltpu.HBM)] * 2,
            out_specs=[WHOLE] * 5,
            scratch_shapes=[
                pltpu.VMEM(af.shape, af.dtype),
                pltpu.VMEM((qr, tokens // steps), F32),
                pltpu.SemaphoreType.DMA((steps + 1,)),
            ],
        ),
        out_shape=[jax.ShapeDtypeStruct((qr // 4, tokens), F32)] * 4
        + [jax.ShapeDtypeStruct(a.shape, a.dtype)],
        compiler_params=params(24 * MIB),
        cost_estimate=cost(),
        name="act",
    )(idx, in_hbm(af), in_hbm(a))


def layer_z_kernel(idx, a, w_in, keep, send, *rest, first, relative):
    rows, half = keep.shape[1:]
    width = 2 * half

    def columns(j):
        owner = lax.rem(idx[2] + j, 4) if relative else j
        return pl.ds(pl.multiple_of(owner * width, width), width)

    def step(j, w):
        acc = jnp.dot(
            a[first : first + rows, :], w[:, columns(j)], preferred_element_type=F32
        )
        low, high = acc[:, :half], acc[:, half:]
        at_low = idx[3] == 0
        keep[j] = jnp.where(at_low, low, high)
        send[j] = jnp.where(at_low, high, low)

    if rest:
        w, sems = rest
        copies = [
            pltpu.make_async_copy(w_in.at[:, columns(j)], w.at[:, columns(j)], sems.at[j])
            for j in range(4)
        ]
        for copy in copies:
            copy.start()
        for j in range(4):
            copies[j].wait()
            step(j, w)
    else:
        pl.loop(0, 4)(lambda j: step(j, w_in))


def layer_z_first(idx, a, w, first, rows, relative, load=False):
    shape = jax.ShapeDtypeStruct((4, rows, w.shape[1] // 8), F32)
    return pl.pallas_call(
        functools.partial(layer_z_kernel, first=first, relative=relative),
        grid_spec=pltpu.PrefetchScalarGridSpec(
            num_scalar_prefetch=1,
            grid=(),
            in_specs=[WHOLE, pl.BlockSpec(memory_space=pltpu.HBM) if load else WHOLE],
            out_specs=[WHOLE] * (2 + load),
            scratch_shapes=[pltpu.SemaphoreType.DMA((4,))] * load,
        ),
        out_shape=[shape] * 2 + [jax.ShapeDtypeStruct(w.shape, w.dtype)] * load,
        compiler_params=params(24 * MIB),
        cost_estimate=cost(),
        name="layer_z",
    )(idx, in_vmem(a), in_hbm(w) if load else in_vmem(w))


def layer_y_kernel(idx, a, w, out, *, first):
    _, rows, width = out.shape

    @pl.loop(0, 4)
    def _(j):
        start = pl.multiple_of(j * width, width)
        out[j] = jnp.dot(
            a[first : first + rows, :], w[:, pl.ds(start, width)], preferred_element_type=F32
        )


def layer_y_first(idx, a, w, first, rows):
    return pl.pallas_call(
        functools.partial(layer_y_kernel, first=first),
        grid_spec=pltpu.PrefetchScalarGridSpec(
            num_scalar_prefetch=1, grid=(), in_specs=[WHOLE] * 2, out_specs=WHOLE
        ),
        out_shape=jax.ShapeDtypeStruct((4, rows, w.shape[1] // 4), F32),
        compiler_params=params(24 * MIB),
        cost_estimate=cost(),
        name="layer_y",
    )(idx, in_vmem(a), in_vmem(w))


def score_kernel(idx, og, gf, a1, b1, a2, b2, a3, b3, mine, other, out, *, ranks):
    bf = jnp.bfloat16
    lhs = jnp.concatenate([gf[...]] + [b[...].astype(bf) for b in (b1, b2, b3)], axis=1)
    rhs = jnp.concatenate([og[...]] + [a[...].astype(bf) for a in (a1, a2, a3)], axis=1)
    grad = lax.dot_general(lhs, rhs, (((1,), (1,)), ((), ())), preferred_element_type=F32)
    rows = mine.shape[1]
    parts = []
    for c in range(2):
        for b in range(4):
            j = lax.rem(b + 4 - idx[2], 4)
            act = jnp.where(idx[1] == c, mine[j], other[j])
            at = (c * 4 + b) * rows
            product = grad[at : at + rows, :] * act
            for q in range(0, rows, ranks):
                parts.append(jnp.sum(product[q : q + ranks], axis=0, keepdims=True))
    out[...] = jnp.concatenate(parts, axis=0)


def scores(idx, og, gf, near, far, mine, other, ranks):
    tokens, width = og.shape
    qr = gf.shape[0] // 4
    tile = 256
    assert qr % tile == 0 and tokens % qr == 0
    spec = lambda rows, at: pl.BlockSpec((rows, width), lambda i, idx: (at(i, idx), 0))
    skip, step = qr // tile, (tokens + 2 * qr) // tile
    in_specs = [
        spec(tile, lambda i, idx: i),
        spec(qr, lambda i, idx: idx[0]),
        spec(tile, lambda i, idx: skip + i),
        spec(qr, lambda i, idx: 0),
        spec(tile, lambda i, idx: step + skip + i),
        spec(qr, lambda i, idx: tokens // qr + 2),
        spec(tile, lambda i, idx: i),
        spec(qr, lambda i, idx: tokens // qr),
    ]
    args = [og, gf, near, near, near, near, far, far]
    for act in (mine, other):
        in_specs.append(pl.BlockSpec((4, act.shape[1], tile), lambda i, idx: (0, 0, i)))
        args.append(act)
    return pl.pallas_call(
        functools.partial(score_kernel, ranks=ranks),
        grid_spec=pltpu.PrefetchScalarGridSpec(
            num_scalar_prefetch=1,
            grid=(tokens // tile,),
            in_specs=in_specs,
            out_specs=pl.BlockSpec((qr // ranks, tile), lambda i, idx: (0, i)),
        ),
        out_shape=jax.ShapeDtypeStruct((qr // ranks, tokens), F32),
        compiler_params=params(24 * MIB),
        cost_estimate=cost(),
        name="scores",
    )(idx, *args)


def along_y(parts, shifts=(1, 3, 2)):
    got = [lax.ppermute(parts[j], "tensor", y_shift(j)) for j in shifts]
    return (parts[0] + got[2]) + (got[0] + got[1])


def scatter_y(parts):
    groups = [[2 * i + z for i in range(4)] for z in range(2)]
    return lax.psum_scatter(parts, "tensor", scatter_dimension=0, axis_index_groups=groups)


def body(activations, down_weight, output_grads, act_factors, grad_factors, rank_weight):
    tokens = activations.shape[0]
    queries, ranks, hidden = act_factors.shape
    pipe, tensor = lax.axis_index("pipe"), lax.axis_index("tensor")
    x, core, y, z = pipe // 2, pipe % 2, tensor // 2, tensor % 2
    idx = jnp.stack([x, core, y, z]).astype(jnp.int32)
    gf = grad_factors.reshape(-1, grad_factors.shape[2])

    swap = functools.partial(lax.ppermute, axis_name="pipe", perm=core_swap())
    ring = functools.partial(lax.ppermute, axis_name="pipe", perm=x_ring())
    packed, other = pack(idx, output_grads, gf)
    got = swap(other)
    at = after(idx, packed)
    *pieces, held = act_pieces(at, act_factors.reshape(queries * ranks, hidden), activations)
    own = along_y(pieces)

    got, pieces[0] = lax.optimization_barrier((got, pieces[0]))
    near = ring(jnp.concatenate([packed, got]))

    at = after(idx, pieces[0])
    keep0, send0, weight = layer_z_first(at, held, down_weight, 0, 192, True, load=True)
    got0 = lax.ppermute(send0, "tensor", z_swap())
    at = after(idx, keep0)
    parts = layer_y_first(at, held, weight, 768, 256)
    wide = scatter_y(parts)
    at = after(idx, parts)
    keep1, send1 = layer_z_first(at, held, weight, 192, 320, True)
    at = after(idx, keep1)
    keep2, send2 = layer_z_first(at, held, weight, 512, 256, True)

    own, keep1, keep2 = lax.optimization_barrier((own, keep1, keep2))
    own = own + lax.ppermute(own, "tensor", z_swap())
    weights = (rank_weight * (1.0 / math.sqrt(ranks))).reshape(4, -1)
    own = own * lax.dynamic_index_in_dim(weights, y, 0, keepdims=False)[:, None]

    own, near, send1, got0 = lax.optimization_barrier((own, near, send1, got0))
    far = ring(near[gf.shape[0] // 4 : packed.shape[0]])
    got1 = lax.ppermute(send1, "tensor", z_swap())
    mine = jnp.stack(
        [own] + [lax.ppermute(own, "tensor", y_shift(-j)) for j in (1, 2, 3)]
    )
    mine, far, got1, wide = lax.optimization_barrier((mine, far, got1, wide))
    other = swap(mine)
    out0 = along_y(jnp.concatenate([keep0 + got0, keep1 + got1], axis=1))
    out0 = out0.astype(jnp.bfloat16)
    got2 = lax.ppermute(send2, "tensor", z_swap())

    share = scores(idx, output_grads, gf, near, far, mine, other, ranks)
    raw = lax.dynamic_slice_in_dim(share, core * queries, queries, 0)
    raw = raw + swap(lax.dynamic_slice_in_dim(share, (1 - core) * queries, queries, 0))
    raw = along_y([raw] * 4)
    raw, got2, out0 = lax.optimization_barrier((raw, got2, out0))
    half = keep0.shape[2]
    send = lax.dynamic_slice_in_dim(wide, (1 - z) * half, half, 1)
    keep = lax.dynamic_slice_in_dim(wide, z * half, half, 1)
    out2 = (keep + lax.ppermute(send, "tensor", z_swap())).astype(jnp.bfloat16)
    out1 = along_y(keep2 + got2).astype(jnp.bfloat16)
    raw = raw + lax.ppermute(raw, "tensor", z_swap())

    square = jnp.sum((raw * raw).reshape(queries, -1, 128), axis=1)
    got = [lax.ppermute(square, "dp", dp_shift(j)) for j in (1, 3, 2)]
    square = (square + got[2]) + (got[0] + got[1])
    square, out1 = lax.optimization_barrier((square, out1))
    spread = jnp.sum(square, axis=1, keepdims=True) / (tokens * lax.axis_size("dp"))
    influence = raw / jnp.sqrt(spread + 1e-06)
    return (jnp.concatenate([out0, out1, out2], axis=0), influence.T)


def solution(mesh):
    return jax.shard_map(
        body,
        mesh=mesh,
        in_specs=(
            P("dp", "tensor"),
            P("tensor", "pipe"),
            P("dp", ("pipe", "tensor")),
            P("pipe", None, "tensor"),
            P(None, None, ("pipe", "tensor")),
            P("pipe", None),
        ),
        out_specs=(P("dp", ("pipe", "tensor")), P("dp", "pipe")),
        check_vma=False,
    )
```

time: 824 us -> 144 us (0.17)
  waiting for transfers between devices: 766 us -> 39.5 us
  starting transfers between devices: 0.12 us -> 38.8 us
  Pallas kernels: 0 us -> 31.2 us
  matrix products: 24.1 us -> 0 us
  blocking collectives: 13.4 us -> 0 us
  local copies, waits for them, and re-layouts: 1.45 us -> 12.7 us
    psum x2 -> x0, waiting for transfers between devices: 663 us -> none  [the longest x1 593 us: body(): summed_all = lax.psum(grad_flat, ('pipe', 'tensor'))]
    reduce_scatter x1, waiting for transfers between devices: 103 us -> 0.02 us  [scatter_y(): lax.psum_scatter(parts, 'tensor', scatter_dimension=0, axis_index_groups=...]
    ppermute x0 -> x29, waiting for transfers between devices: none -> 39.5 us  [the longest x12 15.3 us: along_y(): got = [lax.ppermute(parts[j], 'tensor', y_shift(j)) for j in shifts]]
    ppermute x0 -> x29, starting transfers between devices: none -> 38.8 us  [the longest x12 19.8 us: along_y(): got = [lax.ppermute(parts[j], 'tensor', y_shift(j)) for j in shifts]]
    pallas_call x0 -> x7, Pallas kernels: none -> 31.2 us  [the longest x3 13.3 us: layer_z_first(): pl.pallas_call(functools.partial(layer_z_kernel, first=first, relative=re...]
    dot_general x3 -> x0, matrix products: 24.1 us -> none  [the longest x1 13.5 us: body(): jnp.dot(activations, down_weight, preferred_element_type=jnp.float32)]
    psum x1 -> x0, blocking collectives: 13.4 us -> none  [body(): square_sum = lax.psum(jnp.sum(raw_scores * raw_scores, axis=0), 'dp')]
    unnamed x8 -> x24, local copies, waits for them, and re-layouts: 1.45 us -> 11.6 us
  transfers between devices with their start and end apart: 3 -> 30, of which waited for: 3 -> 11; matrix products, arithmetic and copies ran while one was open for 2% -> 3% of each run, Pallas kernels for 0% -> 21%
where the time goes in v3:
time: 144 us
  waiting for transfers between devices  39.5 us (27%)
  starting transfers between devices  38.8 us (27%)
  Pallas kernels  31.2 us (22%)
  between operations  14.4 us (10%)
  local copies, waits for them, and re-layouts  12.7 us (9%)
  other arithmetic  7.05 us (5%)
    ppermute x12, starting transfers between devices, along_y(): got = [lax.ppermute(parts[j], 'tensor', y_shift(j)) for j in shifts]  19.8 us
    ppermute x12, waiting for transfers between devices, along_y(): got = [lax.ppermute(parts[j], 'tensor', y_shift(j)) for j in shifts]  15.3 us
    pallas_call x3, Pallas kernels, layer_z_first(): pl.pallas_call(functools.partial(layer_z_kernel, first=first, relative=re...  13.3 us
    ppermute x3, waiting for transfers between devices, body(): lax.ppermute(own, 'tensor', y_shift(-j))  12.4 us
    unnamed x24, local copies, waits for them, and re-layouts  11.6 us
    ppermute x3, starting transfers between devices, body(): got = [lax.ppermute(square, 'dp', dp_shift(j)) for j in (1, 3, 2)]  9.11 us
    pallas_call x1, Pallas kernels, act_pieces(): pl.pallas_call(act_kernel, grid_spec=pltpu.PrefetchScalarGridSpec(num_sca...  8.03 us
    ppermute x1, waiting for transfers between devices, body(): own = own + lax.ppermute(own, 'tensor', z_swap())  6.86 us
  transfers between devices with their start and end apart: 30, of which 11 were waited for; matrix products, arithmetic and copies ran while one was open for 3% of the time, Pallas kernels for 21%

profile of v3, /device:TPU:2, one launch (start us, length us, event | category | flops | bytes accessed | tf_op | source)
XLA Modules:
  0.0 143.7 jit_solution(3999974100395513486)
XLA Ops:
  7.3 1.7 %pack.1 = (f32[2048,128]{1,0:T(8,128)S(1)}, f32[1536,128]{1,0:T(8,128)S(1)}) custom-call(s32[4]{0:T(128)S(1)} %pad_add_fusion.idx, bf16[1024,128]{1,0:T(8,128)(2,1)} %og.1, bf16[2048,128]{1,0:T(8,128)(2,1)} %bitcast.45), custom_call_target="tpu_custom_call" | custom-call | tf_op jit(solution)/shard_map/pack/pallas_call | solution.py:83
  9.2 8.0 %act.1 = (f32[64,1024]{1,0:T(8,128)S(1)}, f32[64,1024]{1,0:T(8,128)}, f32[64,1024]{1,0:T(8,128)}, f32[64,1024]{1,0:T(8,128)S(1)}, bf16[1024,3584]{1,0:T(8,128)(2,1)S(1)}) custom-call(s32[4]{0:T(128)S(1)} %pad_add_fusion.idx, bf16[256,3584]{1,0:T(8,128)(2,1)} %bitcast.47, bf16[1024,3584]{1,0:T(8,128)(2,1)} %a_hbm.1), custom_call_target="tpu_custom_call" | custom-call | tf_op jit(solution)/shard_map/act/pallas_call | solution.py:134
  17.2 1.5 %pad_maximum_fusion = f32[3584,128]{1,0:T(8,128)} fusion(f32[1536,128]{1,0:T(8,128)S(1)} %collective-permute-done.4, f32[2048,128]{1,0:T(8,128)S(1)} %get-tuple-element.37), kind=kLoop, calls=%fused_computation | loop fusion | flops 458752 | bytes 3670016 | tf_op jit(solution)/shard_map/concatenate | solution.py:310
  18.7 1.5 %collective-permute-start.5 = (f32[3584,128]{1,0:T(8,128)}, f32[3584,128]{1,0:T(8,128)S(1)}, u32[]{:S(2)}, u32[]{:S(2)}) collective-permute-start(f32[3584,128]{1,0:T(8,128)} %pad_maximum_fusion), channel_id=1, source_target_pairs={{0,16},{8,56},{16,32},{24,8},{32,48},{40,24},{48,0},{56,40},{1,17}... | collective-permute-start | bytes 5505032 | tf_op jit(solution)/shard_map/ppermute | solution.py:310
  20.2 5.5 %layer_z.3 = (f32[4,192,128]{2,1,0:T(8,128)S(1)}, f32[4,192,128]{2,1,0:T(8,128)S(1)}, bf16[3584,1024]{1,0:T(8,128)(2,1)S(1)}) custom-call(s32[4]{0:T(128)S(1)} %pad_add_fusion.idx, bf16[1024,3584]{1,0:T(8,128)(2,1)S(1)} %get-tuple-element.43.a, bf16[3584,1024]{1,0:T(8,128)(2,1)} %w_in.1), custom_call_target="tpu_custom_call" | custom-call | tf_op jit(solution)/shard_map/layer_z/pallas_call | solution.py:189
  25.7 0.7 copy-done.8
  26.5 4.3 %layer_y.1 = f32[4,256,256]{2,1,0:T(8,128)} custom-call(s32[4]{0:T(128)S(1)} %pad_add_fusion.idx, bf16[1024,3584]{1,0:T(8,128)(2,1)S(1)} %get-tuple-element.43.a, bf16[3584,1024]{1,0:T(8,128)(2,1)S(1)} %get-tuple-element.46.w.w_in), custom_call_target="tpu_custom_call" | custom-call | tf_op jit(solution)/shard_map/layer_y/pallas_call | solution.py:217
  30.7 3.0 %copy-done.2 = bf16[3584,1024]{1,0:T(8,128)(2,1)} copy-done((bf16[3584,1024]{1,0:T(8,128)(2,1)}, bf16[3584,1024]{1,0:T(8,128)(2,1)S(1)}, u32[]{:S(2)}) %copy-start.2) | copy-done | bytes 7340056
  33.8 3.3 %collective-permute-start = (f32[64,1024]{1,0:T(8,128)}, f32[64,1024]{1,0:T(8,128)S(1)}, u32[]{:S(2)}, u32[]{:S(2)}) collective-permute-start(f32[64,1024]{1,0:T(8,128)} %get-tuple-element.40), channel_id=1, source_target_pairs={{0,4},{1,5},{2,6},{3,7},{4,0},{5,1},{6,2},{7,3},{8,12},{9,13},{10,... | collective-permute-start | bytes 786440 | tf_op jit(solution)/shard_map/ppermute | solution.py:284
  37.0 0.7 collective-permute-start.1
  37.7 2.6 %collective-permute-start.2 = (f32[64,1024]{1,0:T(8,128)S(1)}, f32[64,1024]{1,0:T(8,128)S(1)}, u32[]{:S(2)}, u32[]{:S(2)}) collective-permute-start(f32[64,1024]{1,0:T(8,128)S(1)} %get-tuple-element.42), channel_id=1, source_target_pairs={{0,6},{1,7},{2,0},{3,1},{4,2},{5,3},{6,4},{7,5},{8,14},{9,15},{10,... | collective-permute-start | bytes 786440 | tf_op jit(solution)/shard_map/ppermute | solution.py:284
  40.3 1.9 %collective-permute-start.6 = (f32[4,192,128]{2,1,0:T(8,128)S(1)}, f32[4,192,128]{2,1,0:T(8,128)}, u32[]{:S(2)}, u32[]{:S(2)}) collective-permute-start(f32[4,192,128]{2,1,0:T(8,128)S(1)} %get-tuple-element.55), channel_id=1, source_target_pairs={{0,1},{1,0},{2,3},{3,2},{4,5},{5,4},{6,7},{7,6},{8,9},{9,8},{10,11... | collective-permute-start | bytes 1179656 | tf_op jit(solution)/shard_map/ppermute | solution.py:314
  42.2 3.1 %copy-done.1 = bf16[1024,3584]{1,0:T(8,128)(2,1)S(1)} copy-done((bf16[1024,3584]{1,0:T(8,128)(2,1)S(1)}, bf16[1024,3584]{1,0:T(8,128)(2,1)}, u32[]{:S(2)}) %copy-start.1) | copy-done | bytes 7340056
  45.3 3.2 %copy-done.3 = bf16[3584,1024]{1,0:T(8,128)(2,1)S(1)} copy-done((bf16[3584,1024]{1,0:T(8,128)(2,1)S(1)}, bf16[3584,1024]{1,0:T(8,128)(2,1)}, u32[]{:S(2)}) %copy-start.3) | copy-done | bytes 7340056
  48.5 4.6 %layer_z.4 = (f32[4,320,128]{2,1,0:T(8,128)S(1)}, f32[4,320,128]{2,1,0:T(8,128)}) custom-call(s32[4]{0:T(128)S(1)} %pad_add_fusion.idx, bf16[1024,3584]{1,0:T(8,128)(2,1)S(1)} %copy-done.1, bf16[3584,1024]{1,0:T(8,128)(2,1)S(1)} %copy-done.3), custom_call_target="tpu_custom_call" | custom-call | tf_op jit(solution)/shard_map/layer_z/pallas_call | solution.py:189
  53.1 3.3 %layer_z.5 = (f32[4,256,128]{2,1,0:T(8,128)S(1)}, f32[4,256,128]{2,1,0:T(8,128)S(1)}) custom-call(s32[4]{0:T(128)S(1)} %pad_add_fusion.idx, bf16[1024,3584]{1,0:T(8,128)(2,1)S(1)} %copy-done.1, bf16[3584,1024]{1,0:T(8,128)(2,1)S(1)} %copy-done.3), custom_call_target="tpu_custom_call" | custom-call | tf_op jit(solution)/shard_map/layer_z/pallas_call | solution.py:189
  56.3 0.8 copy-done.6
  57.2 0.7 copy-done.9
  58.0 6.9 %collective-permute-done.3 = f32[64,1024]{1,0:T(8,128)S(1)} collective-permute-done((f32[64,1024]{1,0:T(8,128)S(1)}, f32[64,1024]{1,0:T(8,128)S(1)}, u32[]{:S(2)}, u32[]{:S(2)}) %collective-permute-start.3) | collective-permute-done | bytes 262176 | tf_op jit(solution)/shard_map/ppermute | solution.py:324
  65.0 1.0 slice.27
  66.0 1.5 %collective-permute-start.10 = (f32[1536,128]{1,0:T(8,128)}, f32[1536,128]{1,0:T(8,128)}, u32[]{:S(2)}, u32[]{:S(2)}) collective-permute-start(f32[1536,128]{1,0:T(8,128)} %slice.27), channel_id=1, source_target_pairs={{0,16},{8,56},{16,32},{24,8},{32,48},{40,24},{48,0},{56,40},{1,17}... | collective-permute-start | bytes 2359304 | tf_op jit(solution)/shard_map/ppermute | solution.py:329
  67.7 1.7 %collective-permute-start.8 = (f32[64,1024]{1,0:T(8,128)S(1)}, f32[64,1024]{1,0:T(8,128)S(1)}, u32[]{:S(2)}, u32[]{:S(2)}) collective-permute-start(f32[64,1024]{1,0:T(8,128)S(1)} %add_multiply_fusion), channel_id=1, source_target_pairs={{0,4},{1,5},{2,6},{3,7},{4,0},{5,1},{6,2},{7,3},{8,12},{9,13},{10,... | collective-permute-start | bytes 786440 | tf_op jit(solution)/shard_map/ppermute | solution.py:332
  69.5 1.5 %collective-permute-start.7 = (f32[64,1024]{1,0:T(8,128)S(1)}, f32[64,1024]{1,0:T(8,128)S(1)}, u32[]{:S(2)}, u32[]{:S(2)}) collective-permute-start(f32[64,1024]{1,0:T(8,128)S(1)} %add_multiply_fusion), channel_id=1, source_target_pairs={{0,6},{1,7},{2,0},{3,1},{4,2},{5,3},{6,4},{7,5},{8,14},{9,15},{10,... | collective-permute-start | bytes 786440 | tf_op jit(solution)/shard_map/ppermute | solution.py:332
  71.0 11.8 %collective-permute-done.9 = f32[64,1024]{1,0:T(8,128)S(1)} collective-permute-done((f32[64,1024]{1,0:T(8,128)S(1)}, f32[64,1024]{1,0:T(8,128)S(1)}, u32[]{:S(2)}, u32[]{:S(2)}) %collective-permute-start.9) | collective-permute-done | bytes 262176 | tf_op jit(solution)/shard_map/ppermute | solution.py:332
  82.8 0.6 collective-permute-done.7
  83.5 1.1 collective-permute-done.11
  84.6 0.8 collective-permute-start.17
  85.3 1.2 add.114
  86.5 1.2 add.115
  87.8 2.4 %collective-permute-start.20 = (f32[512,128]{1,0:T(8,128)S(1)}, f32[512,128]{1,0:T(8,128)S(1)}, u32[]{:S(2)}, u32[]{:S(2)}) collective-permute-start(f32[512,128]{1,0:T(8,128)S(1)} %get-tuple-element.74), channel_id=1, source_target_pairs={{0,6},{1,7},{2,0},{3,1},{4,2},{5,3},{6,4},{7,5},{8,14},{9,15},{10,... | collective-permute-start | bytes 786440 | tf_op jit(solution)/shard_map/ppermute | solution.py:284
  90.2 1.0 collective-permute-start.19
  91.2 3.9 %scores.1 = f32[16,1024]{1,0:T(8,128)S(1)} custom-call(s32[4]{0:T(128)S(1)} %pad_add_fusion.idx, bf16[1024,128]{1,0:T(8,128)(2,1)S(1)} %copy-done.5, bf16[2048,128]{1,0:T(8,128)(2,1)S(1)} %bitcast.46, f32[3584,128]{1,0:T(8,128)S(1)} %collective-permute-done.5.a1.b1.a2.b2, f32[3584,128]{1,0:T(8,128)S(1)} %collective-permute-done.5.a1.b1.a2.b2, ...), custom_call_target="tpu_custom_call" | custom-call | tf_op jit(solution)/shard_map/scores/pallas_call | solution.py:268
  95.2 1.2 collective-permute-done.13
  96.4 0.4 collective-permute-start.28
  96.8 5.3 %collective-permute-done.20 = f32[512,128]{1,0:T(8,128)S(1)} collective-permute-done((f32[512,128]{1,0:T(8,128)S(1)}, f32[512,128]{1,0:T(8,128)S(1)}, u32[]{:S(2)}, u32[]{:S(2)}) %collective-permute-start.20) | collective-permute-done | bytes 262176 | tf_op jit(solution)/shard_map/ppermute | solution.py:284
  102.1 3.7 %collective-permute-start.16 = (f32[8,1024]{1,0:T(8,128)S(1)}, f32[8,1024]{1,0:T(8,128)S(1)}, u32[]{:S(2)}, u32[]{:S(2)}) collective-permute-start(f32[8,1024]{1,0:T(8,128)S(1)} %dynamic-slice_add_fusion), channel_id=1, source_target_pairs={{0,6},{1,7},{2,0},{3,1},{4,2},{5,3},{6,4},{7,5},{8,14},{9,15},{10,... | collective-permute-start | bytes 98312 | tf_op jit(solution)/shard_map/ppermute | solution.py:284
  105.8 1.5 %collective-permute-start.14 = (f32[8,1024]{1,0:T(8,128)S(1)}, f32[8,1024]{1,0:T(8,128)S(1)}, u32[]{:S(2)}, u32[]{:S(2)}) collective-permute-start(f32[8,1024]{1,0:T(8,128)S(1)} %dynamic-slice_add_fusion), channel_id=1, source_target_pairs={{0,4},{1,5},{2,6},{3,7},{4,0},{5,1},{6,2},{7,3},{8,12},{9,13},{10,... | collective-permute-start | bytes 98312 | tf_op jit(solution)/shard_map/ppermute | solution.py:284
  107.4 3.5 %collective-permute-done.15 = f32[8,1024]{1,0:T(8,128)S(1)} collective-permute-done((f32[8,1024]{1,0:T(8,128)S(1)}, f32[8,1024]{1,0:T(8,128)S(1)}, u32[]{:S(2)}, u32[]{:S(2)}) %collective-permute-start.15) | collective-permute-done | bytes 32800 | tf_op jit(solution)/shard_map/ppermute | solution.py:284
  111.5 1.1 add.123
  112.6 2.7 %collective-permute-done.21 = f32[8,1024]{1,0:T(8,128)S(1)} collective-permute-done((f32[8,1024]{1,0:T(8,128)S(1)}, f32[8,1024]{1,0:T(8,128)S(1)}, u32[]{:S(2)}, u32[]{:S(2)}) %collective-permute-start.21) | collective-permute-done | bytes 32800 | tf_op jit(solution)/shard_map/ppermute | solution.py:350
  115.3 5.3 %collective-permute-start.24 = (f32[8,128]{1,0:T(8,128)S(1)}, f32[8,128]{1,0:T(8,128)S(1)}, u32[]{:S(2)}, u32[]{:S(2)}) collective-permute-start(f32[8,128]{1,0:T(8,128)S(1)} %get-tuple-element.72), channel_id=1, source_target_pairs={{0,192},{64,0},{128,64},{192,128},{1,193},{65,1},{129,65},{193,129... | collective-permute-start | bytes 12296 | tf_op jit(solution)/shard_map/ppermute | solution.py:353
  120.6 3.8 %collective-permute-start.22 = (f32[8,128]{1,0:T(8,128)S(1)}, f32[8,128]{1,0:T(8,128)S(1)}, u32[]{:S(2)}, u32[]{:S(2)}) collective-permute-start(f32[8,128]{1,0:T(8,128)S(1)} %get-tuple-element.72), channel_id=1, source_target_pairs={{0,128},{64,192},{128,0},{192,64},{1,129},{65,193},{129,1},{193,65... | collective-permute-start | bytes 12296 | tf_op jit(solution)/shard_map/ppermute | solution.py:353
  124.5 3.2 %collective-permute-start.27 = (f32[256,128]{1,0:T(8,128)S(1)}, f32[256,128]{1,0:T(8,128)S(1)}, u32[]{:S(2)}, u32[]{:S(2)}) collective-permute-start(f32[256,128]{1,0:T(8,128)S(1)} %get-tuple-element.77), channel_id=1, source_target_pairs={{0,6},{1,7},{2,0},{3,1},{4,2},{5,3},{6,4},{7,5},{8,14},{9,15},{10,... | collective-permute-start | bytes 393224 | tf_op jit(solution)/shard_map/ppermute | solution.py:284
  127.7 1.6 %collective-permute-start.25 = (f32[256,128]{1,0:T(8,128)S(1)}, f32[256,128]{1,0:T(8,128)S(1)}, u32[]{:S(2)}, u32[]{:S(2)}) collective-permute-start(f32[256,128]{1,0:T(8,128)S(1)} %get-tuple-element.79), channel_id=1, source_target_pairs={{0,4},{1,5},{2,6},{3,7},{4,0},{5,1},{6,2},{7,3},{8,12},{9,13},{10,... | collective-permute-start | bytes 393224 | tf_op jit(solution)/shard_map/ppermute | solution.py:284
  129.3 0.9 collective-permute-done.27
  130.2 5.1 %collective-permute-done.26 = f32[256,128]{1,0:T(8,128)S(1)} collective-permute-done((f32[256,128]{1,0:T(8,128)S(1)}, f32[256,128]{1,0:T(8,128)S(1)}, u32[]{:S(2)}, u32[]{:S(2)}) %collective-permute-start.26) | collective-permute-done | bytes 131104 | tf_op jit(solution)/shard_map/ppermute | solution.py:284
  135.4 0.7 divide_bitcast_fusion
  136.1 0.7 pad_maximum_fusion.3
  (71 shorter events, 2.0 us)
Async XLA Ops:
  7.2 76.3 %reduce-scatter.2.cloned.1.call-start = ((), (), s32[]{:S(2)}) async-start(), calls=%async_computation.1 | async-start | bytes 1310720 | tf_op jit(solution)/shard_map/reduce_scatter | solution.py:290
  9.1 8.1 %collective-permute-start.4 = (f32[1536,128]{1,0:T(8,128)S(1)}, f32[1536,128]{1,0:T(8,128)S(1)}, u32[]{:S(2)}, u32[]{:S(2)}) collective-permute-start(f32[1536,128]{1,0:T(8,128)S(1)} %get-tuple-element.52), channel_id=1, source_target_pairs={{0,8},{8,0},{16,24},{24,16},{32,40},{40,32},{48,56},{56,48},{1,9},... | collective-permute-start | bytes 2359304 | tf_op jit(solution)/shard_map/ppermute | solution.py:304
  17.2 9.3 %copy-start = (bf16[1024,3584]{1,0:T(8,128)(2,1)}, bf16[1024,3584]{1,0:T(8,128)(2,1)S(1)}, u32[]{:S(2)}) copy-start(bf16[1024,3584]{1,0:T(8,128)(2,1)S(1)} %get-tuple-element.43.a) | copy-start | bytes 22020100
  18.7 46.3 %collective-permute-start.5 = (f32[3584,128]{1,0:T(8,128)}, f32[3584,128]{1,0:T(8,128)S(1)}, u32[]{:S(2)}, u32[]{:S(2)}) collective-permute-start(f32[3584,128]{1,0:T(8,128)} %pad_maximum_fusion), channel_id=1, source_target_pairs={{0,16},{8,56},{16,32},{24,8},{32,48},{40,24},{48,0},{56,40},{1,17}... | collective-permute-start | bytes 5505032 | tf_op jit(solution)/shard_map/ppermute | solution.py:310
  25.7 0.7 copy-start.8
  30.7 3.0 %copy-start.2 = (bf16[3584,1024]{1,0:T(8,128)(2,1)}, bf16[3584,1024]{1,0:T(8,128)(2,1)S(1)}, u32[]{:S(2)}) copy-start(bf16[3584,1024]{1,0:T(8,128)(2,1)S(1)} %get-tuple-element.46.w.w_in) | copy-start | bytes 22020100
  33.8 23.4 %collective-permute-start = (f32[64,1024]{1,0:T(8,128)}, f32[64,1024]{1,0:T(8,128)S(1)}, u32[]{:S(2)}, u32[]{:S(2)}) collective-permute-start(f32[64,1024]{1,0:T(8,128)} %get-tuple-element.40), channel_id=1, source_target_pairs={{0,4},{1,5},{2,6},{3,7},{4,0},{5,1},{6,2},{7,3},{8,12},{9,13},{10,... | collective-permute-start | bytes 786440 | tf_op jit(solution)/shard_map/ppermute | solution.py:284
  37.0 20.1 %collective-permute-start.1 = (f32[64,1024]{1,0:T(8,128)}, f32[64,1024]{1,0:T(8,128)S(1)}, u32[]{:S(2)}, u32[]{:S(2)}) collective-permute-start(f32[64,1024]{1,0:T(8,128)} %get-tuple-element.41), channel_id=1, source_target_pairs={{0,2},{1,3},{2,4},{3,5},{4,6},{5,7},{6,0},{7,1},{8,10},{9,11},{10,... | collective-permute-start | bytes 786440 | tf_op jit(solution)/shard_map/ppermute | solution.py:284
  37.7 19.4 %collective-permute-start.2 = (f32[64,1024]{1,0:T(8,128)S(1)}, f32[64,1024]{1,0:T(8,128)S(1)}, u32[]{:S(2)}, u32[]{:S(2)}) collective-permute-start(f32[64,1024]{1,0:T(8,128)S(1)} %get-tuple-element.42), channel_id=1, source_target_pairs={{0,6},{1,7},{2,0},{3,1},{4,2},{5,3},{6,4},{7,5},{8,14},{9,15},{10,... | collective-permute-start | bytes 786440 | tf_op jit(solution)/shard_map/ppermute | solution.py:284
  40.3 24.7 %collective-permute-start.6 = (f32[4,192,128]{2,1,0:T(8,128)S(1)}, f32[4,192,128]{2,1,0:T(8,128)}, u32[]{:S(2)}, u32[]{:S(2)}) collective-permute-start(f32[4,192,128]{2,1,0:T(8,128)S(1)} %get-tuple-element.55), channel_id=1, source_target_pairs={{0,1},{1,0},{2,3},{3,2},{4,5},{5,4},{6,7},{7,6},{8,9},{9,8},{10,11... | collective-permute-start | bytes 1179656 | tf_op jit(solution)/shard_map/ppermute | solution.py:314
  42.2 3.1 %copy-start.1 = (bf16[1024,3584]{1,0:T(8,128)(2,1)S(1)}, bf16[1024,3584]{1,0:T(8,128)(2,1)}, u32[]{:S(2)}) copy-start(bf16[1024,3584]{1,0:T(8,128)(2,1)} %copy-done) | copy-start | bytes 22020100
  45.3 3.2 %copy-start.3 = (bf16[3584,1024]{1,0:T(8,128)(2,1)S(1)}, bf16[3584,1024]{1,0:T(8,128)(2,1)}, u32[]{:S(2)}) copy-start(bf16[3584,1024]{1,0:T(8,128)(2,1)} %copy-done.2) | copy-start | bytes 22020100
  53.1 4.9 %copy-start.11 = (f32[8,32]{1,0:T(8,128)S(1)}, f32[8,32]{1,0:T(8,128)}, u32[]{:S(2)}) copy-start(f32[8,32]{1,0:T(8,128)} %param.11) | copy-start | bytes 3076
  56.3 0.8 copy-start.6
  57.1 0.8 copy-start.9
  57.9 7.0 %collective-permute-start.3 = (f32[64,1024]{1,0:T(8,128)S(1)}, f32[64,1024]{1,0:T(8,128)S(1)}, u32[]{:S(2)}, u32[]{:S(2)}) collective-permute-start(f32[64,1024]{1,0:T(8,128)S(1)} %add_add_fusion), channel_id=1, source_target_pairs={{0,1},{1,0},{2,3},{3,2},{4,5},{5,4},{6,7},{7,6},{8,9},{9,8},{10,11... | collective-permute-start | bytes 786440 | tf_op jit(solution)/shard_map/ppermute | solution.py:324
  66.0 18.6 %collective-permute-start.10 = (f32[1536,128]{1,0:T(8,128)}, f32[1536,128]{1,0:T(8,128)}, u32[]{:S(2)}, u32[]{:S(2)}) collective-permute-start(f32[1536,128]{1,0:T(8,128)} %slice.27), channel_id=1, source_target_pairs={{0,16},{8,56},{16,32},{24,8},{32,48},{40,24},{48,0},{56,40},{1,17}... | collective-permute-start | bytes 2359304 | tf_op jit(solution)/shard_map/ppermute | solution.py:329
  67.5 17.1 %collective-permute-start.11 = (f32[4,320,128]{2,1,0:T(8,128)}, f32[4,320,128]{2,1,0:T(8,128)}, u32[]{:S(2)}, u32[]{:S(2)}) collective-permute-start(f32[4,320,128]{2,1,0:T(8,128)} %get-tuple-element.58), channel_id=1, source_target_pairs={{0,1},{1,0},{2,3},{3,2},{4,5},{5,4},{6,7},{7,6},{8,9},{9,8},{10,11... | collective-permute-start | bytes 1966088 | tf_op jit(solution)/shard_map/ppermute | solution.py:330
  67.7 15.0 %collective-permute-start.9 = (f32[64,1024]{1,0:T(8,128)S(1)}, f32[64,1024]{1,0:T(8,128)S(1)}, u32[]{:S(2)}, u32[]{:S(2)}) collective-permute-start(f32[64,1024]{1,0:T(8,128)S(1)} %add_multiply_fusion), channel_id=1, source_target_pairs={{0,2},{1,3},{2,4},{3,5},{4,6},{5,7},{6,0},{7,1},{8,10},{9,11},{10,... | collective-permute-start | bytes 786440 | tf_op jit(solution)/shard_map/ppermute | solution.py:332
  67.7 15.0 %collective-permute-start.8 = (f32[64,1024]{1,0:T(8,128)S(1)}, f32[64,1024]{1,0:T(8,128)S(1)}, u32[]{:S(2)}, u32[]{:S(2)}) collective-permute-start(f32[64,1024]{1,0:T(8,128)S(1)} %add_multiply_fusion), channel_id=1, source_target_pairs={{0,4},{1,5},{2,6},{3,7},{4,0},{5,1},{6,2},{7,3},{8,12},{9,13},{10,... | collective-permute-start | bytes 786440 | tf_op jit(solution)/shard_map/ppermute | solution.py:332
  69.5 13.9 %collective-permute-start.7 = (f32[64,1024]{1,0:T(8,128)S(1)}, f32[64,1024]{1,0:T(8,128)S(1)}, u32[]{:S(2)}, u32[]{:S(2)}) collective-permute-start(f32[64,1024]{1,0:T(8,128)S(1)} %add_multiply_fusion), channel_id=1, source_target_pairs={{0,6},{1,7},{2,0},{3,1},{4,2},{5,3},{6,4},{7,5},{8,14},{9,15},{10,... | collective-permute-start | bytes 786440 | tf_op jit(solution)/shard_map/ppermute | solution.py:332
  84.6 6.6 %collective-permute-start.12 = (f32[4,64,1024]{2,1,0:T(8,128)S(1)}, f32[4,64,1024]{2,1,0:T(8,128)}, u32[]{:S(2)}, u32[]{:S(2)}) collective-permute-start(f32[4,64,1024]{2,1,0:T(8,128)S(1)} %pad_maximum_fusion.1.mine), channel_id=1, source_target_pairs={{0,8},{8,0},{16,24},{24,16},{32,40},{40,32},{48,56},{56,48},{1,9},... | collective-permute-start | bytes 3145736 | tf_op jit(solution)/shard_map/ppermute | solution.py:335
  84.6 26.7 %collective-permute-start.17 = (f32[4,256,128]{2,1,0:T(8,128)}, f32[4,256,128]{2,1,0:T(8,128)}, u32[]{:S(2)}, u32[]{:S(2)}) collective-permute-start(f32[4,256,128]{2,1,0:T(8,128)} %copy-done.9), channel_id=1, source_target_pairs={{0,1},{1,0},{2,3},{3,2},{4,5},{5,4},{6,7},{7,6},{8,9},{9,8},{10,11... | collective-permute-start | bytes 1572872 | tf_op jit(solution)/shard_map/ppermute | solution.py:338
  86.5 4.7 %copy-start.4 = (bf16[64,32,128]{2,1,0:T(8,128)(2,1)S(1)}, bf16[64,32,128]{2,1,0:T(8,128)(2,1)}, u32[]{:S(2)}) copy-start(bf16[64,32,128]{2,1,0:T(8,128)(2,1)} %param.10) | copy-start | bytes 1572868
  86.5 4.7 %copy-start.5 = (bf16[1024,128]{1,0:T(8,128)(2,1)S(1)}, bf16[1024,128]{1,0:T(8,128)(2,1)}, u32[]{:S(2)}) copy-start(bf16[1024,128]{1,0:T(8,128)(2,1)} %og.1) | copy-start | bytes 786436
  87.8 14.3 %collective-permute-start.20 = (f32[512,128]{1,0:T(8,128)S(1)}, f32[512,128]{1,0:T(8,128)S(1)}, u32[]{:S(2)}, u32[]{:S(2)}) collective-permute-start(f32[512,128]{1,0:T(8,128)S(1)} %get-tuple-element.74), channel_id=1, source_target_pairs={{0,6},{1,7},{2,0},{3,1},{4,2},{5,3},{6,4},{7,5},{8,14},{9,15},{10,... | collective-permute-start | bytes 786440 | tf_op jit(solution)/shard_map/ppermute | solution.py:284
  90.2 15.5 %collective-permute-start.18 = (f32[512,128]{1,0:T(8,128)S(1)}, f32[512,128]{1,0:T(8,128)S(1)}, u32[]{:S(2)}, u32[]{:S(2)}) collective-permute-start(f32[512,128]{1,0:T(8,128)S(1)} %get-tuple-element.75), channel_id=1, source_target_pairs={{0,4},{1,5},{2,6},{3,7},{4,0},{5,1},{6,2},{7,3},{8,12},{9,13},{10,... | collective-permute-start | bytes 786440 | tf_op jit(solution)/shard_map/ppermute | solution.py:284
  90.2 5.0 %copy-start.10 = (f32[1,256,256]{2,1,0:T(8,128)S(1)}, f32[1,256,256]{2,1,0:T(8,128)}, u32[]{:S(2)}) copy-start(f32[1,256,256]{2,1,0:T(8,128)} %reduce-scatter.2.cloned.1.call-done) | copy-start | bytes 786436
  90.2 15.5 %collective-permute-start.19 = (f32[512,128]{1,0:T(8,128)S(1)}, f32[512,128]{1,0:T(8,128)S(1)}, u32[]{:S(2)}, u32[]{:S(2)}) collective-permute-start(f32[512,128]{1,0:T(8,128)S(1)} %get-tuple-element.76), channel_id=1, source_target_pairs={{0,2},{1,3},{2,4},{3,5},{4,6},{5,7},{6,0},{7,1},{8,10},{9,11},{10,... | collective-permute-start | bytes 786440 | tf_op jit(solution)/shard_map/ppermute | solution.py:284
  95.1 16.4 %copy-start.7 = (f32[4,256,128]{2,1,0:T(8,128)S(1)}, f32[4,256,128]{2,1,0:T(8,128)}, u32[]{:S(2)}) copy-start(f32[4,256,128]{2,1,0:T(8,128)} %copy-done.6) | copy-start | bytes 1572868
  95.1 1.3 collective-permute-start.13
  96.4 15.0 %collective-permute-start.28 = (f32[256,128]{1,0:T(8,128)S(1)}, f32[256,128]{1,0:T(8,128)S(1)}, u32[]{:S(2)}, u32[]{:S(2)}) collective-permute-start(f32[256,128]{1,0:T(8,128)S(1)} %constant_dynamic-slice_fusion), channel_id=1, source_target_pairs={{0,1},{1,0},{2,3},{3,2},{4,5},{5,4},{6,7},{7,6},{8,9},{9,8},{10,11... | collective-permute-start | bytes 393224 | tf_op jit(solution)/shard_map/ppermute | solution.py:348
  102.1 5.3 %collective-permute-start.16 = (f32[8,1024]{1,0:T(8,128)S(1)}, f32[8,1024]{1,0:T(8,128)S(1)}, u32[]{:S(2)}, u32[]{:S(2)}) collective-permute-start(f32[8,1024]{1,0:T(8,128)S(1)} %dynamic-slice_add_fusion), channel_id=1, source_target_pairs={{0,6},{1,7},{2,0},{3,1},{4,2},{5,3},{6,4},{7,5},{8,14},{9,15},{10,... | collective-permute-start | bytes 98312 | tf_op jit(solution)/shard_map/ppermute | solution.py:284
  105.8 5.1 %collective-permute-start.15 = (f32[8,1024]{1,0:T(8,128)S(1)}, f32[8,1024]{1,0:T(8,128)S(1)}, u32[]{:S(2)}, u32[]{:S(2)}) collective-permute-start(f32[8,1024]{1,0:T(8,128)S(1)} %dynamic-slice_add_fusion), channel_id=1, source_target_pairs={{0,2},{1,3},{2,4},{3,5},{4,6},{5,7},{6,0},{7,1},{8,10},{9,11},{10,... | collective-permute-start | bytes 98312 | tf_op jit(solution)/shard_map/ppermute | solution.py:284
  105.8 5.5 %collective-permute-start.14 = (f32[8,1024]{1,0:T(8,128)S(1)}, f32[8,1024]{1,0:T(8,128)S(1)}, u32[]{:S(2)}, u32[]{:S(2)}) collective-permute-start(f32[8,1024]{1,0:T(8,128)S(1)} %dynamic-slice_add_fusion), channel_id=1, source_target_pairs={{0,4},{1,5},{2,6},{3,7},{4,0},{5,1},{6,2},{7,3},{8,12},{9,13},{10,... | collective-permute-start | bytes 98312 | tf_op jit(solution)/shard_map/ppermute | solution.py:284
  111.3 4.0 %collective-permute-start.21 = (f32[8,1024]{1,0:T(8,128)S(1)}, f32[8,1024]{1,0:T(8,128)S(1)}, u32[]{:S(2)}, u32[]{:S(2)}) collective-permute-start(f32[8,1024]{1,0:T(8,128)S(1)} %add_add_fusion.1), channel_id=1, source_target_pairs={{0,1},{1,0},{2,3},{3,2},{4,5},{5,4},{6,7},{7,6},{8,9},{9,8},{10,11... | collective-permute-start | bytes 98312 | tf_op jit(solution)/shard_map/ppermute | solution.py:350
  115.3 12.4 %collective-permute-start.24 = (f32[8,128]{1,0:T(8,128)S(1)}, f32[8,128]{1,0:T(8,128)S(1)}, u32[]{:S(2)}, u32[]{:S(2)}) collective-permute-start(f32[8,128]{1,0:T(8,128)S(1)} %get-tuple-element.72), channel_id=1, source_target_pairs={{0,192},{64,0},{128,64},{192,128},{1,193},{65,1},{129,65},{193,129... | collective-permute-start | bytes 12296 | tf_op jit(solution)/shard_map/ppermute | solution.py:353
  120.6 8.6 %collective-permute-start.23 = (f32[8,128]{1,0:T(8,128)S(1)}, f32[8,128]{1,0:T(8,128)S(1)}, u32[]{:S(2)}, u32[]{:S(2)}) collective-permute-start(f32[8,128]{1,0:T(8,128)S(1)} %get-tuple-element.72), channel_id=1, source_target_pairs={{0,64},{64,128},{128,192},{192,0},{1,65},{65,129},{129,193},{193,1... | collective-permute-start | bytes 12296 | tf_op jit(solution)/shard_map/ppermute | solution.py:353
  120.6 8.6 %collective-permute-start.22 = (f32[8,128]{1,0:T(8,128)S(1)}, f32[8,128]{1,0:T(8,128)S(1)}, u32[]{:S(2)}, u32[]{:S(2)}) collective-permute-start(f32[8,128]{1,0:T(8,128)S(1)} %get-tuple-element.72), channel_id=1, source_target_pairs={{0,128},{64,192},{128,0},{192,64},{1,129},{65,193},{129,1},{193,65... | collective-permute-start | bytes 12296 | tf_op jit(solution)/shard_map/ppermute | solution.py:353
  124.5 5.7 %collective-permute-start.27 = (f32[256,128]{1,0:T(8,128)S(1)}, f32[256,128]{1,0:T(8,128)S(1)}, u32[]{:S(2)}, u32[]{:S(2)}) collective-permute-start(f32[256,128]{1,0:T(8,128)S(1)} %get-tuple-element.77), channel_id=1, source_target_pairs={{0,6},{1,7},{2,0},{3,1},{4,2},{5,3},{6,4},{7,5},{8,14},{9,15},{10,... | collective-permute-start | bytes 393224 | tf_op jit(solution)/shard_map/ppermute | solution.py:284
  127.7 7.6 %collective-permute-start.26 = (f32[256,128]{1,0:T(8,128)S(1)}, f32[256,128]{1,0:T(8,128)S(1)}, u32[]{:S(2)}, u32[]{:S(2)}) collective-permute-start(f32[256,128]{1,0:T(8,128)S(1)} %get-tuple-element.78), channel_id=1, source_target_pairs={{0,2},{1,3},{2,4},{3,5},{4,6},{5,7},{6,0},{7,1},{8,10},{9,11},{10,... | collective-permute-start | bytes 393224 | tf_op jit(solution)/shard_map/ppermute | solution.py:284
  127.7 7.6 %collective-permute-start.25 = (f32[256,128]{1,0:T(8,128)S(1)}, f32[256,128]{1,0:T(8,128)S(1)}, u32[]{:S(2)}, u32[]{:S(2)}) collective-permute-start(f32[256,128]{1,0:T(8,128)S(1)} %get-tuple-element.79), channel_id=1, source_target_pairs={{0,4},{1,5},{2,6},{3,7},{4,0},{5,1},{6,2},{7,3},{8,12},{9,13},{10,... | collective-permute-start | bytes 393224 | tf_op jit(solution)/shard_map/ppermute | solution.py:284
Sparse Core Ops, SparseCore 0:
  33.9 28.4 reduce-scatter.1

commit v4 on v3

v4 whole, which is shorter than its diff:
```python
import functools
import math

import jax
import jax.numpy as jnp
from jax import lax
from jax.experimental import pallas as pl
from jax.experimental.pallas import tpu as pltpu
from jax.sharding import PartitionSpec as P

F32 = jnp.float32
MIB = 1 << 20
WHOLE = pl.BlockSpec(memory_space=pltpu.VMEM)
PACK_COST = 40 * MIB
ACT_COST = 20 * MIB


def x_ring():
    return [(p, ((p // 2 + 1 - 2 * (p % 2)) % 4) * 2 + p % 2) for p in range(8)]


def core_swap():
    return [(p, p ^ 1) for p in range(8)]


def y_shift(d):
    return [(t, ((t // 2 + d) % 4) * 2 + t % 2) for t in range(8)]


def y_pair():
    return [(t, t ^ 2) for t in range(8)]


def z_swap():
    return [(t, t ^ 1) for t in range(8)]


def dp_shift(d):
    return [(i, (i + d) % 4) for i in range(4)]


def params(limit):
    return pltpu.CompilerParams(vmem_limit_bytes=limit)


def cost(nbytes=0):
    return pl.CostEstimate(flops=0, bytes_accessed=nbytes, transcendentals=0)


def in_hbm(value):
    return pltpu.with_memory_space_constraint(value, pltpu.HBM)


def in_vmem(value):
    return pltpu.with_memory_space_constraint(value, pltpu.VMEM)


def after(value, *others):
    return lax.optimization_barrier((value, *others))[0]


def pack_kernel(idx, og_hbm, gf_hbm, *refs):
    *hbm, mine, other, a, af, weight, og, gf, sems = refs
    held = (a, af, weight)
    copies = [
        pltpu.make_async_copy(src, dst, sems.at[i])
        for i, (src, dst) in enumerate(((og_hbm, og), (gf_hbm, gf), *zip(hbm, held)))
    ]
    for copy in copies:
        copy.start()
    tokens = og.shape[0]
    rows = gf.shape[0] // 4

    def gf_rows(distance):
        start = lax.rem(idx[0] + distance, 4) * rows
        return gf[pl.ds(pl.multiple_of(start, rows), rows), :].astype(F32)

    copies[0].wait()
    wide = og[...].astype(F32)
    other[rows : rows + tokens, :] = wide
    mine[rows : rows + tokens, :] = wide
    copies[1].wait()
    other[:rows, :] = gf_rows(3 - 2 * idx[1])
    mine[:rows, :] = gf_rows(1 + 2 * idx[1])
    mine[rows + tokens :, :] = gf_rows(2)
    for copy in copies[2:]:
        copy.wait()


def pack(idx, og, gf, held):
    tokens, width = og.shape
    rows = gf.shape[0] // 4
    return pl.pallas_call(
        pack_kernel,
        grid_spec=pltpu.PrefetchScalarGridSpec(
            num_scalar_prefetch=1,
            grid=(),
            in_specs=[pl.BlockSpec(memory_space=pltpu.HBM)] * (2 + len(held)),
            out_specs=[WHOLE] * (2 + len(held)),
            scratch_shapes=[
                pltpu.VMEM(og.shape, og.dtype),
                pltpu.VMEM(gf.shape, gf.dtype),
                pltpu.SemaphoreType.DMA((2 + len(held),)),
            ],
        ),
        out_shape=[
            jax.ShapeDtypeStruct((r, width), F32) for r in (tokens + 2 * rows, tokens + rows)
        ]
        + [jax.ShapeDtypeStruct(v.shape, v.dtype) for v in held],
        compiler_params=params(4 * MIB),
        cost_estimate=cost(PACK_COST),
        name="pack",
    )(idx, *map(in_hbm, (og, gf, *held)))


def act_kernel(idx, weight, af, a, out0, out1, out2, out3, scratch, *, scale):
    rows = out0.shape[0]
    tile = scratch.shape[1]
    queries, ranks = weight.shape
    diagonal = lax.broadcasted_iota(jnp.int32, (ranks, ranks), 0) == lax.broadcasted_iota(
        jnp.int32, (ranks, ranks), 1
    )
    column = jnp.concatenate(
        [
            jnp.sum(
                jnp.where(diagonal, weight[q : q + 1, :] * scale, 0.0), axis=1, keepdims=True
            )
            for q in range(queries)
        ],
        axis=0,
    )

    @pl.loop(0, a.shape[0] // tile)
    def _(i):
        at = pl.ds(pl.multiple_of(i * tile, tile), tile)
        scratch[...] = column * lax.dot_general(
            af[...], a[at, :], (((1,), (1,)), ((), ())), preferred_element_type=F32
        )
        for j, out in enumerate((out0, out1, out2, out3)):
            start = pl.multiple_of(lax.rem(idx[2] + j, 4) * rows, rows)
            out[:, at] = scratch[pl.ds(start, rows), :]


def act_pieces(idx, weight, af, a):
    qr, tokens = af.shape[0], a.shape[0]
    return pl.pallas_call(
        functools.partial(act_kernel, scale=1.0 / math.sqrt(weight.shape[1])),
        grid_spec=pltpu.PrefetchScalarGridSpec(
            num_scalar_prefetch=1,
            grid=(),
            in_specs=[WHOLE] * 3,
            out_specs=[WHOLE] * 4,
            scratch_shapes=[pltpu.VMEM((qr, 256), F32)],
        ),
        out_shape=[jax.ShapeDtypeStruct((qr // 4, tokens), F32)] * 4,
        compiler_params=params(8 * MIB),
        cost_estimate=cost(ACT_COST),
        name="act",
    )(idx, weight, in_vmem(af), in_vmem(a))


def layer_kernel(idx, a, w, *outs, first, blocks):
    width = w.shape[1] // 4

    @pl.loop(0, 4)
    def _(j):
        owner = lax.rem(idx[2] + j, 4)
        acc = jnp.dot(
            a[first : first + sum(blocks), :],
            w[:, pl.ds(pl.multiple_of(owner * width, width), width)],
            preferred_element_type=F32,
        )
        low, high = acc[:, : width // 2], acc[:, width // 2 :]
        at_low = idx[3] == 0
        at = 0
        for rows, keep, send in zip(blocks, outs[0::2], outs[1::2]):
            keep[j] = jnp.where(at_low, low[at : at + rows], high[at : at + rows])
            send[j] = jnp.where(at_low, high[at : at + rows], low[at : at + rows])
            at += rows


def layer(idx, a, w, first, blocks):
    shapes = [
        jax.ShapeDtypeStruct((4, rows, w.shape[1] // 8), F32) for rows in blocks for _ in range(2)
    ]
    return pl.pallas_call(
        functools.partial(layer_kernel, first=first, blocks=blocks),
        grid_spec=pltpu.PrefetchScalarGridSpec(
            num_scalar_prefetch=1,
            grid=(),
            in_specs=[WHOLE] * 2,
            out_specs=[WHOLE] * len(shapes),
        ),
        out_shape=shapes,
        compiler_params=params(8 * MIB),
        cost_estimate=cost(),
        name="layer",
    )(idx, in_vmem(a), in_vmem(w))


def score_kernel(idx, og, gf, a1, b1, a2, b2, a3, b3, mine, other, keep, send, *, ranks):
    bf = jnp.bfloat16
    lhs = jnp.concatenate([gf[...]] + [b[...].astype(bf) for b in (b1, b2, b3)], axis=1)
    rhs = jnp.concatenate([og[...]] + [a[...].astype(bf) for a in (a1, a2, a3)], axis=1)
    grad = lax.dot_general(lhs, rhs, (((1,), (1,)), ((), ())), preferred_element_type=F32)
    rows = mine.shape[1]
    sums = []
    for c in range(2):
        parts = []
        for b in range(4):
            j = lax.rem(b + 4 - idx[2], 4)
            act = jnp.where(idx[1] == c, mine[j], other[j])
            at = (c * 4 + b) * rows
            product = grad[at : at + rows, :] * act
            for q in range(0, rows, ranks):
                parts.append(jnp.sum(product[q : q + ranks], axis=0, keepdims=True))
        sums.append(jnp.concatenate(parts, axis=0))
    keep[...] = jnp.where(idx[1] == 0, sums[0], sums[1])
    send[...] = jnp.where(idx[1] == 0, sums[1], sums[0])


def scores(idx, og, gf, near, far, mine, other, ranks):
    tokens, width = og.shape
    qr = gf.shape[0] // 4
    tile = 256
    assert qr % tile == 0 and tokens % qr == 0
    spec = lambda rows, at: pl.BlockSpec((rows, width), lambda i, idx: (at(i, idx), 0))
    skip = qr // tile
    in_specs = [
        spec(tile, lambda i, idx: i),
        spec(qr, lambda i, idx: idx[0]),
        spec(tile, lambda i, idx: skip + i),
        spec(qr, lambda i, idx: 0),
        spec(tile, lambda i, idx: skip + i),
        spec(qr, lambda i, idx: 0),
        spec(tile, lambda i, idx: i),
        spec(qr, lambda i, idx: tokens // qr),
    ]
    args = [in_hbm(og), in_hbm(gf), near[0], near[0], near[1], near[1], far, far]
    for act in (mine, other):
        in_specs.append(pl.BlockSpec((4, act.shape[1], tile), lambda i, idx: (0, 0, i)))
        args.append(act)
    half = qr // ranks // 2
    return pl.pallas_call(
        functools.partial(score_kernel, ranks=ranks),
        grid_spec=pltpu.PrefetchScalarGridSpec(
            num_scalar_prefetch=1,
            grid=(tokens // tile,),
            in_specs=in_specs,
            out_specs=[pl.BlockSpec((half, tile), lambda i, idx: (0, i))] * 2,
        ),
        out_shape=[jax.ShapeDtypeStruct((half, tokens), F32)] * 2,
        compiler_params=params(16 * MIB),
        cost_estimate=cost(),
        name="scores",
    )(idx, *args)


def send_y(parts):
    return [lax.ppermute(parts[j], "tensor", y_shift(j)) for j in (1, 3, 2)]


def sum_y(part, got):
    return (part + got[2]) + (got[0] + got[1])


def body(activations, down_weight, output_grads, act_factors, grad_factors, rank_weight):
    tokens = activations.shape[0]
    queries, ranks, hidden = act_factors.shape
    pipe, tensor = lax.axis_index("pipe"), lax.axis_index("tensor")
    x, core, y, z = pipe // 2, pipe % 2, tensor // 2, tensor % 2
    idx = jnp.stack([x, core, y, z]).astype(jnp.int32)
    gf = grad_factors.reshape(-1, grad_factors.shape[2])

    swap = functools.partial(lax.ppermute, axis_name="pipe", perm=core_swap())
    ring = functools.partial(lax.ppermute, axis_name="pipe", perm=x_ring())
    packed, got, activations, act_factors, rank_weight = pack(
        idx,
        output_grads,
        gf,
        (activations, act_factors.reshape(queries * ranks, hidden), rank_weight),
    )
    got = swap(got)

    near0 = ring(packed)

    at = after(idx, packed)
    pieces = list(act_pieces(at, rank_weight, act_factors, activations))
    got, pieces[0] = lax.optimization_barrier((got, pieces[0]))
    near1 = ring(got)
    own = sum_y(pieces[0], send_y(pieces))

    at = after(idx, pieces[0])
    keep0, send0 = layer(at, activations, down_weight, 0, (192,))
    send0, near0 = lax.optimization_barrier((send0, near0))
    got0 = lax.ppermute(send0, "tensor", z_swap())
    at = after(idx, keep0)
    keep1, send1, keep2, send2 = layer(at, activations, down_weight, 192, (320, 512))

    own, near0, near1, send1 = lax.optimization_barrier((own, near0, near1, send1))
    far = ring(near0[gf.shape[0] // 4 :])
    own = own + lax.ppermute(own, "tensor", z_swap())

    own, send1, got0 = lax.optimization_barrier((own, send1, got0))
    got1 = lax.ppermute(send1, "tensor", z_swap())
    mine = jnp.stack(
        [own] + [lax.ppermute(own, "tensor", y_shift(-j)) for j in (1, 2, 3)]
    )
    mine, far, got1, send2 = lax.optimization_barrier((mine, far, got1, send2))
    other = swap(mine)
    got2 = lax.ppermute(send2, "tensor", z_swap())
    keep1 = jnp.concatenate([keep0 + got0, keep1 + got1], axis=1)
    got1 = send_y(keep1)

    raw, send = scores(idx, output_grads, gf, (near0, near1), far, mine, other, ranks)
    raw = raw + swap(send)
    raw = raw + lax.ppermute(raw, "tensor", y_shift(2))
    raw, got1 = lax.optimization_barrier((raw, got1))
    raw = raw + lax.ppermute(raw, "tensor", y_pair())
    raw = raw + lax.ppermute(raw, "tensor", z_swap())

    square = jnp.sum((raw * raw).reshape(queries, -1, 128), axis=1)
    square, got2 = lax.optimization_barrier((square, got2))
    keep2 = keep2 + got2
    got2 = send_y(keep2)
    square = square + lax.ppermute(square, "dp", dp_shift(2))
    square = square + lax.ppermute(square, "dp", [(i, i ^ 1) for i in range(4)])
    spread = jnp.sum(square, axis=1, keepdims=True) / (tokens * lax.axis_size("dp"))
    influence = raw / jnp.sqrt(spread + 1e-06)
    outputs = [
        sum_y(keep[0], got).astype(jnp.bfloat16)
        for keep, got in ((keep1, got1), (keep2, got2))
    ]
    return (jnp.concatenate(outputs, axis=0), influence.T)


def solution(mesh):
    return jax.shard_map(
        body,
        mesh=mesh,
        in_specs=(
            P("dp", "tensor"),
            P("tensor", "pipe"),
            P("dp", ("pipe", "tensor")),
            P("pipe", None, "tensor"),
            P(None, None, ("pipe", "tensor")),
            P("pipe", None),
        ),
        out_specs=(P("dp", ("pipe", "tensor")), P("dp", "pipe")),
        check_vma=False,
    )
```

time: 144 us -> 115 us (0.80)
  between operations: 14.4 us -> 0.88 us
  local copies, waits for them, and re-layouts: 12.7 us -> 0.11 us
  waiting for transfers between devices: 39.5 us -> 50 us
  Pallas kernels: 31.2 us -> 21.9 us
  other arithmetic: 7.05 us -> 2.3 us
    pallas_call x5 -> x3, Pallas kernels: 25.6 us -> 13.7 us  [the longest x2 10.3 us: layer(): pl.pallas_call(functools.partial(layer_kernel, first=first, blocks=blocks...]
    unnamed x24 -> x4, local copies, waits for them, and re-layouts: 11.6 us -> 0.01 us
    ppermute x20 -> x18, waiting for transfers between devices: 16.4 us -> 22.8 us  [the longest x9 10.4 us: send_y(): return [lax.ppermute(parts[j], 'tensor', y_shift(j)) for j in (1, 3, 2)]]
    ppermute x1, waiting for transfers between devices: 6.86 us -> 12.7 us  [body(): own = own + lax.ppermute(own, 'tensor', z_swap())]
    add x7 -> x9, other arithmetic: 3.61 us -> 0.38 us  [the longest x2 0.16 us: body(): keep1 = jnp.concatenate([keep0 + got0, keep1 + got1], axis=1)]
    pallas_call x1, Pallas kernels: 1.73 us -> 4.67 us  [pack(): pl.pallas_call(pack_kernel, grid_spec=pltpu.PrefetchScalarGridSpec(num_sc...]
    ppermute x20 -> x18, starting transfers between devices: 32.5 us -> 30 us  [the longest x9 14.4 us: send_y(): return [lax.ppermute(parts[j], 'tensor', y_shift(j)) for j in (1, 3, 2)]]
    ppermute x3, waiting for transfers between devices: 12.4 us -> 10.9 us  [body(): lax.ppermute(own, 'tensor', y_shift(-j))]
  transfers between devices with their start and end apart: 30 -> 27, of which waited for: 11 -> 10; matrix products, arithmetic and copies ran while one was open for 3% -> 1% of each run, Pallas kernels for 21% -> 15%
where the time goes in v4:
time: 115 us
  waiting for transfers between devices  50 us (43%)
  starting transfers between devices  39.3 us (34%)
  Pallas kernels  21.9 us (19%)
  other arithmetic  2.3 us (2%)
    ppermute x9, starting transfers between devices, send_y(): return [lax.ppermute(parts[j], 'tensor', y_shift(j)) for j in (1, 3, 2)]  14.4 us
    ppermute x1, waiting for transfers between devices, body(): own = own + lax.ppermute(own, 'tensor', z_swap())  12.7 us
    ppermute x3, waiting for transfers between devices, body(): lax.ppermute(own, 'tensor', y_shift(-j))  10.9 us
    ppermute x9, waiting for transfers between devices, send_y(): return [lax.ppermute(parts[j], 'tensor', y_shift(j)) for j in (1, 3, 2)]  10.4 us
    pallas_call x2, Pallas kernels, layer(): pl.pallas_call(functools.partial(layer_kernel, first=first, blocks=blocks...  10.3 us
    ppermute x1, starting transfers between devices, body(): square = square + lax.ppermute(square, 'dp', dp_shift(2))  6.4 us
    ppermute x1, waiting for transfers between devices, body(): raw = raw + lax.ppermute(raw, 'tensor', y_shift(2))  5.92 us
    pallas_call x1, Pallas kernels, pack(): pl.pallas_call(pack_kernel, grid_spec=pltpu.PrefetchScalarGridSpec(num_sc...  4.67 us
  transfers between devices with their start and end apart: 27, of which 10 were waited for; matrix products, arithmetic and copies ran while one was open for 1% of the time, Pallas kernels for 15%

profile of v4, /device:TPU:2, one launch (start us, length us, event | category | flops | bytes accessed | tf_op | source)
XLA Modules:
  0.0 114.5 jit_solution(1685438346049600998)
XLA Ops:
  0.7 0.1 pad_add_fusion.idx
  0.7 4.7 %pack.1 = (f32[2048,128]{1,0:T(8,128)S(1)}, f32[1536,128]{1,0:T(8,128)S(1)}, bf16[1024,3584]{1,0:T(8,128)(2,1)S(1)}, bf16[256,3584]{1,0:T(8,128)(2,1)S(1)}, f32[8,32]{1,0:T(8,128)S(1)}) custom-call(s32[4]{0:T(128)S(1)} %pad_add_fusion.idx, bf16[1024,128]{1,0:T(8,128)(2,1)} %og.1, bf16[2048,128]{1,0:T(8,128)(2,1)} %bitcast.44, bf16[1024,3584]{1,0:T(8,128)(2,1)} %refs_0_.1, ...), custom_call_target="tpu_custom_call" | custom-call | bytes 41943040 | tf_op jit(solution)/shard_map/pack/pallas_call | solution.py:93
  5.4 0.1 collective-permute-start
  5.5 1.6 %collective-permute-start.4 = (f32[2048,128]{1,0:T(8,128)S(1)}, f32[2048,128]{1,0:T(8,128)S(1)}, u32[]{:S(2)}, u32[]{:S(2)}) collective-permute-start(f32[2048,128]{1,0:T(8,128)S(1)} %get-tuple-element.44), channel_id=1, source_target_pairs={{0,16},{8,56},{16,32},{24,8},{32,48},{40,24},{48,0},{56,40},{1,17}... | collective-permute-start | bytes 3145736 | tf_op jit(solution)/shard_map/ppermute | solution.py:285
  7.1 3.4 %act.1 = (f32[64,1024]{1,0:T(8,128)S(1)}, f32[64,1024]{1,0:T(8,128)S(1)}, f32[64,1024]{1,0:T(8,128)S(1)}, f32[64,1024]{1,0:T(8,128)S(1)}) custom-call(s32[4]{0:T(128)S(1)} %pad_add_fusion.idx, f32[8,32]{1,0:T(8,128)S(1)} %get-tuple-element.46.weight, bf16[256,3584]{1,0:T(8,128)(2,1)S(1)} %get-tuple-element.47.af, bf16[1024,3584]{1,0:T(8,128)(2,1)S(1)} %get-tuple-element.48.a), custom_call_target="tpu_custom_call" | custom-call | bytes 20971520 | tf_op jit(solution)/shard_map/act/pallas_call | solution.py:146
  10.6 1.3 %collective-permute-start.5 = (f32[1536,128]{1,0:T(8,128)S(1)}, f32[1536,128]{1,0:T(8,128)S(1)}, u32[]{:S(2)}, u32[]{:S(2)}) collective-permute-start(f32[1536,128]{1,0:T(8,128)S(1)} %collective-permute-done), channel_id=1, source_target_pairs={{0,16},{8,56},{16,32},{24,8},{32,48},{40,24},{48,0},{56,40},{1,17}... | collective-permute-start | bytes 2359304 | tf_op jit(solution)/shard_map/ppermute | solution.py:290
  11.8 3.2 %collective-permute-start.1 = (f32[64,1024]{1,0:T(8,128)S(1)}, f32[64,1024]{1,0:T(8,128)S(1)}, u32[]{:S(2)}, u32[]{:S(2)}) collective-permute-start(f32[64,1024]{1,0:T(8,128)S(1)} %get-tuple-element.53), channel_id=1, source_target_pairs={{0,4},{1,5},{2,6},{3,7},{4,0},{5,1},{6,2},{7,3},{8,12},{9,13},{10,... | collective-permute-start | bytes 786440 | tf_op jit(solution)/shard_map/ppermute | solution.py:260
  15.0 0.7 collective-permute-start.2
  15.7 2.6 %collective-permute-start.3 = (f32[64,1024]{1,0:T(8,128)S(1)}, f32[64,1024]{1,0:T(8,128)S(1)}, u32[]{:S(2)}, u32[]{:S(2)}) collective-permute-start(f32[64,1024]{1,0:T(8,128)S(1)} %get-tuple-element.55), channel_id=1, source_target_pairs={{0,6},{1,7},{2,0},{3,1},{4,2},{5,3},{6,4},{7,5},{8,14},{9,15},{10,... | collective-permute-start | bytes 786440 | tf_op jit(solution)/shard_map/ppermute | solution.py:260
  18.3 2.8 %layer.2 = (f32[4,192,128]{2,1,0:T(8,128)S(1)}, f32[4,192,128]{2,1,0:T(8,128)S(1)}) custom-call(s32[4]{0:T(128)S(1)} %pad_add_fusion.idx, bf16[1024,3584]{1,0:T(8,128)(2,1)S(1)} %get-tuple-element.48.a, bf16[3584,1024]{1,0:T(8,128)(2,1)S(1)} %bitcast.43), custom_call_target="tpu_custom_call" | custom-call | tf_op jit(solution)/shard_map/layer/pallas_call | solution.py:186
  21.1 7.5 %layer.3 = (f32[4,320,128]{2,1,0:T(8,128)S(1)}, f32[4,320,128]{2,1,0:T(8,128)S(1)}, f32[4,512,128]{2,1,0:T(8,128)S(1)}, f32[4,512,128]{2,1,0:T(8,128)S(1)}) custom-call(s32[4]{0:T(128)S(1)} %pad_add_fusion.idx, bf16[1024,3584]{1,0:T(8,128)(2,1)S(1)} %get-tuple-element.48.a, bf16[3584,1024]{1,0:T(8,128)(2,1)S(1)} %bitcast.43), custom_call_target="tpu_custom_call" | custom-call | tf_op jit(solution)/shard_map/layer/pallas_call | solution.py:186
  28.6 2.0 %collective-permute-start.7 = (f32[4,192,128]{2,1,0:T(8,128)S(1)}, f32[4,192,128]{2,1,0:T(8,128)S(1)}, u32[]{:S(2)}, u32[]{:S(2)}) collective-permute-start(f32[4,192,128]{2,1,0:T(8,128)S(1)} %get-tuple-element.63), channel_id=1, source_target_pairs={{0,1},{1,0},{2,3},{3,2},{4,5},{5,4},{6,7},{7,6},{8,9},{9,8},{10,11... | collective-permute-start | bytes 1179656 | tf_op jit(solution)/shard_map/ppermute | solution.py:296
  30.7 0.2 collective-permute-start.6
  30.9 1.5 %collective-permute-start.11 = (f32[1536,128]{1,0:T(8,128)S(1)}, f32[1536,128]{1,0:T(8,128)S(1)}, u32[]{:S(2)}, u32[]{:S(2)}) collective-permute-start(f32[1536,128]{1,0:T(8,128)S(1)} %slice.27), channel_id=1, source_target_pairs={{0,16},{8,56},{16,32},{24,8},{32,48},{40,24},{48,0},{56,40},{1,17}... | collective-permute-start | bytes 2359304 | tf_op jit(solution)/shard_map/ppermute | solution.py:301
  32.4 12.7 %collective-permute-done.6 = f32[64,1024]{1,0:T(8,128)S(1)} collective-permute-done((f32[64,1024]{1,0:T(8,128)S(1)}, f32[64,1024]{1,0:T(8,128)S(1)}, u32[]{:S(2)}, u32[]{:S(2)}) %collective-permute-start.6) | collective-permute-done | bytes 262176 | tf_op jit(solution)/shard_map/ppermute | solution.py:302
  45.1 1.8 %collective-permute-start.12 = (f32[4,320,128]{2,1,0:T(8,128)S(1)}, f32[4,320,128]{2,1,0:T(8,128)S(1)}, u32[]{:S(2)}, u32[]{:S(2)}) collective-permute-start(f32[4,320,128]{2,1,0:T(8,128)S(1)} %get-tuple-element.68), channel_id=1, source_target_pairs={{0,1},{1,0},{2,3},{3,2},{4,5},{5,4},{6,7},{7,6},{8,9},{9,8},{10,11... | collective-permute-start | bytes 1966088 | tf_op jit(solution)/shard_map/ppermute | solution.py:305
  47.0 1.8 %collective-permute-start.9 = (f32[64,1024]{1,0:T(8,128)S(1)}, f32[64,1024]{1,0:T(8,128)S(1)}, u32[]{:S(2)}, u32[]{:S(2)}) collective-permute-start(f32[64,1024]{1,0:T(8,128)S(1)} %add.79), channel_id=1, source_target_pairs={{0,4},{1,5},{2,6},{3,7},{4,0},{5,1},{6,2},{7,3},{8,12},{9,13},{10,... | collective-permute-start | bytes 786440 | tf_op jit(solution)/shard_map/ppermute | solution.py:307
  48.7 1.5 %collective-permute-start.8 = (f32[64,1024]{1,0:T(8,128)S(1)}, f32[64,1024]{1,0:T(8,128)S(1)}, u32[]{:S(2)}, u32[]{:S(2)}) collective-permute-start(f32[64,1024]{1,0:T(8,128)S(1)} %add.79), channel_id=1, source_target_pairs={{0,6},{1,7},{2,0},{3,1},{4,2},{5,3},{6,4},{7,5},{8,14},{9,15},{10,... | collective-permute-start | bytes 786440 | tf_op jit(solution)/shard_map/ppermute | solution.py:307
  50.2 10.2 %collective-permute-done.10 = f32[64,1024]{1,0:T(8,128)S(1)} collective-permute-done((f32[64,1024]{1,0:T(8,128)S(1)}, f32[64,1024]{1,0:T(8,128)S(1)}, u32[]{:S(2)}, u32[]{:S(2)}) %collective-permute-start.10) | collective-permute-done | bytes 262176 | tf_op jit(solution)/shard_map/ppermute | solution.py:307
  60.4 0.6 collective-permute-done.8
  61.1 0.1 pad_maximum_fusion.mine
  61.2 0.1 collective-permute-start.13
  61.3 1.0 collective-permute-start.21
  62.4 0.1 add.81
  62.5 0.7 collective-permute-start.18
  63.2 2.3 %collective-permute-start.16 = (f32[512,128]{1,0:T(8,128)S(1)}, f32[512,128]{1,0:T(8,128)S(1)}, u32[]{:S(2)}, u32[]{:S(2)}) collective-permute-start(f32[512,128]{1,0:T(8,128)S(1)} %get-tuple-element.90), channel_id=1, source_target_pairs={{0,2},{1,3},{2,4},{3,5},{4,6},{5,7},{6,0},{7,1},{8,10},{9,11},{10,... | collective-permute-start | bytes 786440 | tf_op jit(solution)/shard_map/ppermute | solution.py:260
  65.6 0.9 collective-permute-start.17
  66.5 3.5 %scores.1 = (f32[8,1024]{1,0:T(8,128)S(1)}, f32[8,1024]{1,0:T(8,128)S(1)}) custom-call(s32[4]{0:T(128)S(1)} %pad_add_fusion.idx, bf16[1024,128]{1,0:T(8,128)(2,1)} %og.1, bf16[2048,128]{1,0:T(8,128)(2,1)} %bitcast.45, f32[2048,128]{1,0:T(8,128)S(1)} %collective-permute-done.4.a1.b1, f32[2048,128]{1,0:T(8,128)S(1)} %collective-permute-done.4.a1.b1, ...), custom_call_target="tpu_custom_call" | custom-call | tf_op jit(solution)/shard_map/scores/pallas_call | solution.py:244
  70.0 0.1 collective-permute-start.14
  70.1 1.2 %collective-permute-done.14 = f32[8,1024]{1,0:T(8,128)S(1)} collective-permute-done((f32[8,1024]{1,0:T(8,128)S(1)}, f32[8,1024]{1,0:T(8,128)S(1)}, u32[]{:S(2)}, u32[]{:S(2)}) %collective-permute-start.14) | collective-permute-done | bytes 32800 | tf_op jit(solution)/shard_map/ppermute | solution.py:316
  71.3 1.7 %collective-permute-start.15 = (f32[8,1024]{1,0:T(8,128)S(1)}, f32[8,1024]{1,0:T(8,128)S(1)}, u32[]{:S(2)}, u32[]{:S(2)}) collective-permute-start(f32[8,1024]{1,0:T(8,128)S(1)} %add.82), channel_id=1, source_target_pairs={{0,4},{1,5},{2,6},{3,7},{4,0},{5,1},{6,2},{7,3},{8,12},{9,13},{10,... | collective-permute-start | bytes 98312 | tf_op jit(solution)/shard_map/ppermute | solution.py:317
  73.0 5.9 %collective-permute-done.15 = f32[8,1024]{1,0:T(8,128)S(1)} collective-permute-done((f32[8,1024]{1,0:T(8,128)S(1)}, f32[8,1024]{1,0:T(8,128)S(1)}, u32[]{:S(2)}, u32[]{:S(2)}) %collective-permute-start.15) | collective-permute-done | bytes 32800 | tf_op jit(solution)/shard_map/ppermute | solution.py:317
  79.0 0.1 collective-permute-start.19
  79.1 3.9 %collective-permute-done.19 = f32[8,1024]{1,0:T(8,128)S(1)} collective-permute-done((f32[8,1024]{1,0:T(8,128)S(1)}, f32[8,1024]{1,0:T(8,128)S(1)}, u32[]{:S(2)}, u32[]{:S(2)}) %collective-permute-start.19) | collective-permute-done | bytes 32800 | tf_op jit(solution)/shard_map/ppermute | solution.py:319
  83.0 1.0 collective-permute-start.20
  84.0 3.6 %collective-permute-done.20 = f32[8,1024]{1,0:T(8,128)S(1)} collective-permute-done((f32[8,1024]{1,0:T(8,128)S(1)}, f32[8,1024]{1,0:T(8,128)S(1)}, u32[]{:S(2)}, u32[]{:S(2)}) %collective-permute-start.20) | collective-permute-done | bytes 32800 | tf_op jit(solution)/shard_map/ppermute | solution.py:320
  87.6 6.4 %collective-permute-start.25 = (f32[8,128]{1,0:T(8,128)S(1)}, f32[8,128]{1,0:T(8,128)S(1)}, u32[]{:S(2)}, u32[]{:S(2)}) collective-permute-start(f32[8,128]{1,0:T(8,128)S(1)} %get-tuple-element.83), channel_id=1, source_target_pairs={{0,128},{64,192},{128,0},{192,64},{1,129},{65,193},{129,1},{193,65... | collective-permute-start | bytes 12296 | tf_op jit(solution)/shard_map/ppermute | solution.py:326
  94.0 0.1 add.89
  94.2 1.4 %collective-permute-done.25 = f32[8,128]{1,0:T(8,128)S(1)} collective-permute-done((f32[8,128]{1,0:T(8,128)S(1)}, f32[8,128]{1,0:T(8,128)S(1)}, u32[]{:S(2)}, u32[]{:S(2)}) %collective-permute-start.25) | collective-permute-done | bytes 4128 | tf_op jit(solution)/shard_map/ppermute | solution.py:326
  95.6 2.9 %collective-permute-start.26 = (f32[8,128]{1,0:T(8,128)S(1)}, f32[8,128]{1,0:T(8,128)S(1)}, u32[]{:S(2)}, u32[]{:S(2)}) collective-permute-start(f32[8,128]{1,0:T(8,128)S(1)} %add.93), channel_id=1, source_target_pairs={{0,64},{64,0},{128,192},{192,128},{1,65},{65,1},{129,193},{193,129... | collective-permute-start | bytes 12296 | tf_op jit(solution)/shard_map/ppermute | solution.py:327
  98.5 2.4 %collective-permute-start.24 = (f32[512,128]{1,0:T(8,128)S(1)}, f32[512,128]{1,0:T(8,128)S(1)}, u32[]{:S(2)}, u32[]{:S(2)}) collective-permute-start(f32[512,128]{1,0:T(8,128)S(1)} %get-tuple-element.86), channel_id=1, source_target_pairs={{0,6},{1,7},{2,0},{3,1},{4,2},{5,3},{6,4},{7,5},{8,14},{9,15},{10,... | collective-permute-start | bytes 786440 | tf_op jit(solution)/shard_map/ppermute | solution.py:260
  101.0 1.6 %collective-permute-start.22 = (f32[512,128]{1,0:T(8,128)S(1)}, f32[512,128]{1,0:T(8,128)S(1)}, u32[]{:S(2)}, u32[]{:S(2)}) collective-permute-start(f32[512,128]{1,0:T(8,128)S(1)} %get-tuple-element.88), channel_id=1, source_target_pairs={{0,4},{1,5},{2,6},{3,7},{4,0},{5,1},{6,2},{7,3},{8,12},{9,13},{10,... | collective-permute-start | bytes 786440 | tf_op jit(solution)/shard_map/ppermute | solution.py:260
  102.5 0.1 add_reduce_fusion
  102.7 0.7 divide_bitcast_fusion
  103.4 7.1 %collective-permute-done.24 = f32[512,128]{1,0:T(8,128)S(1)} collective-permute-done((f32[512,128]{1,0:T(8,128)S(1)}, f32[512,128]{1,0:T(8,128)S(1)}, u32[]{:S(2)}, u32[]{:S(2)}) %collective-permute-start.24) | collective-permute-done | bytes 262176 | tf_op jit(solution)/shard_map/ppermute | solution.py:260
  110.5 3.2 %collective-permute-done.23 = f32[512,128]{1,0:T(8,128)S(1)} collective-permute-done((f32[512,128]{1,0:T(8,128)S(1)}, f32[512,128]{1,0:T(8,128)S(1)}, u32[]{:S(2)}, u32[]{:S(2)}) %collective-permute-start.23) | collective-permute-done | bytes 262176 | tf_op jit(solution)/shard_map/ppermute | solution.py:260
  113.7 0.1 fusion.11
  113.8 0.7 pad_maximum_fusion.2
  (37 shorter events, 0.5 us)
Async XLA Ops:
  0.7 17.5 %slice-start = ((s8[7340032]{0:T(1024)(128)(4,1)}), s8[4194304]{0:T(1024)(128)(4,1)S(1)}, s32[]{:S(2)}) async-start(s8[7340032]{0:T(1024)(128)(4,1)} %bitcast.42), calls=%async_computation | async-start | bytes 8388608
  0.7 17.5 %slice-start.1 = ((s8[7340032]{0:T(1024)(128)(4,1)}), s8[3145728]{0:T(1024)(128)(4,1)S(1)}, s32[]{:S(2)}) async-start(s8[7340032]{0:T(1024)(128)(4,1)} %bitcast.42), calls=%async_computation.1 | async-start | bytes 6291456
  5.4 5.1 %collective-permute-start = (f32[1536,128]{1,0:T(8,128)S(1)}, f32[1536,128]{1,0:T(8,128)S(1)}, u32[]{:S(2)}, u32[]{:S(2)}) collective-permute-start(f32[1536,128]{1,0:T(8,128)S(1)} %get-tuple-element.43), channel_id=1, source_target_pairs={{0,8},{8,0},{16,24},{24,16},{32,40},{40,32},{48,56},{56,48},{1,9},... | collective-permute-start | bytes 2359304 | tf_op jit(solution)/shard_map/ppermute | solution.py:283
  5.5 23.0 %collective-permute-start.4 = (f32[2048,128]{1,0:T(8,128)S(1)}, f32[2048,128]{1,0:T(8,128)S(1)}, u32[]{:S(2)}, u32[]{:S(2)}) collective-permute-start(f32[2048,128]{1,0:T(8,128)S(1)} %get-tuple-element.44), channel_id=1, source_target_pairs={{0,16},{8,56},{16,32},{24,8},{32,48},{40,24},{48,0},{56,40},{1,17}... | collective-permute-start | bytes 3145736 | tf_op jit(solution)/shard_map/ppermute | solution.py:285
  10.6 20.1 %collective-permute-start.5 = (f32[1536,128]{1,0:T(8,128)S(1)}, f32[1536,128]{1,0:T(8,128)S(1)}, u32[]{:S(2)}, u32[]{:S(2)}) collective-permute-start(f32[1536,128]{1,0:T(8,128)S(1)} %collective-permute-done), channel_id=1, source_target_pairs={{0,16},{8,56},{16,32},{24,8},{32,48},{40,24},{48,0},{56,40},{1,17}... | collective-permute-start | bytes 2359304 | tf_op jit(solution)/shard_map/ppermute | solution.py:290
  11.8 18.7 %collective-permute-start.1 = (f32[64,1024]{1,0:T(8,128)S(1)}, f32[64,1024]{1,0:T(8,128)S(1)}, u32[]{:S(2)}, u32[]{:S(2)}) collective-permute-start(f32[64,1024]{1,0:T(8,128)S(1)} %get-tuple-element.53), channel_id=1, source_target_pairs={{0,4},{1,5},{2,6},{3,7},{4,0},{5,1},{6,2},{7,3},{8,12},{9,13},{10,... | collective-permute-start | bytes 786440 | tf_op jit(solution)/shard_map/ppermute | solution.py:260
  15.0 15.5 %collective-permute-start.2 = (f32[64,1024]{1,0:T(8,128)S(1)}, f32[64,1024]{1,0:T(8,128)S(1)}, u32[]{:S(2)}, u32[]{:S(2)}) collective-permute-start(f32[64,1024]{1,0:T(8,128)S(1)} %get-tuple-element.54), channel_id=1, source_target_pairs={{0,2},{1,3},{2,4},{3,5},{4,6},{5,7},{6,0},{7,1},{8,10},{9,11},{10,... | collective-permute-start | bytes 786440 | tf_op jit(solution)/shard_map/ppermute | solution.py:260
  15.7 14.9 %collective-permute-start.3 = (f32[64,1024]{1,0:T(8,128)S(1)}, f32[64,1024]{1,0:T(8,128)S(1)}, u32[]{:S(2)}, u32[]{:S(2)}) collective-permute-start(f32[64,1024]{1,0:T(8,128)S(1)} %get-tuple-element.55), channel_id=1, source_target_pairs={{0,6},{1,7},{2,0},{3,1},{4,2},{5,3},{6,4},{7,5},{8,14},{9,15},{10,... | collective-permute-start | bytes 786440 | tf_op jit(solution)/shard_map/ppermute | solution.py:260
  28.6 16.6 %collective-permute-start.7 = (f32[4,192,128]{2,1,0:T(8,128)S(1)}, f32[4,192,128]{2,1,0:T(8,128)S(1)}, u32[]{:S(2)}, u32[]{:S(2)}) collective-permute-start(f32[4,192,128]{2,1,0:T(8,128)S(1)} %get-tuple-element.63), channel_id=1, source_target_pairs={{0,1},{1,0},{2,3},{3,2},{4,5},{5,4},{6,7},{7,6},{8,9},{9,8},{10,11... | collective-permute-start | bytes 1179656 | tf_op jit(solution)/shard_map/ppermute | solution.py:296
  30.7 14.4 %collective-permute-start.6 = (f32[64,1024]{1,0:T(8,128)S(1)}, f32[64,1024]{1,0:T(8,128)S(1)}, u32[]{:S(2)}, u32[]{:S(2)}) collective-permute-start(f32[64,1024]{1,0:T(8,128)S(1)} %add_add_fusion), channel_id=1, source_target_pairs={{0,1},{1,0},{2,3},{3,2},{4,5},{5,4},{6,7},{7,6},{8,9},{9,8},{10,11... | collective-permute-start | bytes 786440 | tf_op jit(solution)/shard_map/ppermute | solution.py:302
  30.9 30.3 %collective-permute-start.11 = (f32[1536,128]{1,0:T(8,128)S(1)}, f32[1536,128]{1,0:T(8,128)S(1)}, u32[]{:S(2)}, u32[]{:S(2)}) collective-permute-start(f32[1536,128]{1,0:T(8,128)S(1)} %slice.27), channel_id=1, source_target_pairs={{0,16},{8,56},{16,32},{24,8},{32,48},{40,24},{48,0},{56,40},{1,17}... | collective-permute-start | bytes 2359304 | tf_op jit(solution)/shard_map/ppermute | solution.py:301
  45.1 16.1 %collective-permute-start.12 = (f32[4,320,128]{2,1,0:T(8,128)S(1)}, f32[4,320,128]{2,1,0:T(8,128)S(1)}, u32[]{:S(2)}, u32[]{:S(2)}) collective-permute-start(f32[4,320,128]{2,1,0:T(8,128)S(1)} %get-tuple-element.68), channel_id=1, source_target_pairs={{0,1},{1,0},{2,3},{3,2},{4,5},{5,4},{6,7},{7,6},{8,9},{9,8},{10,11... | collective-permute-start | bytes 1966088 | tf_op jit(solution)/shard_map/ppermute | solution.py:305
  47.0 13.5 %collective-permute-start.10 = (f32[64,1024]{1,0:T(8,128)S(1)}, f32[64,1024]{1,0:T(8,128)S(1)}, u32[]{:S(2)}, u32[]{:S(2)}) collective-permute-start(f32[64,1024]{1,0:T(8,128)S(1)} %add.79), channel_id=1, source_target_pairs={{0,2},{1,3},{2,4},{3,5},{4,6},{5,7},{6,0},{7,1},{8,10},{9,11},{10,... | collective-permute-start | bytes 786440 | tf_op jit(solution)/shard_map/ppermute | solution.py:307
  47.0 13.5 %collective-permute-start.9 = (f32[64,1024]{1,0:T(8,128)S(1)}, f32[64,1024]{1,0:T(8,128)S(1)}, u32[]{:S(2)}, u32[]{:S(2)}) collective-permute-start(f32[64,1024]{1,0:T(8,128)S(1)} %add.79), channel_id=1, source_target_pairs={{0,4},{1,5},{2,6},{3,7},{4,0},{5,1},{6,2},{7,3},{8,12},{9,13},{10,... | collective-permute-start | bytes 786440 | tf_op jit(solution)/shard_map/ppermute | solution.py:307
  48.7 12.3 %collective-permute-start.8 = (f32[64,1024]{1,0:T(8,128)S(1)}, f32[64,1024]{1,0:T(8,128)S(1)}, u32[]{:S(2)}, u32[]{:S(2)}) collective-permute-start(f32[64,1024]{1,0:T(8,128)S(1)} %add.79), channel_id=1, source_target_pairs={{0,6},{1,7},{2,0},{3,1},{4,2},{5,3},{6,4},{7,5},{8,14},{9,15},{10,... | collective-permute-start | bytes 786440 | tf_op jit(solution)/shard_map/ppermute | solution.py:307
  61.2 5.3 %collective-permute-start.13 = (f32[4,64,1024]{2,1,0:T(8,128)S(1)}, f32[4,64,1024]{2,1,0:T(8,128)S(1)}, u32[]{:S(2)}, u32[]{:S(2)}) collective-permute-start(f32[4,64,1024]{2,1,0:T(8,128)S(1)} %pad_maximum_fusion.mine), channel_id=1, source_target_pairs={{0,8},{8,0},{16,24},{24,16},{32,40},{40,32},{48,56},{56,48},{1,9},... | collective-permute-start | bytes 3145736 | tf_op jit(solution)/shard_map/ppermute | solution.py:310
  61.3 26.3 %collective-permute-start.21 = (f32[4,512,128]{2,1,0:T(8,128)S(1)}, f32[4,512,128]{2,1,0:T(8,128)S(1)}, u32[]{:S(2)}, u32[]{:S(2)}) collective-permute-start(f32[4,512,128]{2,1,0:T(8,128)S(1)} %get-tuple-element.81), channel_id=1, source_target_pairs={{0,1},{1,0},{2,3},{3,2},{4,5},{5,4},{6,7},{7,6},{8,9},{9,8},{10,11... | collective-permute-start | bytes 3145736 | tf_op jit(solution)/shard_map/ppermute | solution.py:311
  62.5 16.4 %collective-permute-start.18 = (f32[512,128]{1,0:T(8,128)S(1)}, f32[512,128]{1,0:T(8,128)S(1)}, u32[]{:S(2)}, u32[]{:S(2)}) collective-permute-start(f32[512,128]{1,0:T(8,128)S(1)} %get-tuple-element.89), channel_id=1, source_target_pairs={{0,4},{1,5},{2,6},{3,7},{4,0},{5,1},{6,2},{7,3},{8,12},{9,13},{10,... | collective-permute-start | bytes 786440 | tf_op jit(solution)/shard_map/ppermute | solution.py:260
  63.2 15.7 %collective-permute-start.16 = (f32[512,128]{1,0:T(8,128)S(1)}, f32[512,128]{1,0:T(8,128)S(1)}, u32[]{:S(2)}, u32[]{:S(2)}) collective-permute-start(f32[512,128]{1,0:T(8,128)S(1)} %get-tuple-element.90), channel_id=1, source_target_pairs={{0,2},{1,3},{2,4},{3,5},{4,6},{5,7},{6,0},{7,1},{8,10},{9,11},{10,... | collective-permute-start | bytes 786440 | tf_op jit(solution)/shard_map/ppermute | solution.py:260
  65.6 13.4 %collective-permute-start.17 = (f32[512,128]{1,0:T(8,128)S(1)}, f32[512,128]{1,0:T(8,128)S(1)}, u32[]{:S(2)}, u32[]{:S(2)}) collective-permute-start(f32[512,128]{1,0:T(8,128)S(1)} %get-tuple-element.91), channel_id=1, source_target_pairs={{0,6},{1,7},{2,0},{3,1},{4,2},{5,3},{6,4},{7,5},{8,14},{9,15},{10,... | collective-permute-start | bytes 786440 | tf_op jit(solution)/shard_map/ppermute | solution.py:260
  70.0 1.3 %collective-permute-start.14 = (f32[8,1024]{1,0:T(8,128)S(1)}, f32[8,1024]{1,0:T(8,128)S(1)}, u32[]{:S(2)}, u32[]{:S(2)}) collective-permute-start(f32[8,1024]{1,0:T(8,128)S(1)} %get-tuple-element.75), channel_id=1, source_target_pairs={{0,8},{8,0},{16,24},{24,16},{32,40},{40,32},{48,56},{56,48},{1,9},... | collective-permute-start | bytes 98312 | tf_op jit(solution)/shard_map/ppermute | solution.py:316
  71.3 7.6 %collective-permute-start.15 = (f32[8,1024]{1,0:T(8,128)S(1)}, f32[8,1024]{1,0:T(8,128)S(1)}, u32[]{:S(2)}, u32[]{:S(2)}) collective-permute-start(f32[8,1024]{1,0:T(8,128)S(1)} %add.82), channel_id=1, source_target_pairs={{0,4},{1,5},{2,6},{3,7},{4,0},{5,1},{6,2},{7,3},{8,12},{9,13},{10,... | collective-permute-start | bytes 98312 | tf_op jit(solution)/shard_map/ppermute | solution.py:317
  79.0 4.0 %collective-permute-start.19 = (f32[8,1024]{1,0:T(8,128)S(1)}, f32[8,1024]{1,0:T(8,128)S(1)}, u32[]{:S(2)}, u32[]{:S(2)}) collective-permute-start(f32[8,1024]{1,0:T(8,128)S(1)} %add.83), channel_id=1, source_target_pairs={{0,2},{1,3},{2,0},{3,1},{4,6},{5,7},{6,4},{7,5},{8,10},{9,11},{10,... | collective-permute-start | bytes 98312 | tf_op jit(solution)/shard_map/ppermute | solution.py:319
  83.0 4.6 %collective-permute-start.20 = (f32[8,1024]{1,0:T(8,128)S(1)}, f32[8,1024]{1,0:T(8,128)S(1)}, u32[]{:S(2)}, u32[]{:S(2)}) collective-permute-start(f32[8,1024]{1,0:T(8,128)S(1)} %add.87), channel_id=1, source_target_pairs={{0,1},{1,0},{2,3},{3,2},{4,5},{5,4},{6,7},{7,6},{8,9},{9,8},{10,11... | collective-permute-start | bytes 98312 | tf_op jit(solution)/shard_map/ppermute | solution.py:320
  87.6 8.0 %collective-permute-start.25 = (f32[8,128]{1,0:T(8,128)S(1)}, f32[8,128]{1,0:T(8,128)S(1)}, u32[]{:S(2)}, u32[]{:S(2)}) collective-permute-start(f32[8,128]{1,0:T(8,128)S(1)} %get-tuple-element.83), channel_id=1, source_target_pairs={{0,128},{64,192},{128,0},{192,64},{1,129},{65,193},{129,1},{193,65... | collective-permute-start | bytes 12296 | tf_op jit(solution)/shard_map/ppermute | solution.py:326
  95.6 7.0 %collective-permute-start.26 = (f32[8,128]{1,0:T(8,128)S(1)}, f32[8,128]{1,0:T(8,128)S(1)}, u32[]{:S(2)}, u32[]{:S(2)}) collective-permute-start(f32[8,128]{1,0:T(8,128)S(1)} %add.93), channel_id=1, source_target_pairs={{0,64},{64,0},{128,192},{192,128},{1,65},{65,1},{129,193},{193,129... | collective-permute-start | bytes 12296 | tf_op jit(solution)/shard_map/ppermute | solution.py:327
  98.5 12.0 %collective-permute-start.24 = (f32[512,128]{1,0:T(8,128)S(1)}, f32[512,128]{1,0:T(8,128)S(1)}, u32[]{:S(2)}, u32[]{:S(2)}) collective-permute-start(f32[512,128]{1,0:T(8,128)S(1)} %get-tuple-element.86), channel_id=1, source_target_pairs={{0,6},{1,7},{2,0},{3,1},{4,2},{5,3},{6,4},{7,5},{8,14},{9,15},{10,... | collective-permute-start | bytes 786440 | tf_op jit(solution)/shard_map/ppermute | solution.py:260
  101.0 12.7 %collective-permute-start.23 = (f32[512,128]{1,0:T(8,128)S(1)}, f32[512,128]{1,0:T(8,128)S(1)}, u32[]{:S(2)}, u32[]{:S(2)}) collective-permute-start(f32[512,128]{1,0:T(8,128)S(1)} %get-tuple-element.87), channel_id=1, source_target_pairs={{0,2},{1,3},{2,4},{3,5},{4,6},{5,7},{6,0},{7,1},{8,10},{9,11},{10,... | collective-permute-start | bytes 786440 | tf_op jit(solution)/shard_map/ppermute | solution.py:260
  101.0 12.7 %collective-permute-start.22 = (f32[512,128]{1,0:T(8,128)S(1)}, f32[512,128]{1,0:T(8,128)S(1)}, u32[]{:S(2)}, u32[]{:S(2)}) collective-permute-start(f32[512,128]{1,0:T(8,128)S(1)} %get-tuple-element.88), channel_id=1, source_target_pairs={{0,4},{1,5},{2,6},{3,7},{4,0},{5,1},{6,2},{7,3},{8,12},{9,13},{10,... | collective-permute-start | bytes 786440 | tf_op jit(solution)/shard_map/ppermute | solution.py:260

commit v5 on v4

--- a/solution.py
+++ b/solution.py
@@ -159,14 +159,14 @@
     )(idx, weight, in_vmem(af), in_vmem(a))
 
 
-def layer_kernel(idx, a, w, *outs, first, blocks):
+def layer_kernel(idx, a, w, *outs, blocks):
     width = w.shape[1] // 4
 
     @pl.loop(0, 4)
     def _(j):
         owner = lax.rem(idx[2] + j, 4)
         acc = jnp.dot(
-            a[first : first + sum(blocks), :],
+            a[...],
             w[:, pl.ds(pl.multiple_of(owner * width, width), width)],
             preferred_element_type=F32,
         )
@@ -177,25 +177,48 @@
             keep[j] = jnp.where(at_low, low[at : at + rows], high[at : at + rows])
             send[j] = jnp.where(at_low, high[at : at + rows], low[at : at + rows])
             at += rows
-
-
-def layer(idx, a, w, first, blocks):
-    shapes = [
-        jax.ShapeDtypeStruct((4, rows, w.shape[1] // 8), F32) for rows in blocks for _ in range(2)
-    ]
-    return pl.pallas_call(
-        functools.partial(layer_kernel, first=first, blocks=blocks),
+        outs[-1][j] = acc[at:]
+
+
+def layer(idx, a, w, blocks):
+    width = w.shape[1] // 4
+    shapes = [(4, rows, width // 2) for rows in blocks for _ in range(2)]
+    shapes.append((4, a.shape[0] - sum(blocks), width))
+    return pl.pallas_call(
+        functools.partial(layer_kernel, blocks=blocks),
         grid_spec=pltpu.PrefetchScalarGridSpec(
             num_scalar_prefetch=1,
             grid=(),
             in_specs=[WHOLE] * 2,
             out_specs=[WHOLE] * len(shapes),
         ),
-        out_shape=shapes,
+        out_shape=[jax.ShapeDtypeStruct(shape, F32) for shape in shapes],
         compiler_params=params(8 * MIB),
         cost_estimate=cost(),
         name="layer",
     )(idx, in_vmem(a), in_vmem(w))
+
+
+def halves_kernel(idx, a, b, c, d, keep, send):
+    total = (a[...] + d[...]) + (b[...] + c[...])
+    half = keep.shape[1]
+    low, high = total[:, :half], total[:, half:]
+    keep[...] = jnp.where(idx[3] == 0, low, high)
+    send[...] = jnp.where(idx[3] == 0, high, low)
+
+
+def halves(idx, parts):
+    rows, width = parts[0].shape
+    return pl.pallas_call(
+        halves_kernel,
+        grid_spec=pltpu.PrefetchScalarGridSpec(
+            num_scalar_prefetch=1, grid=(), in_specs=[WHOLE] * 4, out_specs=[WHOLE] * 2
+        ),
+        out_shape=[jax.ShapeDtypeStruct((rows, width // 2), F32)] * 2,
+        compiler_params=params(8 * MIB),
+        cost_estimate=cost(),
+        name="halves",
+    )(idx, *parts)
 
 
 def score_kernel(idx, og, gf, a1, b1, a2, b2, a3, b3, mine, other, keep, send, *, ranks):
@@ -222,7 +245,7 @@
 def scores(idx, og, gf, near, far, mine, other, ranks):
     tokens, width = og.shape
     qr = gf.shape[0] // 4
-    tile = 256
+    tile = 512
     assert qr % tile == 0 and tokens % qr == 0
     spec = lambda rows, at: pl.BlockSpec((rows, width), lambda i, idx: (at(i, idx), 0))
     skip = qr // tile
@@ -291,47 +314,43 @@
     own = sum_y(pieces[0], send_y(pieces))
 
     at = after(idx, pieces[0])
-    keep0, send0 = layer(at, activations, down_weight, 0, (192,))
-    send0, near0 = lax.optimization_barrier((send0, near0))
+    keep0, send0, keep1, send1, parts = layer(at, activations, down_weight, (352, 288))
+
+    own, send0 = lax.optimization_barrier((own, send0))
+    own = own + lax.ppermute(own, "tensor", z_swap())
+
+    own, send0, near0, near1 = lax.optimization_barrier((own, send0, near0, near1))
     got0 = lax.ppermute(send0, "tensor", z_swap())
-    at = after(idx, keep0)
-    keep1, send1, keep2, send2 = layer(at, activations, down_weight, 192, (320, 512))
-
-    own, near0, near1, send1 = lax.optimization_barrier((own, near0, near1, send1))
     far = ring(near0[gf.shape[0] // 4 :])
-    own = own + lax.ppermute(own, "tensor", z_swap())
-
-    own, send1, got0 = lax.optimization_barrier((own, send1, got0))
-    got1 = lax.ppermute(send1, "tensor", z_swap())
     mine = jnp.stack(
         [own] + [lax.ppermute(own, "tensor", y_shift(-j)) for j in (1, 2, 3)]
     )
-    mine, far, got1, send2 = lax.optimization_barrier((mine, far, got1, send2))
+    mine, far, got0, send1, parts = lax.optimization_barrier((mine, far, got0, send1, parts))
     other = swap(mine)
-    got2 = lax.ppermute(send2, "tensor", z_swap())
-    keep1 = jnp.concatenate([keep0 + got0, keep1 + got1], axis=1)
-    got1 = send_y(keep1)
+    got1 = lax.ppermute(send1, "tensor", z_swap())
+    got = send_y(parts)
 
     raw, send = scores(idx, output_grads, gf, (near0, near1), far, mine, other, ranks)
     raw = raw + swap(send)
+    raw, got1 = lax.optimization_barrier((raw, got1))
+    raw = raw + lax.ppermute(raw, "tensor", z_swap())
     raw = raw + lax.ppermute(raw, "tensor", y_shift(2))
-    raw, got1 = lax.optimization_barrier((raw, got1))
+    raw, got = lax.optimization_barrier((raw, got))
+    keep, send = halves(idx, [parts[0], *got])
+    out1 = (keep + lax.ppermute(send, "tensor", z_swap())).astype(jnp.bfloat16)
     raw = raw + lax.ppermute(raw, "tensor", y_pair())
-    raw = raw + lax.ppermute(raw, "tensor", z_swap())
+    raw, keep0, keep1 = lax.optimization_barrier((raw, keep0, keep1))
+    keep0 = jnp.concatenate([keep0 + got0, keep1 + got1], axis=1)
+    got0 = send_y(keep0)
 
     square = jnp.sum((raw * raw).reshape(queries, -1, 128), axis=1)
-    square, got2 = lax.optimization_barrier((square, got2))
-    keep2 = keep2 + got2
-    got2 = send_y(keep2)
     square = square + lax.ppermute(square, "dp", dp_shift(2))
+    square, got0[0], got0[1], got0[2] = lax.optimization_barrier((square, *got0))
     square = square + lax.ppermute(square, "dp", [(i, i ^ 1) for i in range(4)])
     spread = jnp.sum(square, axis=1, keepdims=True) / (tokens * lax.axis_size("dp"))
     influence = raw / jnp.sqrt(spread + 1e-06)
-    outputs = [
-        sum_y(keep[0], got).astype(jnp.bfloat16)
-        for keep, got in ((keep1, got1), (keep2, got2))
-    ]
-    return (jnp.concatenate(outputs, axis=0), influence.T)
+    out0 = sum_y(keep0[0], got0).astype(jnp.bfloat16)
+    return (jnp.concatenate([out0, out1], axis=0), influence.T)
 
 
 def solution(mesh):

time: 115 us -> 105 us (0.913)
  waiting for transfers between devices: 50 us -> 34.2 us
  starting transfers between devices: 39.3 us -> 47.4 us
  Pallas kernels: 21.9 us -> 20 us
    ppermute x9, waiting for transfers between devices: 10.4 us -> 2.13 us  [send_y(): return [lax.ppermute(parts[j], 'tensor', y_shift(j)) for j in (1, 3, 2)]]
    ppermute x1, waiting for transfers between devices: 12.7 us -> 6.15 us  [body(): own = own + lax.ppermute(own, 'tensor', z_swap())]
    ppermute x1, waiting for transfers between devices: 0.01 us -> 5.49 us  [body(): got1 = lax.ppermute(send1, 'tensor', z_swap())]
    ppermute x1, waiting for transfers between devices: 3.9 us -> 0.01 us  [body(): raw = raw + lax.ppermute(raw, 'tensor', y_pair())]
    ppermute x9, starting transfers between devices: 14.4 us -> 17.7 us  [send_y(): return [lax.ppermute(parts[j], 'tensor', y_shift(j)) for j in (1, 3, 2)]]
    ppermute x1, waiting for transfers between devices: 5.92 us -> 3.49 us  [body(): raw = raw + lax.ppermute(raw, 'tensor', y_shift(2))]
    ppermute x1, starting transfers between devices: 0.2 us -> 2 us  [body(): own = own + lax.ppermute(own, 'tensor', z_swap())]
    ppermute x1, starting transfers between devices: 0.09 us -> 1.77 us  [body(): raw = raw + lax.ppermute(raw, 'tensor', y_pair())]
  transfers between devices with their start and end apart: 27 -> 27, of which waited for: 10 -> 13; matrix products, arithmetic and copies ran while one was open for 1% -> 1% of each run, Pallas kernels for 15% -> 15%
where the time goes in v5:
time: 105 us
  starting transfers between devices  47.4 us (45%)
  waiting for transfers between devices  34.2 us (33%)
  Pallas kernels  20 us (19%)
  other arithmetic  2.24 us (2%)
    ppermute x9, starting transfers between devices, send_y(): return [lax.ppermute(parts[j], 'tensor', y_shift(j)) for j in (1, 3, 2)]  17.7 us
    ppermute x3, waiting for transfers between devices, body(): lax.ppermute(own, 'tensor', y_shift(-j))  10.9 us
    pallas_call x1, Pallas kernels, layer(): pl.pallas_call(functools.partial(layer_kernel, blocks=blocks), grid_spec=...  8.81 us
    ppermute x1, starting transfers between devices, body(): square = square + lax.ppermute(square, 'dp', dp_shift(2))  6.45 us
    ppermute x1, waiting for transfers between devices, body(): own = own + lax.ppermute(own, 'tensor', z_swap())  6.15 us
    ppermute x1, waiting for transfers between devices, body(): got1 = lax.ppermute(send1, 'tensor', z_swap())  5.49 us
    ppermute x3, starting transfers between devices, body(): lax.ppermute(own, 'tensor', y_shift(-j))  4.66 us
    pallas_call x1, Pallas kernels, pack(): pl.pallas_call(pack_kernel, grid_spec=pltpu.PrefetchScalarGridSpec(num_sc...  4.43 us
  transfers between devices with their start and end apart: 27, of which 13 were waited for; matrix products, arithmetic and copies ran while one was open for 1% of the time, Pallas kernels for 15%

profile of v5, /device:TPU:2, one launch (start us, length us, event | category | flops | bytes accessed | tf_op | source)
XLA Modules:
  0.0 104.8 jit_solution(15032882360958164302)
XLA Ops:
  0.7 4.4 %pack.1 = (f32[2048,128]{1,0:T(8,128)S(1)}, f32[1536,128]{1,0:T(8,128)S(1)}, bf16[1024,3584]{1,0:T(8,128)(2,1)S(1)}, bf16[256,3584]{1,0:T(8,128)(2,1)S(1)}, f32[8,32]{1,0:T(8,128)S(1)}) custom-call(s32[4]{0:T(128)S(1)} %pad_add_fusion.idx, bf16[1024,128]{1,0:T(8,128)(2,1)} %og.1, bf16[2048,128]{1,0:T(8,128)(2,1)} %bitcast.36, bf16[1024,3584]{1,0:T(8,128)(2,1)} %refs_0_.1, ...), custom_call_target="tpu_custom_call" | custom-call | bytes 41943040 | tf_op jit(solution)/shard_map/pack/pallas_call | solution.py:93
  5.3 1.6 %collective-permute-start.5 = (f32[2048,128]{1,0:T(8,128)S(1)}, f32[2048,128]{1,0:T(8,128)S(1)}, u32[]{:S(2)}, u32[]{:S(2)}) collective-permute-start(f32[2048,128]{1,0:T(8,128)S(1)} %get-tuple-element.49), channel_id=1, source_target_pairs={{0,16},{8,56},{16,32},{24,8},{32,48},{40,24},{48,0},{56,40},{1,17}... | collective-permute-start | bytes 3145736 | tf_op jit(solution)/shard_map/ppermute | solution.py:308
  6.9 3.4 %act.1 = (f32[64,1024]{1,0:T(8,128)S(1)}, f32[64,1024]{1,0:T(8,128)S(1)}, f32[64,1024]{1,0:T(8,128)S(1)}, f32[64,1024]{1,0:T(8,128)S(1)}) custom-call(s32[4]{0:T(128)S(1)} %pad_add_fusion.idx, f32[8,32]{1,0:T(8,128)S(1)} %get-tuple-element.51.weight, bf16[256,3584]{1,0:T(8,128)(2,1)S(1)} %get-tuple-element.52.af, bf16[1024,3584]{1,0:T(8,128)(2,1)S(1)} %get-tuple-element.53.a), custom_call_target="tpu_custom_call" | custom-call | bytes 20971520 | tf_op jit(solution)/shard_map/act/pallas_call | solution.py:146
  10.3 1.3 %collective-permute-start.6 = (f32[1536,128]{1,0:T(8,128)S(1)}, f32[1536,128]{1,0:T(8,128)S(1)}, u32[]{:S(2)}, u32[]{:S(2)}) collective-permute-start(f32[1536,128]{1,0:T(8,128)S(1)} %collective-permute-done), channel_id=1, source_target_pairs={{0,16},{8,56},{16,32},{24,8},{32,48},{40,24},{48,0},{56,40},{1,17}... | collective-permute-start | bytes 2359304 | tf_op jit(solution)/shard_map/ppermute | solution.py:313
  11.6 3.2 %collective-permute-start.1 = (f32[64,1024]{1,0:T(8,128)S(1)}, f32[64,1024]{1,0:T(8,128)S(1)}, u32[]{:S(2)}, u32[]{:S(2)}) collective-permute-start(f32[64,1024]{1,0:T(8,128)S(1)} %get-tuple-element.56), channel_id=1, source_target_pairs={{0,4},{1,5},{2,6},{3,7},{4,0},{5,1},{6,2},{7,3},{8,12},{9,13},{10,... | collective-permute-start | bytes 786440 | tf_op jit(solution)/shard_map/ppermute | solution.py:283
  14.8 0.7 collective-permute-start.2
  15.5 2.6 %collective-permute-start.3 = (f32[64,1024]{1,0:T(8,128)S(1)}, f32[64,1024]{1,0:T(8,128)S(1)}, u32[]{:S(2)}, u32[]{:S(2)}) collective-permute-start(f32[64,1024]{1,0:T(8,128)S(1)} %get-tuple-element.58), channel_id=1, source_target_pairs={{0,6},{1,7},{2,0},{3,1},{4,2},{5,3},{6,4},{7,5},{8,14},{9,15},{10,... | collective-permute-start | bytes 786440 | tf_op jit(solution)/shard_map/ppermute | solution.py:283
  18.0 8.8 %layer.1 = (f32[4,352,128]{2,1,0:T(8,128)S(1)}, f32[4,352,128]{2,1,0:T(8,128)S(1)}, f32[4,288,128]{2,1,0:T(8,128)S(1)}, f32[4,288,128]{2,1,0:T(8,128)S(1)}, f32[4,384,256]{2,1,0:T(8,128)S(1)}) custom-call(s32[4]{0:T(128)S(1)} %pad_add_fusion.idx, bf16[1024,3584]{1,0:T(8,128)(2,1)S(1)} %get-tuple-element.53.a, bf16[3584,1024]{1,0:T(8,128)(2,1)S(1)} %copy-done), custom_call_target="tpu_custom_call" | custom-call | tf_op jit(solution)/shard_map/layer/pallas_call | solution.py:187
  26.8 0.5 collective-permute-done.2
  27.4 0.4 collective-permute-done.3
  27.8 2.0 %collective-permute-start.4 = (f32[64,1024]{1,0:T(8,128)S(1)}, f32[64,1024]{1,0:T(8,128)S(1)}, u32[]{:S(2)}, u32[]{:S(2)}) collective-permute-start(f32[64,1024]{1,0:T(8,128)S(1)} %add_add_fusion), channel_id=1, source_target_pairs={{0,1},{1,0},{2,3},{3,2},{4,5},{5,4},{6,7},{7,6},{8,9},{9,8},{10,11... | collective-permute-start | bytes 786440 | tf_op jit(solution)/shard_map/ppermute | solution.py:320
  29.8 6.1 %collective-permute-done.4 = f32[64,1024]{1,0:T(8,128)S(1)} collective-permute-done((f32[64,1024]{1,0:T(8,128)S(1)}, f32[64,1024]{1,0:T(8,128)S(1)}, u32[]{:S(2)}, u32[]{:S(2)}) %collective-permute-start.4) | collective-permute-done | bytes 262176 | tf_op jit(solution)/shard_map/ppermute | solution.py:320
  36.1 0.9 collective-permute-start.10
  37.0 1.0 collective-permute-start.11
  38.0 1.6 %collective-permute-start.9 = (f32[64,1024]{1,0:T(8,128)S(1)}, f32[64,1024]{1,0:T(8,128)S(1)}, u32[]{:S(2)}, u32[]{:S(2)}) collective-permute-start(f32[64,1024]{1,0:T(8,128)S(1)} %add.70), channel_id=1, source_target_pairs={{0,2},{1,3},{2,4},{3,5},{4,6},{5,7},{6,0},{7,1},{8,10},{9,11},{10,... | collective-permute-start | bytes 786440 | tf_op jit(solution)/shard_map/ppermute | solution.py:326
  39.6 2.9 %collective-permute-start.8 = (f32[64,1024]{1,0:T(8,128)S(1)}, f32[64,1024]{1,0:T(8,128)S(1)}, u32[]{:S(2)}, u32[]{:S(2)}) collective-permute-start(f32[64,1024]{1,0:T(8,128)S(1)} %add.70), channel_id=1, source_target_pairs={{0,4},{1,5},{2,6},{3,7},{4,0},{5,1},{6,2},{7,3},{8,12},{9,13},{10,... | collective-permute-start | bytes 786440 | tf_op jit(solution)/shard_map/ppermute | solution.py:326
  42.5 0.2 collective-permute-start.7
  42.7 4.6 %collective-permute-done.9 = f32[64,1024]{1,0:T(8,128)S(1)} collective-permute-done((f32[64,1024]{1,0:T(8,128)S(1)}, f32[64,1024]{1,0:T(8,128)S(1)}, u32[]{:S(2)}, u32[]{:S(2)}) %collective-permute-start.9) | collective-permute-done | bytes 262176 | tf_op jit(solution)/shard_map/ppermute | solution.py:326
  47.3 6.3 %collective-permute-done.8 = f32[64,1024]{1,0:T(8,128)S(1)} collective-permute-done((f32[64,1024]{1,0:T(8,128)S(1)}, f32[64,1024]{1,0:T(8,128)S(1)}, u32[]{:S(2)}, u32[]{:S(2)}) %collective-permute-start.8) | collective-permute-done | bytes 262176 | tf_op jit(solution)/shard_map/ppermute | solution.py:326
  53.6 0.1 pad_maximum_fusion.mine
  53.8 1.5 %collective-permute-start.14 = (f32[4,288,128]{2,1,0:T(8,128)S(1)}, f32[4,288,128]{2,1,0:T(8,128)S(1)}, u32[]{:S(2)}, u32[]{:S(2)}) collective-permute-start(f32[4,288,128]{2,1,0:T(8,128)S(1)} %get-tuple-element.74), channel_id=1, source_target_pairs={{0,1},{1,0},{2,3},{3,2},{4,5},{5,4},{6,7},{7,6},{8,9},{9,8},{10,11... | collective-permute-start | bytes 1769480 | tf_op jit(solution)/shard_map/ppermute | solution.py:330
  55.3 0.1 slice_bitcast_fusion.1
  55.4 2.3 %collective-permute-start.19 = (f32[384,256]{1,0:T(8,128)S(1)}, f32[384,256]{1,0:T(8,128)S(1)}, u32[]{:S(2)}, u32[]{:S(2)}) collective-permute-start(f32[384,256]{1,0:T(8,128)S(1)} %get-tuple-element.94), channel_id=1, source_target_pairs={{0,4},{1,5},{2,6},{3,7},{4,0},{5,1},{6,2},{7,3},{8,12},{9,13},{10,... | collective-permute-start | bytes 1179656 | tf_op jit(solution)/shard_map/ppermute | solution.py:283
  57.7 2.4 %collective-permute-start.18 = (f32[384,256]{1,0:T(8,128)S(1)}, f32[384,256]{1,0:T(8,128)S(1)}, u32[]{:S(2)}, u32[]{:S(2)}) collective-permute-start(f32[384,256]{1,0:T(8,128)S(1)} %get-tuple-element.96), channel_id=1, source_target_pairs={{0,6},{1,7},{2,0},{3,1},{4,2},{5,3},{6,4},{7,5},{8,14},{9,15},{10,... | collective-permute-start | bytes 1179656 | tf_op jit(solution)/shard_map/ppermute | solution.py:283
  60.1 2.7 %scores.1 = (f32[8,1024]{1,0:T(8,128)S(1)}, f32[8,1024]{1,0:T(8,128)S(1)}) custom-call(s32[4]{0:T(128)S(1)} %pad_add_fusion.idx, bf16[1024,128]{1,0:T(8,128)(2,1)} %og.1, bf16[2048,128]{1,0:T(8,128)(2,1)} %bitcast.37, f32[2048,128]{1,0:T(8,128)S(1)} %collective-permute-done.5.a1.b1, f32[2048,128]{1,0:T(8,128)S(1)} %collective-permute-done.5.a1.b1, ...), custom_call_target="tpu_custom_call" | custom-call | tf_op jit(solution)/shard_map/scores/pallas_call | solution.py:267
  62.9 1.2 %collective-permute-done.13 = f32[8,1024]{1,0:T(8,128)S(1)} collective-permute-done((f32[8,1024]{1,0:T(8,128)S(1)}, f32[8,1024]{1,0:T(8,128)S(1)}, u32[]{:S(2)}, u32[]{:S(2)}) %collective-permute-start.13) | collective-permute-done | bytes 32800 | tf_op jit(solution)/shard_map/ppermute | solution.py:334
  64.1 5.5 %collective-permute-done.14 = f32[4,288,128]{2,1,0:T(8,128)S(1)} collective-permute-done((f32[4,288,128]{2,1,0:T(8,128)S(1)}, f32[4,288,128]{2,1,0:T(8,128)S(1)}, u32[]{:S(2)}, u32[]{:S(2)}) %collective-permute-start.14) | collective-permute-done | bytes 589856 | tf_op jit(solution)/shard_map/ppermute | solution.py:330
  69.6 1.5 %collective-permute-start.15 = (f32[8,1024]{1,0:T(8,128)S(1)}, f32[8,1024]{1,0:T(8,128)S(1)}, u32[]{:S(2)}, u32[]{:S(2)}) collective-permute-start(f32[8,1024]{1,0:T(8,128)S(1)} %add.71), channel_id=1, source_target_pairs={{0,1},{1,0},{2,3},{3,2},{4,5},{5,4},{6,7},{7,6},{8,9},{9,8},{10,11... | collective-permute-start | bytes 98312 | tf_op jit(solution)/shard_map/ppermute | solution.py:336
  71.0 2.5 %collective-permute-done.15 = f32[8,1024]{1,0:T(8,128)S(1)} collective-permute-done((f32[8,1024]{1,0:T(8,128)S(1)}, f32[8,1024]{1,0:T(8,128)S(1)}, u32[]{:S(2)}, u32[]{:S(2)}) %collective-permute-start.15) | collective-permute-done | bytes 32800 | tf_op jit(solution)/shard_map/ppermute | solution.py:336
  73.5 1.9 %collective-permute-start.16 = (f32[8,1024]{1,0:T(8,128)S(1)}, f32[8,1024]{1,0:T(8,128)S(1)}, u32[]{:S(2)}, u32[]{:S(2)}) collective-permute-start(f32[8,1024]{1,0:T(8,128)S(1)} %add.72), channel_id=1, source_target_pairs={{0,4},{1,5},{2,6},{3,7},{4,0},{5,1},{6,2},{7,3},{8,12},{9,13},{10,... | collective-permute-start | bytes 98312 | tf_op jit(solution)/shard_map/ppermute | solution.py:337
  75.4 3.5 %collective-permute-done.16 = f32[8,1024]{1,0:T(8,128)S(1)} collective-permute-done((f32[8,1024]{1,0:T(8,128)S(1)}, f32[8,1024]{1,0:T(8,128)S(1)}, u32[]{:S(2)}, u32[]{:S(2)}) %collective-permute-start.16) | collective-permute-done | bytes 32800 | tf_op jit(solution)/shard_map/ppermute | solution.py:337
  79.0 1.8 %collective-permute-start.20 = (f32[8,1024]{1,0:T(8,128)S(1)}, f32[8,1024]{1,0:T(8,128)S(1)}, u32[]{:S(2)}, u32[]{:S(2)}) collective-permute-start(f32[8,1024]{1,0:T(8,128)S(1)} %add.73), channel_id=1, source_target_pairs={{0,2},{1,3},{2,0},{3,1},{4,6},{5,7},{6,4},{7,5},{8,10},{9,11},{10,... | collective-permute-start | bytes 98312 | tf_op jit(solution)/shard_map/ppermute | solution.py:341
  80.7 0.6 halves.1
  81.3 1.6 %collective-permute-start.25 = (f32[384,128]{1,0:T(8,128)S(1)}, f32[384,128]{1,0:T(8,128)S(1)}, u32[]{:S(2)}, u32[]{:S(2)}) collective-permute-start(f32[384,128]{1,0:T(8,128)S(1)} %get-tuple-element.92), channel_id=1, source_target_pairs={{0,1},{1,0},{2,3},{3,2},{4,5},{5,4},{6,7},{7,6},{8,9},{9,8},{10,11... | collective-permute-start | bytes 589832 | tf_op jit(solution)/shard_map/ppermute | solution.py:340
  83.0 0.1 add.75
  83.1 0.1 add.76
  83.3 3.4 %collective-permute-start.24 = (f32[640,128]{1,0:T(8,128)S(1)}, f32[640,128]{1,0:T(8,128)S(1)}, u32[]{:S(2)}, u32[]{:S(2)}) collective-permute-start(f32[640,128]{1,0:T(8,128)S(1)} %get-tuple-element.98), channel_id=1, source_target_pairs={{0,4},{1,5},{2,6},{3,7},{4,0},{5,1},{6,2},{7,3},{8,12},{9,13},{10,... | collective-permute-start | bytes 983048 | tf_op jit(solution)/shard_map/ppermute | solution.py:283
  86.7 1.1 %collective-permute-start.22 = (f32[640,128]{1,0:T(8,128)S(1)}, f32[640,128]{1,0:T(8,128)S(1)}, u32[]{:S(2)}, u32[]{:S(2)}) collective-permute-start(f32[640,128]{1,0:T(8,128)S(1)} %get-tuple-element.99), channel_id=1, source_target_pairs={{0,2},{1,3},{2,4},{3,5},{4,6},{5,7},{6,0},{7,1},{8,10},{9,11},{10,... | collective-permute-start | bytes 983048 | tf_op jit(solution)/shard_map/ppermute | solution.py:283
  87.8 2.1 %collective-permute-start.23 = (f32[640,128]{1,0:T(8,128)S(1)}, f32[640,128]{1,0:T(8,128)S(1)}, u32[]{:S(2)}, u32[]{:S(2)}) collective-permute-start(f32[640,128]{1,0:T(8,128)S(1)} %get-tuple-element.100), channel_id=1, source_target_pairs={{0,6},{1,7},{2,0},{3,1},{4,2},{5,3},{6,4},{7,5},{8,14},{9,15},{10,... | collective-permute-start | bytes 983048 | tf_op jit(solution)/shard_map/ppermute | solution.py:283
  89.9 6.4 %collective-permute-start.21 = (f32[8,128]{1,0:T(8,128)S(1)}, f32[8,128]{1,0:T(8,128)S(1)}, u32[]{:S(2)}, u32[]{:S(2)}) collective-permute-start(f32[8,128]{1,0:T(8,128)S(1)} %bitcast_reduce_fusion), channel_id=1, source_target_pairs={{0,128},{64,192},{128,0},{192,64},{1,129},{65,193},{129,1},{193,65... | collective-permute-start | bytes 12296 | tf_op jit(solution)/shard_map/ppermute | solution.py:347
  96.3 1.6 %collective-permute-done.21 = f32[8,128]{1,0:T(8,128)S(1)} collective-permute-done((f32[8,128]{1,0:T(8,128)S(1)}, f32[8,128]{1,0:T(8,128)S(1)}, u32[]{:S(2)}, u32[]{:S(2)}) %collective-permute-start.21) | collective-permute-done | bytes 4128 | tf_op jit(solution)/shard_map/ppermute | solution.py:347
  98.0 1.1 %collective-permute-done.22 = f32[640,128]{1,0:T(8,128)S(1)} collective-permute-done((f32[640,128]{1,0:T(8,128)S(1)}, f32[640,128]{1,0:T(8,128)S(1)}, u32[]{:S(2)}, u32[]{:S(2)}) %collective-permute-start.22) | collective-permute-done | bytes 327712 | tf_op jit(solution)/shard_map/ppermute | solution.py:283
  99.0 0.1 collective-permute-done.23
  99.2 3.2 %collective-permute-start.26 = (f32[8,128]{1,0:T(8,128)S(1)}, f32[8,128]{1,0:T(8,128)S(1)}, u32[]{:S(2)}, u32[]{:S(2)}) collective-permute-start(f32[8,128]{1,0:T(8,128)S(1)} %add.77), channel_id=1, source_target_pairs={{0,64},{64,0},{128,192},{192,128},{1,65},{65,1},{129,193},{193,129... | collective-permute-start | bytes 12296 | tf_op jit(solution)/shard_map/ppermute | solution.py:349
  102.5 0.7 pad_maximum_fusion.2
  103.2 0.8 collective-permute-done.26
  104.0 0.1 add_reduce_fusion
  104.1 0.7 divide_bitcast_fusion
  (34 shorter events, 0.8 us)
Async XLA Ops:
  5.2 5.1 %collective-permute-start = (f32[1536,128]{1,0:T(8,128)S(1)}, f32[1536,128]{1,0:T(8,128)S(1)}, u32[]{:S(2)}, u32[]{:S(2)}) collective-permute-start(f32[1536,128]{1,0:T(8,128)S(1)} %get-tuple-element.48), channel_id=1, source_target_pairs={{0,8},{8,0},{16,24},{24,16},{32,40},{40,32},{48,56},{56,48},{1,9},... | collective-permute-start | bytes 2359304 | tf_op jit(solution)/shard_map/ppermute | solution.py:306
  5.3 30.7 %collective-permute-start.5 = (f32[2048,128]{1,0:T(8,128)S(1)}, f32[2048,128]{1,0:T(8,128)S(1)}, u32[]{:S(2)}, u32[]{:S(2)}) collective-permute-start(f32[2048,128]{1,0:T(8,128)S(1)} %get-tuple-element.49), channel_id=1, source_target_pairs={{0,16},{8,56},{16,32},{24,8},{32,48},{40,24},{48,0},{56,40},{1,17}... | collective-permute-start | bytes 3145736 | tf_op jit(solution)/shard_map/ppermute | solution.py:308
  6.8 11.2 %copy-start = (bf16[3584,1024]{1,0:T(8,128)(2,1)S(1)}, bf16[3584,1024]{1,0:T(8,128)(2,1)}, u32[]{:S(2)}) copy-start(bf16[3584,1024]{1,0:T(8,128)(2,1)} %w.1) | copy-start | bytes 22020100
  10.3 25.7 %collective-permute-start.6 = (f32[1536,128]{1,0:T(8,128)S(1)}, f32[1536,128]{1,0:T(8,128)S(1)}, u32[]{:S(2)}, u32[]{:S(2)}) collective-permute-start(f32[1536,128]{1,0:T(8,128)S(1)} %collective-permute-done), channel_id=1, source_target_pairs={{0,16},{8,56},{16,32},{24,8},{32,48},{40,24},{48,0},{56,40},{1,17}... | collective-permute-start | bytes 2359304 | tf_op jit(solution)/shard_map/ppermute | solution.py:313
  11.6 15.3 %collective-permute-start.1 = (f32[64,1024]{1,0:T(8,128)S(1)}, f32[64,1024]{1,0:T(8,128)S(1)}, u32[]{:S(2)}, u32[]{:S(2)}) collective-permute-start(f32[64,1024]{1,0:T(8,128)S(1)} %get-tuple-element.56), channel_id=1, source_target_pairs={{0,4},{1,5},{2,6},{3,7},{4,0},{5,1},{6,2},{7,3},{8,12},{9,13},{10,... | collective-permute-start | bytes 786440 | tf_op jit(solution)/shard_map/ppermute | solution.py:283
  14.8 12.6 %collective-permute-start.2 = (f32[64,1024]{1,0:T(8,128)S(1)}, f32[64,1024]{1,0:T(8,128)S(1)}, u32[]{:S(2)}, u32[]{:S(2)}) collective-permute-start(f32[64,1024]{1,0:T(8,128)S(1)} %get-tuple-element.57), channel_id=1, source_target_pairs={{0,2},{1,3},{2,4},{3,5},{4,6},{5,7},{6,0},{7,1},{8,10},{9,11},{10,... | collective-permute-start | bytes 786440 | tf_op jit(solution)/shard_map/ppermute | solution.py:283
  15.5 12.3 %collective-permute-start.3 = (f32[64,1024]{1,0:T(8,128)S(1)}, f32[64,1024]{1,0:T(8,128)S(1)}, u32[]{:S(2)}, u32[]{:S(2)}) collective-permute-start(f32[64,1024]{1,0:T(8,128)S(1)} %get-tuple-element.58), channel_id=1, source_target_pairs={{0,6},{1,7},{2,0},{3,1},{4,2},{5,3},{6,4},{7,5},{8,14},{9,15},{10,... | collective-permute-start | bytes 786440 | tf_op jit(solution)/shard_map/ppermute | solution.py:283
  27.8 8.1 %collective-permute-start.4 = (f32[64,1024]{1,0:T(8,128)S(1)}, f32[64,1024]{1,0:T(8,128)S(1)}, u32[]{:S(2)}, u32[]{:S(2)}) collective-permute-start(f32[64,1024]{1,0:T(8,128)S(1)} %add_add_fusion), channel_id=1, source_target_pairs={{0,1},{1,0},{2,3},{3,2},{4,5},{5,4},{6,7},{7,6},{8,9},{9,8},{10,11... | collective-permute-start | bytes 786440 | tf_op jit(solution)/shard_map/ppermute | solution.py:320
  36.1 17.6 %collective-permute-start.10 = (f32[1536,128]{1,0:T(8,128)S(1)}, f32[1536,128]{1,0:T(8,128)S(1)}, u32[]{:S(2)}, u32[]{:S(2)}) collective-permute-start(f32[1536,128]{1,0:T(8,128)S(1)} %slice.27), channel_id=1, source_target_pairs={{0,16},{8,56},{16,32},{24,8},{32,48},{40,24},{48,0},{56,40},{1,17}... | collective-permute-start | bytes 2359304 | tf_op jit(solution)/shard_map/ppermute | solution.py:324
  37.0 16.8 %collective-permute-start.11 = (f32[4,352,128]{2,1,0:T(8,128)S(1)}, f32[4,352,128]{2,1,0:T(8,128)S(1)}, u32[]{:S(2)}, u32[]{:S(2)}) collective-permute-start(f32[4,352,128]{2,1,0:T(8,128)S(1)} %get-tuple-element.67), channel_id=1, source_target_pairs={{0,1},{1,0},{2,3},{3,2},{4,5},{5,4},{6,7},{7,6},{8,9},{9,8},{10,11... | collective-permute-start | bytes 2162696 | tf_op jit(solution)/shard_map/ppermute | solution.py:323
  38.0 9.3 %collective-permute-start.9 = (f32[64,1024]{1,0:T(8,128)S(1)}, f32[64,1024]{1,0:T(8,128)S(1)}, u32[]{:S(2)}, u32[]{:S(2)}) collective-permute-start(f32[64,1024]{1,0:T(8,128)S(1)} %add.70), channel_id=1, source_target_pairs={{0,2},{1,3},{2,4},{3,5},{4,6},{5,7},{6,0},{7,1},{8,10},{9,11},{10,... | collective-permute-start | bytes 786440 | tf_op jit(solution)/shard_map/ppermute | solution.py:326
  39.6 14.0 %collective-permute-start.8 = (f32[64,1024]{1,0:T(8,128)S(1)}, f32[64,1024]{1,0:T(8,128)S(1)}, u32[]{:S(2)}, u32[]{:S(2)}) collective-permute-start(f32[64,1024]{1,0:T(8,128)S(1)} %add.70), channel_id=1, source_target_pairs={{0,4},{1,5},{2,6},{3,7},{4,0},{5,1},{6,2},{7,3},{8,12},{9,13},{10,... | collective-permute-start | bytes 786440 | tf_op jit(solution)/shard_map/ppermute | solution.py:326
  42.5 11.2 %collective-permute-start.7 = (f32[64,1024]{1,0:T(8,128)S(1)}, f32[64,1024]{1,0:T(8,128)S(1)}, u32[]{:S(2)}, u32[]{:S(2)}) collective-permute-start(f32[64,1024]{1,0:T(8,128)S(1)} %add.70), channel_id=1, source_target_pairs={{0,6},{1,7},{2,0},{3,1},{4,2},{5,3},{6,4},{7,5},{8,14},{9,15},{10,... | collective-permute-start | bytes 786440 | tf_op jit(solution)/shard_map/ppermute | solution.py:326
  53.7 6.4 %collective-permute-start.12 = (f32[4,64,1024]{2,1,0:T(8,128)S(1)}, f32[4,64,1024]{2,1,0:T(8,128)S(1)}, u32[]{:S(2)}, u32[]{:S(2)}) collective-permute-start(f32[4,64,1024]{2,1,0:T(8,128)S(1)} %pad_maximum_fusion.mine), channel_id=1, source_target_pairs={{0,8},{8,0},{16,24},{24,16},{32,40},{40,32},{48,56},{56,48},{1,9},... | collective-permute-start | bytes 3145736 | tf_op jit(solution)/shard_map/ppermute | solution.py:329
  53.8 15.7 %collective-permute-start.14 = (f32[4,288,128]{2,1,0:T(8,128)S(1)}, f32[4,288,128]{2,1,0:T(8,128)S(1)}, u32[]{:S(2)}, u32[]{:S(2)}) collective-permute-start(f32[4,288,128]{2,1,0:T(8,128)S(1)} %get-tuple-element.74), channel_id=1, source_target_pairs={{0,1},{1,0},{2,3},{3,2},{4,5},{5,4},{6,7},{7,6},{8,9},{9,8},{10,11... | collective-permute-start | bytes 1769480 | tf_op jit(solution)/shard_map/ppermute | solution.py:330
  55.4 23.5 %collective-permute-start.19 = (f32[384,256]{1,0:T(8,128)S(1)}, f32[384,256]{1,0:T(8,128)S(1)}, u32[]{:S(2)}, u32[]{:S(2)}) collective-permute-start(f32[384,256]{1,0:T(8,128)S(1)} %get-tuple-element.94), channel_id=1, source_target_pairs={{0,4},{1,5},{2,6},{3,7},{4,0},{5,1},{6,2},{7,3},{8,12},{9,13},{10,... | collective-permute-start | bytes 1179656 | tf_op jit(solution)/shard_map/ppermute | solution.py:283
  57.7 21.2 %collective-permute-start.18 = (f32[384,256]{1,0:T(8,128)S(1)}, f32[384,256]{1,0:T(8,128)S(1)}, u32[]{:S(2)}, u32[]{:S(2)}) collective-permute-start(f32[384,256]{1,0:T(8,128)S(1)} %get-tuple-element.96), channel_id=1, source_target_pairs={{0,6},{1,7},{2,0},{3,1},{4,2},{5,3},{6,4},{7,5},{8,14},{9,15},{10,... | collective-permute-start | bytes 1179656 | tf_op jit(solution)/shard_map/ppermute | solution.py:283
  60.1 18.8 %collective-permute-start.17 = (f32[384,256]{1,0:T(8,128)S(1)}, f32[384,256]{1,0:T(8,128)S(1)}, u32[]{:S(2)}, u32[]{:S(2)}) collective-permute-start(f32[384,256]{1,0:T(8,128)S(1)} %get-tuple-element.97), channel_id=1, source_target_pairs={{0,2},{1,3},{2,4},{3,5},{4,6},{5,7},{6,0},{7,1},{8,10},{9,11},{10,... | collective-permute-start | bytes 1179656 | tf_op jit(solution)/shard_map/ppermute | solution.py:283
  62.8 1.3 %collective-permute-start.13 = (f32[8,1024]{1,0:T(8,128)S(1)}, f32[8,1024]{1,0:T(8,128)S(1)}, u32[]{:S(2)}, u32[]{:S(2)}) collective-permute-start(f32[8,1024]{1,0:T(8,128)S(1)} %get-tuple-element.73), channel_id=1, source_target_pairs={{0,8},{8,0},{16,24},{24,16},{32,40},{40,32},{48,56},{56,48},{1,9},... | collective-permute-start | bytes 98312 | tf_op jit(solution)/shard_map/ppermute | solution.py:334
  69.6 3.9 %collective-permute-start.15 = (f32[8,1024]{1,0:T(8,128)S(1)}, f32[8,1024]{1,0:T(8,128)S(1)}, u32[]{:S(2)}, u32[]{:S(2)}) collective-permute-start(f32[8,1024]{1,0:T(8,128)S(1)} %add.71), channel_id=1, source_target_pairs={{0,1},{1,0},{2,3},{3,2},{4,5},{5,4},{6,7},{7,6},{8,9},{9,8},{10,11... | collective-permute-start | bytes 98312 | tf_op jit(solution)/shard_map/ppermute | solution.py:336
  73.5 5.4 %collective-permute-start.16 = (f32[8,1024]{1,0:T(8,128)S(1)}, f32[8,1024]{1,0:T(8,128)S(1)}, u32[]{:S(2)}, u32[]{:S(2)}) collective-permute-start(f32[8,1024]{1,0:T(8,128)S(1)} %add.72), channel_id=1, source_target_pairs={{0,4},{1,5},{2,6},{3,7},{4,0},{5,1},{6,2},{7,3},{8,12},{9,13},{10,... | collective-permute-start | bytes 98312 | tf_op jit(solution)/shard_map/ppermute | solution.py:337
  79.0 4.0 %collective-permute-start.20 = (f32[8,1024]{1,0:T(8,128)S(1)}, f32[8,1024]{1,0:T(8,128)S(1)}, u32[]{:S(2)}, u32[]{:S(2)}) collective-permute-start(f32[8,1024]{1,0:T(8,128)S(1)} %add.73), channel_id=1, source_target_pairs={{0,2},{1,3},{2,0},{3,1},{4,6},{5,7},{6,4},{7,5},{8,10},{9,11},{10,... | collective-permute-start | bytes 98312 | tf_op jit(solution)/shard_map/ppermute | solution.py:341
  81.3 16.6 %collective-permute-start.25 = (f32[384,128]{1,0:T(8,128)S(1)}, f32[384,128]{1,0:T(8,128)S(1)}, u32[]{:S(2)}, u32[]{:S(2)}) collective-permute-start(f32[384,128]{1,0:T(8,128)S(1)} %get-tuple-element.92), channel_id=1, source_target_pairs={{0,1},{1,0},{2,3},{3,2},{4,5},{5,4},{6,7},{7,6},{8,9},{9,8},{10,11... | collective-permute-start | bytes 589832 | tf_op jit(solution)/shard_map/ppermute | solution.py:340
  83.3 14.7 %collective-permute-start.24 = (f32[640,128]{1,0:T(8,128)S(1)}, f32[640,128]{1,0:T(8,128)S(1)}, u32[]{:S(2)}, u32[]{:S(2)}) collective-permute-start(f32[640,128]{1,0:T(8,128)S(1)} %get-tuple-element.98), channel_id=1, source_target_pairs={{0,4},{1,5},{2,6},{3,7},{4,0},{5,1},{6,2},{7,3},{8,12},{9,13},{10,... | collective-permute-start | bytes 983048 | tf_op jit(solution)/shard_map/ppermute | solution.py:283
  86.7 12.4 %collective-permute-start.22 = (f32[640,128]{1,0:T(8,128)S(1)}, f32[640,128]{1,0:T(8,128)S(1)}, u32[]{:S(2)}, u32[]{:S(2)}) collective-permute-start(f32[640,128]{1,0:T(8,128)S(1)} %get-tuple-element.99), channel_id=1, source_target_pairs={{0,2},{1,3},{2,4},{3,5},{4,6},{5,7},{6,0},{7,1},{8,10},{9,11},{10,... | collective-permute-start | bytes 983048 | tf_op jit(solution)/shard_map/ppermute | solution.py:283
  87.8 11.4 %collective-permute-start.23 = (f32[640,128]{1,0:T(8,128)S(1)}, f32[640,128]{1,0:T(8,128)S(1)}, u32[]{:S(2)}, u32[]{:S(2)}) collective-permute-start(f32[640,128]{1,0:T(8,128)S(1)} %get-tuple-element.100), channel_id=1, source_target_pairs={{0,6},{1,7},{2,0},{3,1},{4,2},{5,3},{6,4},{7,5},{8,14},{9,15},{10,... | collective-permute-start | bytes 983048 | tf_op jit(solution)/shard_map/ppermute | solution.py:283
  89.9 8.0 %collective-permute-start.21 = (f32[8,128]{1,0:T(8,128)S(1)}, f32[8,128]{1,0:T(8,128)S(1)}, u32[]{:S(2)}, u32[]{:S(2)}) collective-permute-start(f32[8,128]{1,0:T(8,128)S(1)} %bitcast_reduce_fusion), channel_id=1, source_target_pairs={{0,128},{64,192},{128,0},{192,64},{1,129},{65,193},{129,1},{193,65... | collective-permute-start | bytes 12296 | tf_op jit(solution)/shard_map/ppermute | solution.py:347
  99.2 4.8 %collective-permute-start.26 = (f32[8,128]{1,0:T(8,128)S(1)}, f32[8,128]{1,0:T(8,128)S(1)}, u32[]{:S(2)}, u32[]{:S(2)}) collective-permute-start(f32[8,128]{1,0:T(8,128)S(1)} %add.77), channel_id=1, source_target_pairs={{0,64},{64,0},{128,192},{192,128},{1,65},{65,1},{129,193},{193,129... | collective-permute-start | bytes 12296 | tf_op jit(solution)/shard_map/ppermute | solution.py:349

commit v6 on v5

--- a/solution.py
+++ b/solution.py
@@ -314,7 +314,7 @@
     own = sum_y(pieces[0], send_y(pieces))
 
     at = after(idx, pieces[0])
-    keep0, send0, keep1, send1, parts = layer(at, activations, down_weight, (352, 288))
+    keep0, send0, keep1, send1, parts = layer(at, activations, down_weight, (352, 304))
 
     own, send0 = lax.optimization_barrier((own, send0))
     own = own + lax.ppermute(own, "tensor", z_swap())
@@ -332,10 +332,9 @@
 
     raw, send = scores(idx, output_grads, gf, (near0, near1), far, mine, other, ranks)
     raw = raw + swap(send)
-    raw, got1 = lax.optimization_barrier((raw, got1))
     raw = raw + lax.ppermute(raw, "tensor", z_swap())
     raw = raw + lax.ppermute(raw, "tensor", y_shift(2))
-    raw, got = lax.optimization_barrier((raw, got))
+    raw, got, got1 = lax.optimization_barrier((raw, got, got1))
     keep, send = halves(idx, [parts[0], *got])
     out1 = (keep + lax.ppermute(send, "tensor", z_swap())).astype(jnp.bfloat16)
     raw = raw + lax.ppermute(raw, "tensor", y_pair())

time: 105 us -> 105 us (level)
  starting transfers between devices: 47.4 us -> 44.8 us
  waiting for transfers between devices: 34.2 us -> 36.6 us
    ppermute x1, waiting for transfers between devices: 5.49 us -> 0.01 us  [body(): got1 = lax.ppermute(send1, 'tensor', z_swap())]
    ppermute x1, waiting for transfers between devices: 2.45 us -> 6.42 us  [body(): raw = raw + lax.ppermute(raw, 'tensor', z_swap())]
    ppermute x9, waiting for transfers between devices: 2.13 us -> 4.83 us  [send_y(): return [lax.ppermute(parts[j], 'tensor', y_shift(j)) for j in (1, 3, 2)]]
  transfers between devices with their start and end apart: 27 -> 27, of which waited for: 13 -> 14; matrix products, arithmetic and copies ran while one was open for 1% -> 1% of each run, Pallas kernels for 15% -> 15%
where the time goes in v6:
time: 105 us
  starting transfers between devices  44.8 us (43%)
  waiting for transfers between devices  36.6 us (35%)
  Pallas kernels  20 us (19%)
  other arithmetic  2.25 us (2%)
    ppermute x9, starting transfers between devices, send_y(): return [lax.ppermute(parts[j], 'tensor', y_shift(j)) for j in (1, 3, 2)]  17.1 us
    ppermute x3, waiting for transfers between devices, body(): lax.ppermute(own, 'tensor', y_shift(-j))  10.9 us
    pallas_call x1, Pallas kernels, layer(): pl.pallas_call(functools.partial(layer_kernel, blocks=blocks), grid_spec=...  8.81 us
    ppermute x1, waiting for transfers between devices, body(): raw = raw + lax.ppermute(raw, 'tensor', z_swap())  6.42 us
    ppermute x1, starting transfers between devices, body(): square = square + lax.ppermute(square, 'dp', dp_shift(2))  6.31 us
    ppermute x1, waiting for transfers between devices, body(): own = own + lax.ppermute(own, 'tensor', z_swap())  6.15 us
    ppermute x9, waiting for transfers between devices, send_y(): return [lax.ppermute(parts[j], 'tensor', y_shift(j)) for j in (1, 3, 2)]  4.83 us
    ppermute x3, starting transfers between devices, body(): lax.ppermute(own, 'tensor', y_shift(-j))  4.66 us
  transfers between devices with their start and end apart: 27, of which 14 were waited for; matrix products, arithmetic and copies ran while one was open for 1% of the time, Pallas kernels for 15%

profile of v6, /device:TPU:2, one launch (start us, length us, event | category | flops | bytes accessed | tf_op | source)
XLA Modules:
  0.0 104.6 jit_solution(7799784755307839808)
XLA Ops:
  0.7 4.4 %pack.1 = (f32[2048,128]{1,0:T(8,128)S(1)}, f32[1536,128]{1,0:T(8,128)S(1)}, bf16[1024,3584]{1,0:T(8,128)(2,1)S(1)}, bf16[256,3584]{1,0:T(8,128)(2,1)S(1)}, f32[8,32]{1,0:T(8,128)S(1)}) custom-call(s32[4]{0:T(128)S(1)} %pad_add_fusion.idx, bf16[1024,128]{1,0:T(8,128)(2,1)} %og.1, bf16[2048,128]{1,0:T(8,128)(2,1)} %bitcast.36, bf16[1024,3584]{1,0:T(8,128)(2,1)} %refs_0_.1, ...), custom_call_target="tpu_custom_call" | custom-call | bytes 41943040 | tf_op jit(solution)/shard_map/pack/pallas_call | solution.py:93
  5.3 1.6 %collective-permute-start.5 = (f32[2048,128]{1,0:T(8,128)S(1)}, f32[2048,128]{1,0:T(8,128)S(1)}, u32[]{:S(2)}, u32[]{:S(2)}) collective-permute-start(f32[2048,128]{1,0:T(8,128)S(1)} %get-tuple-element.48), channel_id=1, source_target_pairs={{0,16},{8,56},{16,32},{24,8},{32,48},{40,24},{48,0},{56,40},{1,17}... | collective-permute-start | bytes 3145736 | tf_op jit(solution)/shard_map/ppermute | solution.py:308
  6.9 3.4 %act.1 = (f32[64,1024]{1,0:T(8,128)S(1)}, f32[64,1024]{1,0:T(8,128)S(1)}, f32[64,1024]{1,0:T(8,128)S(1)}, f32[64,1024]{1,0:T(8,128)S(1)}) custom-call(s32[4]{0:T(128)S(1)} %pad_add_fusion.idx, f32[8,32]{1,0:T(8,128)S(1)} %get-tuple-element.50.weight, bf16[256,3584]{1,0:T(8,128)(2,1)S(1)} %get-tuple-element.51.af, bf16[1024,3584]{1,0:T(8,128)(2,1)S(1)} %get-tuple-element.52.a), custom_call_target="tpu_custom_call" | custom-call | bytes 20971520 | tf_op jit(solution)/shard_map/act/pallas_call | solution.py:146
  10.3 1.3 %collective-permute-start.6 = (f32[1536,128]{1,0:T(8,128)S(1)}, f32[1536,128]{1,0:T(8,128)S(1)}, u32[]{:S(2)}, u32[]{:S(2)}) collective-permute-start(f32[1536,128]{1,0:T(8,128)S(1)} %collective-permute-done), channel_id=1, source_target_pairs={{0,16},{8,56},{16,32},{24,8},{32,48},{40,24},{48,0},{56,40},{1,17}... | collective-permute-start | bytes 2359304 | tf_op jit(solution)/shard_map/ppermute | solution.py:313
  11.6 3.2 %collective-permute-start.1 = (f32[64,1024]{1,0:T(8,128)S(1)}, f32[64,1024]{1,0:T(8,128)S(1)}, u32[]{:S(2)}, u32[]{:S(2)}) collective-permute-start(f32[64,1024]{1,0:T(8,128)S(1)} %get-tuple-element.55), channel_id=1, source_target_pairs={{0,4},{1,5},{2,6},{3,7},{4,0},{5,1},{6,2},{7,3},{8,12},{9,13},{10,... | collective-permute-start | bytes 786440 | tf_op jit(solution)/shard_map/ppermute | solution.py:283
  14.8 0.7 collective-permute-start.2
  15.5 2.6 %collective-permute-start.3 = (f32[64,1024]{1,0:T(8,128)S(1)}, f32[64,1024]{1,0:T(8,128)S(1)}, u32[]{:S(2)}, u32[]{:S(2)}) collective-permute-start(f32[64,1024]{1,0:T(8,128)S(1)} %get-tuple-element.57), channel_id=1, source_target_pairs={{0,6},{1,7},{2,0},{3,1},{4,2},{5,3},{6,4},{7,5},{8,14},{9,15},{10,... | collective-permute-start | bytes 786440 | tf_op jit(solution)/shard_map/ppermute | solution.py:283
  18.0 8.8 %layer.1 = (f32[4,352,128]{2,1,0:T(8,128)S(1)}, f32[4,352,128]{2,1,0:T(8,128)S(1)}, f32[4,304,128]{2,1,0:T(8,128)S(1)}, f32[4,304,128]{2,1,0:T(8,128)S(1)}, f32[4,368,256]{2,1,0:T(8,128)S(1)}) custom-call(s32[4]{0:T(128)S(1)} %pad_add_fusion.idx, bf16[1024,3584]{1,0:T(8,128)(2,1)S(1)} %get-tuple-element.52.a, bf16[3584,1024]{1,0:T(8,128)(2,1)S(1)} %copy-done), custom_call_target="tpu_custom_call" | custom-call | tf_op jit(solution)/shard_map/layer/pallas_call | solution.py:187
  26.8 0.5 collective-permute-done.2
  27.4 0.4 collective-permute-done.3
  27.8 2.0 %collective-permute-start.4 = (f32[64,1024]{1,0:T(8,128)S(1)}, f32[64,1024]{1,0:T(8,128)S(1)}, u32[]{:S(2)}, u32[]{:S(2)}) collective-permute-start(f32[64,1024]{1,0:T(8,128)S(1)} %add_add_fusion), channel_id=1, source_target_pairs={{0,1},{1,0},{2,3},{3,2},{4,5},{5,4},{6,7},{7,6},{8,9},{9,8},{10,11... | collective-permute-start | bytes 786440 | tf_op jit(solution)/shard_map/ppermute | solution.py:320
  29.8 6.1 %collective-permute-done.4 = f32[64,1024]{1,0:T(8,128)S(1)} collective-permute-done((f32[64,1024]{1,0:T(8,128)S(1)}, f32[64,1024]{1,0:T(8,128)S(1)}, u32[]{:S(2)}, u32[]{:S(2)}) %collective-permute-start.4) | collective-permute-done | bytes 262176 | tf_op jit(solution)/shard_map/ppermute | solution.py:320
  36.1 0.9 collective-permute-start.10
  37.0 1.0 %collective-permute-start.11 = (f32[4,352,128]{2,1,0:T(8,128)S(1)}, f32[4,352,128]{2,1,0:T(8,128)S(1)}, u32[]{:S(2)}, u32[]{:S(2)}) collective-permute-start(f32[4,352,128]{2,1,0:T(8,128)S(1)} %get-tuple-element.66), channel_id=1, source_target_pairs={{0,1},{1,0},{2,3},{3,2},{4,5},{5,4},{6,7},{7,6},{8,9},{9,8},{10,11... | collective-permute-start | bytes 2162696 | tf_op jit(solution)/shard_map/ppermute | solution.py:323
  38.0 1.6 %collective-permute-start.9 = (f32[64,1024]{1,0:T(8,128)S(1)}, f32[64,1024]{1,0:T(8,128)S(1)}, u32[]{:S(2)}, u32[]{:S(2)}) collective-permute-start(f32[64,1024]{1,0:T(8,128)S(1)} %add.70), channel_id=1, source_target_pairs={{0,2},{1,3},{2,4},{3,5},{4,6},{5,7},{6,0},{7,1},{8,10},{9,11},{10,... | collective-permute-start | bytes 786440 | tf_op jit(solution)/shard_map/ppermute | solution.py:326
  39.6 2.9 %collective-permute-start.8 = (f32[64,1024]{1,0:T(8,128)S(1)}, f32[64,1024]{1,0:T(8,128)S(1)}, u32[]{:S(2)}, u32[]{:S(2)}) collective-permute-start(f32[64,1024]{1,0:T(8,128)S(1)} %add.70), channel_id=1, source_target_pairs={{0,4},{1,5},{2,6},{3,7},{4,0},{5,1},{6,2},{7,3},{8,12},{9,13},{10,... | collective-permute-start | bytes 786440 | tf_op jit(solution)/shard_map/ppermute | solution.py:326
  42.5 0.2 collective-permute-start.7
  42.7 4.6 %collective-permute-done.9 = f32[64,1024]{1,0:T(8,128)S(1)} collective-permute-done((f32[64,1024]{1,0:T(8,128)S(1)}, f32[64,1024]{1,0:T(8,128)S(1)}, u32[]{:S(2)}, u32[]{:S(2)}) %collective-permute-start.9) | collective-permute-done | bytes 262176 | tf_op jit(solution)/shard_map/ppermute | solution.py:326
  47.3 6.3 %collective-permute-done.8 = f32[64,1024]{1,0:T(8,128)S(1)} collective-permute-done((f32[64,1024]{1,0:T(8,128)S(1)}, f32[64,1024]{1,0:T(8,128)S(1)}, u32[]{:S(2)}, u32[]{:S(2)}) %collective-permute-start.8) | collective-permute-done | bytes 262176 | tf_op jit(solution)/shard_map/ppermute | solution.py:326
  53.6 0.1 pad_maximum_fusion.mine
  53.8 1.5 %collective-permute-start.19 = (f32[4,304,128]{2,1,0:T(8,128)S(1)}, f32[4,304,128]{2,1,0:T(8,128)S(1)}, u32[]{:S(2)}, u32[]{:S(2)}) collective-permute-start(f32[4,304,128]{2,1,0:T(8,128)S(1)} %get-tuple-element.74), channel_id=1, source_target_pairs={{0,1},{1,0},{2,3},{3,2},{4,5},{5,4},{6,7},{7,6},{8,9},{9,8},{10,11... | collective-permute-start | bytes 1867784 | tf_op jit(solution)/shard_map/ppermute | solution.py:330
  55.3 0.1 slice_bitcast_fusion.1
  55.4 2.3 %collective-permute-start.18 = (f32[368,256]{1,0:T(8,128)S(1)}, f32[368,256]{1,0:T(8,128)S(1)}, u32[]{:S(2)}, u32[]{:S(2)}) collective-permute-start(f32[368,256]{1,0:T(8,128)S(1)} %get-tuple-element.92), channel_id=1, source_target_pairs={{0,4},{1,5},{2,6},{3,7},{4,0},{5,1},{6,2},{7,3},{8,12},{9,13},{10,... | collective-permute-start | bytes 1130504 | tf_op jit(solution)/shard_map/ppermute | solution.py:283
  57.7 2.4 %collective-permute-start.17 = (f32[368,256]{1,0:T(8,128)S(1)}, f32[368,256]{1,0:T(8,128)S(1)}, u32[]{:S(2)}, u32[]{:S(2)}) collective-permute-start(f32[368,256]{1,0:T(8,128)S(1)} %get-tuple-element.94), channel_id=1, source_target_pairs={{0,6},{1,7},{2,0},{3,1},{4,2},{5,3},{6,4},{7,5},{8,14},{9,15},{10,... | collective-permute-start | bytes 1130504 | tf_op jit(solution)/shard_map/ppermute | solution.py:283
  60.1 2.7 %scores.1 = (f32[8,1024]{1,0:T(8,128)S(1)}, f32[8,1024]{1,0:T(8,128)S(1)}) custom-call(s32[4]{0:T(128)S(1)} %pad_add_fusion.idx, bf16[1024,128]{1,0:T(8,128)(2,1)} %og.1, bf16[2048,128]{1,0:T(8,128)(2,1)} %bitcast.37, f32[2048,128]{1,0:T(8,128)S(1)} %collective-permute-done.5.a1.b1, f32[2048,128]{1,0:T(8,128)S(1)} %collective-permute-done.5.a1.b1, ...), custom_call_target="tpu_custom_call" | custom-call | tf_op jit(solution)/shard_map/scores/pallas_call | solution.py:267
  62.9 1.2 %collective-permute-done.13 = f32[8,1024]{1,0:T(8,128)S(1)} collective-permute-done((f32[8,1024]{1,0:T(8,128)S(1)}, f32[8,1024]{1,0:T(8,128)S(1)}, u32[]{:S(2)}, u32[]{:S(2)}) %collective-permute-start.13) | collective-permute-done | bytes 32800 | tf_op jit(solution)/shard_map/ppermute | solution.py:334
  64.1 0.5 collective-permute-start.14
  64.6 6.4 %collective-permute-done.14 = f32[8,1024]{1,0:T(8,128)S(1)} collective-permute-done((f32[8,1024]{1,0:T(8,128)S(1)}, f32[8,1024]{1,0:T(8,128)S(1)}, u32[]{:S(2)}, u32[]{:S(2)}) %collective-permute-start.14) | collective-permute-done | bytes 32800 | tf_op jit(solution)/shard_map/ppermute | solution.py:335
  71.0 1.9 %collective-permute-start.15 = (f32[8,1024]{1,0:T(8,128)S(1)}, f32[8,1024]{1,0:T(8,128)S(1)}, u32[]{:S(2)}, u32[]{:S(2)}) collective-permute-start(f32[8,1024]{1,0:T(8,128)S(1)} %add.72), channel_id=1, source_target_pairs={{0,4},{1,5},{2,6},{3,7},{4,0},{5,1},{6,2},{7,3},{8,12},{9,13},{10,... | collective-permute-start | bytes 98312 | tf_op jit(solution)/shard_map/ppermute | solution.py:336
  72.9 4.0 %collective-permute-done.15 = f32[8,1024]{1,0:T(8,128)S(1)} collective-permute-done((f32[8,1024]{1,0:T(8,128)S(1)}, f32[8,1024]{1,0:T(8,128)S(1)}, u32[]{:S(2)}, u32[]{:S(2)}) %collective-permute-start.15) | collective-permute-done | bytes 32800 | tf_op jit(solution)/shard_map/ppermute | solution.py:336
  76.9 0.3 collective-permute-done.17.c
  77.2 1.6 %collective-permute-start.20 = (f32[8,1024]{1,0:T(8,128)S(1)}, f32[8,1024]{1,0:T(8,128)S(1)}, u32[]{:S(2)}, u32[]{:S(2)}) collective-permute-start(f32[8,1024]{1,0:T(8,128)S(1)} %add.73), channel_id=1, source_target_pairs={{0,2},{1,3},{2,0},{3,1},{4,6},{5,7},{6,4},{7,5},{8,10},{9,11},{10,... | collective-permute-start | bytes 98312 | tf_op jit(solution)/shard_map/ppermute | solution.py:340
  78.8 0.6 halves.1
  79.4 1.1 %collective-permute-start.25 = (f32[368,128]{1,0:T(8,128)S(1)}, f32[368,128]{1,0:T(8,128)S(1)}, u32[]{:S(2)}, u32[]{:S(2)}) collective-permute-start(f32[368,128]{1,0:T(8,128)S(1)} %get-tuple-element.90), channel_id=1, source_target_pairs={{0,1},{1,0},{2,3},{3,2},{4,5},{5,4},{6,7},{7,6},{8,9},{9,8},{10,11... | collective-permute-start | bytes 565256 | tf_op jit(solution)/shard_map/ppermute | solution.py:339
  80.5 0.7 collective-permute-done.20
  81.2 0.1 add.75
  81.5 2.7 %collective-permute-start.24 = (f32[656,128]{1,0:T(8,128)S(1)}, f32[656,128]{1,0:T(8,128)S(1)}, u32[]{:S(2)}, u32[]{:S(2)}) collective-permute-start(f32[656,128]{1,0:T(8,128)S(1)} %get-tuple-element.96), channel_id=1, source_target_pairs={{0,4},{1,5},{2,6},{3,7},{4,0},{5,1},{6,2},{7,3},{8,12},{9,13},{10,... | collective-permute-start | bytes 1007624 | tf_op jit(solution)/shard_map/ppermute | solution.py:283
  84.1 1.4 %collective-permute-start.22 = (f32[656,128]{1,0:T(8,128)S(1)}, f32[656,128]{1,0:T(8,128)S(1)}, u32[]{:S(2)}, u32[]{:S(2)}) collective-permute-start(f32[656,128]{1,0:T(8,128)S(1)} %get-tuple-element.97), channel_id=1, source_target_pairs={{0,2},{1,3},{2,4},{3,5},{4,6},{5,7},{6,0},{7,1},{8,10},{9,11},{10,... | collective-permute-start | bytes 1007624 | tf_op jit(solution)/shard_map/ppermute | solution.py:283
  85.5 1.8 %collective-permute-start.23 = (f32[656,128]{1,0:T(8,128)S(1)}, f32[656,128]{1,0:T(8,128)S(1)}, u32[]{:S(2)}, u32[]{:S(2)}) collective-permute-start(f32[656,128]{1,0:T(8,128)S(1)} %get-tuple-element.98), channel_id=1, source_target_pairs={{0,6},{1,7},{2,0},{3,1},{4,2},{5,3},{6,4},{7,5},{8,14},{9,15},{10,... | collective-permute-start | bytes 1007624 | tf_op jit(solution)/shard_map/ppermute | solution.py:283
  87.4 6.3 %collective-permute-start.21 = (f32[8,128]{1,0:T(8,128)S(1)}, f32[8,128]{1,0:T(8,128)S(1)}, u32[]{:S(2)}, u32[]{:S(2)}) collective-permute-start(f32[8,128]{1,0:T(8,128)S(1)} %bitcast_reduce_fusion), channel_id=1, source_target_pairs={{0,128},{64,192},{128,0},{192,64},{1,129},{65,193},{129,1},{193,65... | collective-permute-start | bytes 12296 | tf_op jit(solution)/shard_map/ppermute | solution.py:346
  93.7 1.6 %collective-permute-done.21 = f32[8,128]{1,0:T(8,128)S(1)} collective-permute-done((f32[8,128]{1,0:T(8,128)S(1)}, f32[8,128]{1,0:T(8,128)S(1)}, u32[]{:S(2)}, u32[]{:S(2)}) %collective-permute-start.21) | collective-permute-done | bytes 4128 | tf_op jit(solution)/shard_map/ppermute | solution.py:346
  95.3 2.9 %collective-permute-done.22 = f32[656,128]{1,0:T(8,128)S(1)} collective-permute-done((f32[656,128]{1,0:T(8,128)S(1)}, f32[656,128]{1,0:T(8,128)S(1)}, u32[]{:S(2)}, u32[]{:S(2)}) %collective-permute-start.22) | collective-permute-done | bytes 335904 | tf_op jit(solution)/shard_map/ppermute | solution.py:283
  98.2 0.7 collective-permute-done.23
  98.9 3.3 %collective-permute-start.26 = (f32[8,128]{1,0:T(8,128)S(1)}, f32[8,128]{1,0:T(8,128)S(1)}, u32[]{:S(2)}, u32[]{:S(2)}) collective-permute-start(f32[8,128]{1,0:T(8,128)S(1)} %add.77), channel_id=1, source_target_pairs={{0,64},{64,0},{128,192},{192,128},{1,65},{65,1},{129,193},{193,129... | collective-permute-start | bytes 12296 | tf_op jit(solution)/shard_map/ppermute | solution.py:348
  102.2 0.7 pad_maximum_fusion.2
  103.0 0.8 collective-permute-done.26
  103.8 0.1 add_reduce_fusion
  103.9 0.7 divide_bitcast_fusion
  (34 shorter events, 0.9 us)
Async XLA Ops:
  5.2 5.1 %collective-permute-start = (f32[1536,128]{1,0:T(8,128)S(1)}, f32[1536,128]{1,0:T(8,128)S(1)}, u32[]{:S(2)}, u32[]{:S(2)}) collective-permute-start(f32[1536,128]{1,0:T(8,128)S(1)} %get-tuple-element.47), channel_id=1, source_target_pairs={{0,8},{8,0},{16,24},{24,16},{32,40},{40,32},{48,56},{56,48},{1,9},... | collective-permute-start | bytes 2359304 | tf_op jit(solution)/shard_map/ppermute | solution.py:306
  5.3 30.7 %collective-permute-start.5 = (f32[2048,128]{1,0:T(8,128)S(1)}, f32[2048,128]{1,0:T(8,128)S(1)}, u32[]{:S(2)}, u32[]{:S(2)}) collective-permute-start(f32[2048,128]{1,0:T(8,128)S(1)} %get-tuple-element.48), channel_id=1, source_target_pairs={{0,16},{8,56},{16,32},{24,8},{32,48},{40,24},{48,0},{56,40},{1,17}... | collective-permute-start | bytes 3145736 | tf_op jit(solution)/shard_map/ppermute | solution.py:308
  6.8 11.2 %copy-start = (bf16[3584,1024]{1,0:T(8,128)(2,1)S(1)}, bf16[3584,1024]{1,0:T(8,128)(2,1)}, u32[]{:S(2)}) copy-start(bf16[3584,1024]{1,0:T(8,128)(2,1)} %w.1) | copy-start | bytes 22020100
  10.3 25.7 %collective-permute-start.6 = (f32[1536,128]{1,0:T(8,128)S(1)}, f32[1536,128]{1,0:T(8,128)S(1)}, u32[]{:S(2)}, u32[]{:S(2)}) collective-permute-start(f32[1536,128]{1,0:T(8,128)S(1)} %collective-permute-done), channel_id=1, source_target_pairs={{0,16},{8,56},{16,32},{24,8},{32,48},{40,24},{48,0},{56,40},{1,17}... | collective-permute-start | bytes 2359304 | tf_op jit(solution)/shard_map/ppermute | solution.py:313
  11.6 15.3 %collective-permute-start.1 = (f32[64,1024]{1,0:T(8,128)S(1)}, f32[64,1024]{1,0:T(8,128)S(1)}, u32[]{:S(2)}, u32[]{:S(2)}) collective-permute-start(f32[64,1024]{1,0:T(8,128)S(1)} %get-tuple-element.55), channel_id=1, source_target_pairs={{0,4},{1,5},{2,6},{3,7},{4,0},{5,1},{6,2},{7,3},{8,12},{9,13},{10,... | collective-permute-start | bytes 786440 | tf_op jit(solution)/shard_map/ppermute | solution.py:283
  14.8 12.6 %collective-permute-start.2 = (f32[64,1024]{1,0:T(8,128)S(1)}, f32[64,1024]{1,0:T(8,128)S(1)}, u32[]{:S(2)}, u32[]{:S(2)}) collective-permute-start(f32[64,1024]{1,0:T(8,128)S(1)} %get-tuple-element.56), channel_id=1, source_target_pairs={{0,2},{1,3},{2,4},{3,5},{4,6},{5,7},{6,0},{7,1},{8,10},{9,11},{10,... | collective-permute-start | bytes 786440 | tf_op jit(solution)/shard_map/ppermute | solution.py:283
  15.5 12.3 %collective-permute-start.3 = (f32[64,1024]{1,0:T(8,128)S(1)}, f32[64,1024]{1,0:T(8,128)S(1)}, u32[]{:S(2)}, u32[]{:S(2)}) collective-permute-start(f32[64,1024]{1,0:T(8,128)S(1)} %get-tuple-element.57), channel_id=1, source_target_pairs={{0,6},{1,7},{2,0},{3,1},{4,2},{5,3},{6,4},{7,5},{8,14},{9,15},{10,... | collective-permute-start | bytes 786440 | tf_op jit(solution)/shard_map/ppermute | solution.py:283
  27.8 8.1 %collective-permute-start.4 = (f32[64,1024]{1,0:T(8,128)S(1)}, f32[64,1024]{1,0:T(8,128)S(1)}, u32[]{:S(2)}, u32[]{:S(2)}) collective-permute-start(f32[64,1024]{1,0:T(8,128)S(1)} %add_add_fusion), channel_id=1, source_target_pairs={{0,1},{1,0},{2,3},{3,2},{4,5},{5,4},{6,7},{7,6},{8,9},{9,8},{10,11... | collective-permute-start | bytes 786440 | tf_op jit(solution)/shard_map/ppermute | solution.py:320
  36.1 17.6 %collective-permute-start.10 = (f32[1536,128]{1,0:T(8,128)S(1)}, f32[1536,128]{1,0:T(8,128)S(1)}, u32[]{:S(2)}, u32[]{:S(2)}) collective-permute-start(f32[1536,128]{1,0:T(8,128)S(1)} %slice.27), channel_id=1, source_target_pairs={{0,16},{8,56},{16,32},{24,8},{32,48},{40,24},{48,0},{56,40},{1,17}... | collective-permute-start | bytes 2359304 | tf_op jit(solution)/shard_map/ppermute | solution.py:324
  37.0 16.8 %collective-permute-start.11 = (f32[4,352,128]{2,1,0:T(8,128)S(1)}, f32[4,352,128]{2,1,0:T(8,128)S(1)}, u32[]{:S(2)}, u32[]{:S(2)}) collective-permute-start(f32[4,352,128]{2,1,0:T(8,128)S(1)} %get-tuple-element.66), channel_id=1, source_target_pairs={{0,1},{1,0},{2,3},{3,2},{4,5},{5,4},{6,7},{7,6},{8,9},{9,8},{10,11... | collective-permute-start | bytes 2162696 | tf_op jit(solution)/shard_map/ppermute | solution.py:323
  38.0 9.3 %collective-permute-start.9 = (f32[64,1024]{1,0:T(8,128)S(1)}, f32[64,1024]{1,0:T(8,128)S(1)}, u32[]{:S(2)}, u32[]{:S(2)}) collective-permute-start(f32[64,1024]{1,0:T(8,128)S(1)} %add.70), channel_id=1, source_target_pairs={{0,2},{1,3},{2,4},{3,5},{4,6},{5,7},{6,0},{7,1},{8,10},{9,11},{10,... | collective-permute-start | bytes 786440 | tf_op jit(solution)/shard_map/ppermute | solution.py:326
  39.6 14.0 %collective-permute-start.8 = (f32[64,1024]{1,0:T(8,128)S(1)}, f32[64,1024]{1,0:T(8,128)S(1)}, u32[]{:S(2)}, u32[]{:S(2)}) collective-permute-start(f32[64,1024]{1,0:T(8,128)S(1)} %add.70), channel_id=1, source_target_pairs={{0,4},{1,5},{2,6},{3,7},{4,0},{5,1},{6,2},{7,3},{8,12},{9,13},{10,... | collective-permute-start | bytes 786440 | tf_op jit(solution)/shard_map/ppermute | solution.py:326
  42.5 11.2 %collective-permute-start.7 = (f32[64,1024]{1,0:T(8,128)S(1)}, f32[64,1024]{1,0:T(8,128)S(1)}, u32[]{:S(2)}, u32[]{:S(2)}) collective-permute-start(f32[64,1024]{1,0:T(8,128)S(1)} %add.70), channel_id=1, source_target_pairs={{0,6},{1,7},{2,0},{3,1},{4,2},{5,3},{6,4},{7,5},{8,14},{9,15},{10,... | collective-permute-start | bytes 786440 | tf_op jit(solution)/shard_map/ppermute | solution.py:326
  53.7 6.4 %collective-permute-start.12 = (f32[4,64,1024]{2,1,0:T(8,128)S(1)}, f32[4,64,1024]{2,1,0:T(8,128)S(1)}, u32[]{:S(2)}, u32[]{:S(2)}) collective-permute-start(f32[4,64,1024]{2,1,0:T(8,128)S(1)} %pad_maximum_fusion.mine), channel_id=1, source_target_pairs={{0,8},{8,0},{16,24},{24,16},{32,40},{40,32},{48,56},{56,48},{1,9},... | collective-permute-start | bytes 3145736 | tf_op jit(solution)/shard_map/ppermute | solution.py:329
  53.8 23.4 %collective-permute-start.19 = (f32[4,304,128]{2,1,0:T(8,128)S(1)}, f32[4,304,128]{2,1,0:T(8,128)S(1)}, u32[]{:S(2)}, u32[]{:S(2)}) collective-permute-start(f32[4,304,128]{2,1,0:T(8,128)S(1)} %get-tuple-element.74), channel_id=1, source_target_pairs={{0,1},{1,0},{2,3},{3,2},{4,5},{5,4},{6,7},{7,6},{8,9},{9,8},{10,11... | collective-permute-start | bytes 1867784 | tf_op jit(solution)/shard_map/ppermute | solution.py:330
  55.4 21.5 %collective-permute-start.18 = (f32[368,256]{1,0:T(8,128)S(1)}, f32[368,256]{1,0:T(8,128)S(1)}, u32[]{:S(2)}, u32[]{:S(2)}) collective-permute-start(f32[368,256]{1,0:T(8,128)S(1)} %get-tuple-element.92), channel_id=1, source_target_pairs={{0,4},{1,5},{2,6},{3,7},{4,0},{5,1},{6,2},{7,3},{8,12},{9,13},{10,... | collective-permute-start | bytes 1130504 | tf_op jit(solution)/shard_map/ppermute | solution.py:283
  57.7 19.5 %collective-permute-start.17 = (f32[368,256]{1,0:T(8,128)S(1)}, f32[368,256]{1,0:T(8,128)S(1)}, u32[]{:S(2)}, u32[]{:S(2)}) collective-permute-start(f32[368,256]{1,0:T(8,128)S(1)} %get-tuple-element.94), channel_id=1, source_target_pairs={{0,6},{1,7},{2,0},{3,1},{4,2},{5,3},{6,4},{7,5},{8,14},{9,15},{10,... | collective-permute-start | bytes 1130504 | tf_op jit(solution)/shard_map/ppermute | solution.py:283
  60.1 17.1 %collective-permute-start.16 = (f32[368,256]{1,0:T(8,128)S(1)}, f32[368,256]{1,0:T(8,128)S(1)}, u32[]{:S(2)}, u32[]{:S(2)}) collective-permute-start(f32[368,256]{1,0:T(8,128)S(1)} %get-tuple-element.95), channel_id=1, source_target_pairs={{0,2},{1,3},{2,4},{3,5},{4,6},{5,7},{6,0},{7,1},{8,10},{9,11},{10,... | collective-permute-start | bytes 1130504 | tf_op jit(solution)/shard_map/ppermute | solution.py:283
  62.8 1.3 %collective-permute-start.13 = (f32[8,1024]{1,0:T(8,128)S(1)}, f32[8,1024]{1,0:T(8,128)S(1)}, u32[]{:S(2)}, u32[]{:S(2)}) collective-permute-start(f32[8,1024]{1,0:T(8,128)S(1)} %get-tuple-element.72), channel_id=1, source_target_pairs={{0,8},{8,0},{16,24},{24,16},{32,40},{40,32},{48,56},{56,48},{1,9},... | collective-permute-start | bytes 98312 | tf_op jit(solution)/shard_map/ppermute | solution.py:334
  64.1 6.9 %collective-permute-start.14 = (f32[8,1024]{1,0:T(8,128)S(1)}, f32[8,1024]{1,0:T(8,128)S(1)}, u32[]{:S(2)}, u32[]{:S(2)}) collective-permute-start(f32[8,1024]{1,0:T(8,128)S(1)} %add.71), channel_id=1, source_target_pairs={{0,1},{1,0},{2,3},{3,2},{4,5},{5,4},{6,7},{7,6},{8,9},{9,8},{10,11... | collective-permute-start | bytes 98312 | tf_op jit(solution)/shard_map/ppermute | solution.py:335
  71.0 5.9 %collective-permute-start.15 = (f32[8,1024]{1,0:T(8,128)S(1)}, f32[8,1024]{1,0:T(8,128)S(1)}, u32[]{:S(2)}, u32[]{:S(2)}) collective-permute-start(f32[8,1024]{1,0:T(8,128)S(1)} %add.72), channel_id=1, source_target_pairs={{0,4},{1,5},{2,6},{3,7},{4,0},{5,1},{6,2},{7,3},{8,12},{9,13},{10,... | collective-permute-start | bytes 98312 | tf_op jit(solution)/shard_map/ppermute | solution.py:336
  77.2 3.9 %collective-permute-start.20 = (f32[8,1024]{1,0:T(8,128)S(1)}, f32[8,1024]{1,0:T(8,128)S(1)}, u32[]{:S(2)}, u32[]{:S(2)}) collective-permute-start(f32[8,1024]{1,0:T(8,128)S(1)} %add.73), channel_id=1, source_target_pairs={{0,2},{1,3},{2,0},{3,1},{4,6},{5,7},{6,4},{7,5},{8,10},{9,11},{10,... | collective-permute-start | bytes 98312 | tf_op jit(solution)/shard_map/ppermute | solution.py:340
  79.4 15.9 %collective-permute-start.25 = (f32[368,128]{1,0:T(8,128)S(1)}, f32[368,128]{1,0:T(8,128)S(1)}, u32[]{:S(2)}, u32[]{:S(2)}) collective-permute-start(f32[368,128]{1,0:T(8,128)S(1)} %get-tuple-element.90), channel_id=1, source_target_pairs={{0,1},{1,0},{2,3},{3,2},{4,5},{5,4},{6,7},{7,6},{8,9},{9,8},{10,11... | collective-permute-start | bytes 565256 | tf_op jit(solution)/shard_map/ppermute | solution.py:339
  81.5 13.9 %collective-permute-start.24 = (f32[656,128]{1,0:T(8,128)S(1)}, f32[656,128]{1,0:T(8,128)S(1)}, u32[]{:S(2)}, u32[]{:S(2)}) collective-permute-start(f32[656,128]{1,0:T(8,128)S(1)} %get-tuple-element.96), channel_id=1, source_target_pairs={{0,4},{1,5},{2,6},{3,7},{4,0},{5,1},{6,2},{7,3},{8,12},{9,13},{10,... | collective-permute-start | bytes 1007624 | tf_op jit(solution)/shard_map/ppermute | solution.py:283
  84.1 14.1 %collective-permute-start.22 = (f32[656,128]{1,0:T(8,128)S(1)}, f32[656,128]{1,0:T(8,128)S(1)}, u32[]{:S(2)}, u32[]{:S(2)}) collective-permute-start(f32[656,128]{1,0:T(8,128)S(1)} %get-tuple-element.97), channel_id=1, source_target_pairs={{0,2},{1,3},{2,4},{3,5},{4,6},{5,7},{6,0},{7,1},{8,10},{9,11},{10,... | collective-permute-start | bytes 1007624 | tf_op jit(solution)/shard_map/ppermute | solution.py:283
  85.5 13.4 %collective-permute-start.23 = (f32[656,128]{1,0:T(8,128)S(1)}, f32[656,128]{1,0:T(8,128)S(1)}, u32[]{:S(2)}, u32[]{:S(2)}) collective-permute-start(f32[656,128]{1,0:T(8,128)S(1)} %get-tuple-element.98), channel_id=1, source_target_pairs={{0,6},{1,7},{2,0},{3,1},{4,2},{5,3},{6,4},{7,5},{8,14},{9,15},{10,... | collective-permute-start | bytes 1007624 | tf_op jit(solution)/shard_map/ppermute | solution.py:283
  87.4 7.9 %collective-permute-start.21 = (f32[8,128]{1,0:T(8,128)S(1)}, f32[8,128]{1,0:T(8,128)S(1)}, u32[]{:S(2)}, u32[]{:S(2)}) collective-permute-start(f32[8,128]{1,0:T(8,128)S(1)} %bitcast_reduce_fusion), channel_id=1, source_target_pairs={{0,128},{64,192},{128,0},{192,64},{1,129},{65,193},{129,1},{193,65... | collective-permute-start | bytes 12296 | tf_op jit(solution)/shard_map/ppermute | solution.py:346
  98.9 4.9 %collective-permute-start.26 = (f32[8,128]{1,0:T(8,128)S(1)}, f32[8,128]{1,0:T(8,128)S(1)}, u32[]{:S(2)}, u32[]{:S(2)}) collective-permute-start(f32[8,128]{1,0:T(8,128)S(1)} %add.77), channel_id=1, source_target_pairs={{0,64},{64,0},{128,192},{192,128},{1,65},{65,1},{129,193},{193,129... | collective-permute-start | bytes 12296 | tf_op jit(solution)/shard_map/ppermute | solution.py:348

commit v7 on v6

--- a/solution.py
+++ b/solution.py
@@ -319,7 +319,7 @@
     own, send0 = lax.optimization_barrier((own, send0))
     own = own + lax.ppermute(own, "tensor", z_swap())
 
-    own, send0, near0, near1 = lax.optimization_barrier((own, send0, near0, near1))
+    own, send0, near1 = lax.optimization_barrier((own, send0, near1))
     got0 = lax.ppermute(send0, "tensor", z_swap())
     far = ring(near0[gf.shape[0] // 4 :])
     mine = jnp.stack(

time: 105 us -> 104 us (level)
  no operation moved by 1% of the time
where the time goes in v7:
time: 104 us
  starting transfers between devices  44.8 us (43%)
  waiting for transfers between devices  35.9 us (35%)
  Pallas kernels  20 us (19%)
  other arithmetic  2.2 us (2%)
    ppermute x9, starting transfers between devices, send_y(): return [lax.ppermute(parts[j], 'tensor', y_shift(j)) for j in (1, 3, 2)]  17.1 us
    ppermute x3, waiting for transfers between devices, body(): lax.ppermute(own, 'tensor', y_shift(-j))  10.5 us
    pallas_call x1, Pallas kernels, layer(): pl.pallas_call(functools.partial(layer_kernel, blocks=blocks), grid_spec=...  8.81 us
    ppermute x1, waiting for transfers between devices, body(): raw = raw + lax.ppermute(raw, 'tensor', z_swap())  6.41 us
    ppermute x1, starting transfers between devices, body(): square = square + lax.ppermute(square, 'dp', dp_shift(2))  6.3 us
    ppermute x1, waiting for transfers between devices, body(): own = own + lax.ppermute(own, 'tensor', z_swap())  6 us
    ppermute x9, waiting for transfers between devices, send_y(): return [lax.ppermute(parts[j], 'tensor', y_shift(j)) for j in (1, 3, 2)]  4.85 us
    ppermute x3, starting transfers between devices, body(): lax.ppermute(own, 'tensor', y_shift(-j))  4.66 us
  transfers between devices with their start and end apart: 27, of which 14 were waited for; matrix products, arithmetic and copies ran while one was open for 1% of the time, Pallas kernels for 15%

profile of v7, /device:TPU:2, one launch (start us, length us, event | category | flops | bytes accessed | tf_op | source)
XLA Modules:
  0.0 103.9 jit_solution(13391366488498079193)
XLA Ops:
  0.7 4.4 %pack.1 = (f32[2048,128]{1,0:T(8,128)S(1)}, f32[1536,128]{1,0:T(8,128)S(1)}, bf16[1024,3584]{1,0:T(8,128)(2,1)S(1)}, bf16[256,3584]{1,0:T(8,128)(2,1)S(1)}, f32[8,32]{1,0:T(8,128)S(1)}) custom-call(s32[4]{0:T(128)S(1)} %pad_add_fusion.idx, bf16[1024,128]{1,0:T(8,128)(2,1)} %og.1, bf16[2048,128]{1,0:T(8,128)(2,1)} %bitcast.36, bf16[1024,3584]{1,0:T(8,128)(2,1)} %refs_0_.1, ...), custom_call_target="tpu_custom_call" | custom-call | bytes 41943040 | tf_op jit(solution)/shard_map/pack/pallas_call | solution.py:93
  5.2 0.1 collective-permute-start.1
  5.3 1.6 %collective-permute-start = (f32[2048,128]{1,0:T(8,128)S(1)}, f32[2048,128]{1,0:T(8,128)S(1)}, u32[]{:S(2)}, u32[]{:S(2)}) collective-permute-start(f32[2048,128]{1,0:T(8,128)S(1)} %get-tuple-element.46), channel_id=1, source_target_pairs={{0,16},{8,56},{16,32},{24,8},{32,48},{40,24},{48,0},{56,40},{1,17}... | collective-permute-start | bytes 3145736 | tf_op jit(solution)/shard_map/ppermute | solution.py:308
  6.9 3.4 %act.1 = (f32[64,1024]{1,0:T(8,128)S(1)}, f32[64,1024]{1,0:T(8,128)S(1)}, f32[64,1024]{1,0:T(8,128)S(1)}, f32[64,1024]{1,0:T(8,128)S(1)}) custom-call(s32[4]{0:T(128)S(1)} %pad_add_fusion.idx, f32[8,32]{1,0:T(8,128)S(1)} %get-tuple-element.49.weight, bf16[256,3584]{1,0:T(8,128)(2,1)S(1)} %get-tuple-element.50.af, bf16[1024,3584]{1,0:T(8,128)(2,1)S(1)} %get-tuple-element.51.a), custom_call_target="tpu_custom_call" | custom-call | bytes 20971520 | tf_op jit(solution)/shard_map/act/pallas_call | solution.py:146
  10.3 1.3 %collective-permute-start.6 = (f32[1536,128]{1,0:T(8,128)S(1)}, f32[1536,128]{1,0:T(8,128)S(1)}, u32[]{:S(2)}, u32[]{:S(2)}) collective-permute-start(f32[1536,128]{1,0:T(8,128)S(1)} %collective-permute-done.1), channel_id=1, source_target_pairs={{0,16},{8,56},{16,32},{24,8},{32,48},{40,24},{48,0},{56,40},{1,17}... | collective-permute-start | bytes 2359304 | tf_op jit(solution)/shard_map/ppermute | solution.py:313
  11.6 3.2 %collective-permute-start.2 = (f32[64,1024]{1,0:T(8,128)S(1)}, f32[64,1024]{1,0:T(8,128)S(1)}, u32[]{:S(2)}, u32[]{:S(2)}) collective-permute-start(f32[64,1024]{1,0:T(8,128)S(1)} %get-tuple-element.54), channel_id=1, source_target_pairs={{0,4},{1,5},{2,6},{3,7},{4,0},{5,1},{6,2},{7,3},{8,12},{9,13},{10,... | collective-permute-start | bytes 786440 | tf_op jit(solution)/shard_map/ppermute | solution.py:283
  14.8 0.7 collective-permute-start.3
  15.5 2.6 %collective-permute-start.4 = (f32[64,1024]{1,0:T(8,128)S(1)}, f32[64,1024]{1,0:T(8,128)S(1)}, u32[]{:S(2)}, u32[]{:S(2)}) collective-permute-start(f32[64,1024]{1,0:T(8,128)S(1)} %get-tuple-element.56), channel_id=1, source_target_pairs={{0,6},{1,7},{2,0},{3,1},{4,2},{5,3},{6,4},{7,5},{8,14},{9,15},{10,... | collective-permute-start | bytes 786440 | tf_op jit(solution)/shard_map/ppermute | solution.py:283
  18.0 8.8 %layer.1 = (f32[4,352,128]{2,1,0:T(8,128)S(1)}, f32[4,352,128]{2,1,0:T(8,128)S(1)}, f32[4,304,128]{2,1,0:T(8,128)S(1)}, f32[4,304,128]{2,1,0:T(8,128)S(1)}, f32[4,368,256]{2,1,0:T(8,128)S(1)}) custom-call(s32[4]{0:T(128)S(1)} %pad_add_fusion.idx, bf16[1024,3584]{1,0:T(8,128)(2,1)S(1)} %get-tuple-element.51.a, bf16[3584,1024]{1,0:T(8,128)(2,1)S(1)} %copy-done), custom_call_target="tpu_custom_call" | custom-call | tf_op jit(solution)/shard_map/layer/pallas_call | solution.py:187
  26.8 0.5 collective-permute-done.3
  27.4 0.4 collective-permute-done.4
  27.8 2.0 %collective-permute-start.5 = (f32[64,1024]{1,0:T(8,128)S(1)}, f32[64,1024]{1,0:T(8,128)S(1)}, u32[]{:S(2)}, u32[]{:S(2)}) collective-permute-start(f32[64,1024]{1,0:T(8,128)S(1)} %add_add_fusion), channel_id=1, source_target_pairs={{0,1},{1,0},{2,3},{3,2},{4,5},{5,4},{6,7},{7,6},{8,9},{9,8},{10,11... | collective-permute-start | bytes 786440 | tf_op jit(solution)/shard_map/ppermute | solution.py:320
  30.0 6.0 %collective-permute-done.5 = f32[64,1024]{1,0:T(8,128)S(1)} collective-permute-done((f32[64,1024]{1,0:T(8,128)S(1)}, f32[64,1024]{1,0:T(8,128)S(1)}, u32[]{:S(2)}, u32[]{:S(2)}) %collective-permute-start.5) | collective-permute-done | bytes 262176 | tf_op jit(solution)/shard_map/ppermute | solution.py:320
  36.0 1.8 %collective-permute-start.11 = (f32[4,352,128]{2,1,0:T(8,128)S(1)}, f32[4,352,128]{2,1,0:T(8,128)S(1)}, u32[]{:S(2)}, u32[]{:S(2)}) collective-permute-start(f32[4,352,128]{2,1,0:T(8,128)S(1)} %get-tuple-element.64), channel_id=1, source_target_pairs={{0,1},{1,0},{2,3},{3,2},{4,5},{5,4},{6,7},{7,6},{8,9},{9,8},{10,11... | collective-permute-start | bytes 2162696 | tf_op jit(solution)/shard_map/ppermute | solution.py:323
  37.9 1.6 %collective-permute-start.9 = (f32[64,1024]{1,0:T(8,128)S(1)}, f32[64,1024]{1,0:T(8,128)S(1)}, u32[]{:S(2)}, u32[]{:S(2)}) collective-permute-start(f32[64,1024]{1,0:T(8,128)S(1)} %add.70), channel_id=1, source_target_pairs={{0,2},{1,3},{2,4},{3,5},{4,6},{5,7},{6,0},{7,1},{8,10},{9,11},{10,... | collective-permute-start | bytes 786440 | tf_op jit(solution)/shard_map/ppermute | solution.py:326
  39.4 2.9 %collective-permute-start.8 = (f32[64,1024]{1,0:T(8,128)S(1)}, f32[64,1024]{1,0:T(8,128)S(1)}, u32[]{:S(2)}, u32[]{:S(2)}) collective-permute-start(f32[64,1024]{1,0:T(8,128)S(1)} %add.70), channel_id=1, source_target_pairs={{0,4},{1,5},{2,6},{3,7},{4,0},{5,1},{6,2},{7,3},{8,12},{9,13},{10,... | collective-permute-start | bytes 786440 | tf_op jit(solution)/shard_map/ppermute | solution.py:326
  42.3 0.2 collective-permute-start.7
  42.5 4.6 %collective-permute-done.9 = f32[64,1024]{1,0:T(8,128)S(1)} collective-permute-done((f32[64,1024]{1,0:T(8,128)S(1)}, f32[64,1024]{1,0:T(8,128)S(1)}, u32[]{:S(2)}, u32[]{:S(2)}) %collective-permute-start.9) | collective-permute-done | bytes 262176 | tf_op jit(solution)/shard_map/ppermute | solution.py:326
  47.1 5.8 %collective-permute-done.8 = f32[64,1024]{1,0:T(8,128)S(1)} collective-permute-done((f32[64,1024]{1,0:T(8,128)S(1)}, f32[64,1024]{1,0:T(8,128)S(1)}, u32[]{:S(2)}, u32[]{:S(2)}) %collective-permute-start.8) | collective-permute-done | bytes 262176 | tf_op jit(solution)/shard_map/ppermute | solution.py:326
  53.0 0.1 pad_maximum_fusion.mine
  53.2 1.5 %collective-permute-start.19 = (f32[4,304,128]{2,1,0:T(8,128)S(1)}, f32[4,304,128]{2,1,0:T(8,128)S(1)}, u32[]{:S(2)}, u32[]{:S(2)}) collective-permute-start(f32[4,304,128]{2,1,0:T(8,128)S(1)} %get-tuple-element.72), channel_id=1, source_target_pairs={{0,1},{1,0},{2,3},{3,2},{4,5},{5,4},{6,7},{7,6},{8,9},{9,8},{10,11... | collective-permute-start | bytes 1867784 | tf_op jit(solution)/shard_map/ppermute | solution.py:330
  54.7 0.1 slice_bitcast_fusion.1
  54.8 2.3 %collective-permute-start.18 = (f32[368,256]{1,0:T(8,128)S(1)}, f32[368,256]{1,0:T(8,128)S(1)}, u32[]{:S(2)}, u32[]{:S(2)}) collective-permute-start(f32[368,256]{1,0:T(8,128)S(1)} %get-tuple-element.90), channel_id=1, source_target_pairs={{0,4},{1,5},{2,6},{3,7},{4,0},{5,1},{6,2},{7,3},{8,12},{9,13},{10,... | collective-permute-start | bytes 1130504 | tf_op jit(solution)/shard_map/ppermute | solution.py:283
  57.1 2.4 %collective-permute-start.17 = (f32[368,256]{1,0:T(8,128)S(1)}, f32[368,256]{1,0:T(8,128)S(1)}, u32[]{:S(2)}, u32[]{:S(2)}) collective-permute-start(f32[368,256]{1,0:T(8,128)S(1)} %get-tuple-element.92), channel_id=1, source_target_pairs={{0,6},{1,7},{2,0},{3,1},{4,2},{5,3},{6,4},{7,5},{8,14},{9,15},{10,... | collective-permute-start | bytes 1130504 | tf_op jit(solution)/shard_map/ppermute | solution.py:283
  59.5 2.7 %scores.1 = (f32[8,1024]{1,0:T(8,128)S(1)}, f32[8,1024]{1,0:T(8,128)S(1)}) custom-call(s32[4]{0:T(128)S(1)} %pad_add_fusion.idx, bf16[1024,128]{1,0:T(8,128)(2,1)} %og.1, bf16[2048,128]{1,0:T(8,128)(2,1)} %bitcast.37, f32[2048,128]{1,0:T(8,128)S(1)} %collective-permute-done.a1.b1, f32[2048,128]{1,0:T(8,128)S(1)} %collective-permute-done.a1.b1, ...), custom_call_target="tpu_custom_call" | custom-call | tf_op jit(solution)/shard_map/scores/pallas_call | solution.py:267
  62.3 1.2 %collective-permute-done.13 = f32[8,1024]{1,0:T(8,128)S(1)} collective-permute-done((f32[8,1024]{1,0:T(8,128)S(1)}, f32[8,1024]{1,0:T(8,128)S(1)}, u32[]{:S(2)}, u32[]{:S(2)}) %collective-permute-start.13) | collective-permute-done | bytes 32800 | tf_op jit(solution)/shard_map/ppermute | solution.py:334
  63.5 0.5 collective-permute-start.14
  64.0 6.4 %collective-permute-done.14 = f32[8,1024]{1,0:T(8,128)S(1)} collective-permute-done((f32[8,1024]{1,0:T(8,128)S(1)}, f32[8,1024]{1,0:T(8,128)S(1)}, u32[]{:S(2)}, u32[]{:S(2)}) %collective-permute-start.14) | collective-permute-done | bytes 32800 | tf_op jit(solution)/shard_map/ppermute | solution.py:335
  70.4 1.9 %collective-permute-start.15 = (f32[8,1024]{1,0:T(8,128)S(1)}, f32[8,1024]{1,0:T(8,128)S(1)}, u32[]{:S(2)}, u32[]{:S(2)}) collective-permute-start(f32[8,1024]{1,0:T(8,128)S(1)} %add.72), channel_id=1, source_target_pairs={{0,4},{1,5},{2,6},{3,7},{4,0},{5,1},{6,2},{7,3},{8,12},{9,13},{10,... | collective-permute-start | bytes 98312 | tf_op jit(solution)/shard_map/ppermute | solution.py:336
  72.3 4.0 %collective-permute-done.15 = f32[8,1024]{1,0:T(8,128)S(1)} collective-permute-done((f32[8,1024]{1,0:T(8,128)S(1)}, f32[8,1024]{1,0:T(8,128)S(1)}, u32[]{:S(2)}, u32[]{:S(2)}) %collective-permute-start.15) | collective-permute-done | bytes 32800 | tf_op jit(solution)/shard_map/ppermute | solution.py:336
  76.3 0.3 collective-permute-done.17.c
  76.6 1.6 %collective-permute-start.20 = (f32[8,1024]{1,0:T(8,128)S(1)}, f32[8,1024]{1,0:T(8,128)S(1)}, u32[]{:S(2)}, u32[]{:S(2)}) collective-permute-start(f32[8,1024]{1,0:T(8,128)S(1)} %add.73), channel_id=1, source_target_pairs={{0,2},{1,3},{2,0},{3,1},{4,6},{5,7},{6,4},{7,5},{8,10},{9,11},{10,... | collective-permute-start | bytes 98312 | tf_op jit(solution)/shard_map/ppermute | solution.py:340
  78.2 0.6 halves.1
  78.8 1.1 %collective-permute-start.25 = (f32[368,128]{1,0:T(8,128)S(1)}, f32[368,128]{1,0:T(8,128)S(1)}, u32[]{:S(2)}, u32[]{:S(2)}) collective-permute-start(f32[368,128]{1,0:T(8,128)S(1)} %get-tuple-element.88), channel_id=1, source_target_pairs={{0,1},{1,0},{2,3},{3,2},{4,5},{5,4},{6,7},{7,6},{8,9},{9,8},{10,11... | collective-permute-start | bytes 565256 | tf_op jit(solution)/shard_map/ppermute | solution.py:339
  79.9 0.7 collective-permute-done.20
  80.6 0.1 add.76
  80.8 2.7 %collective-permute-start.24 = (f32[656,128]{1,0:T(8,128)S(1)}, f32[656,128]{1,0:T(8,128)S(1)}, u32[]{:S(2)}, u32[]{:S(2)}) collective-permute-start(f32[656,128]{1,0:T(8,128)S(1)} %get-tuple-element.94), channel_id=1, source_target_pairs={{0,4},{1,5},{2,6},{3,7},{4,0},{5,1},{6,2},{7,3},{8,12},{9,13},{10,... | collective-permute-start | bytes 1007624 | tf_op jit(solution)/shard_map/ppermute | solution.py:283
  83.5 1.4 %collective-permute-start.22 = (f32[656,128]{1,0:T(8,128)S(1)}, f32[656,128]{1,0:T(8,128)S(1)}, u32[]{:S(2)}, u32[]{:S(2)}) collective-permute-start(f32[656,128]{1,0:T(8,128)S(1)} %get-tuple-element.95), channel_id=1, source_target_pairs={{0,2},{1,3},{2,4},{3,5},{4,6},{5,7},{6,0},{7,1},{8,10},{9,11},{10,... | collective-permute-start | bytes 1007624 | tf_op jit(solution)/shard_map/ppermute | solution.py:283
  84.9 1.8 %collective-permute-start.23 = (f32[656,128]{1,0:T(8,128)S(1)}, f32[656,128]{1,0:T(8,128)S(1)}, u32[]{:S(2)}, u32[]{:S(2)}) collective-permute-start(f32[656,128]{1,0:T(8,128)S(1)} %get-tuple-element.96), channel_id=1, source_target_pairs={{0,6},{1,7},{2,0},{3,1},{4,2},{5,3},{6,4},{7,5},{8,14},{9,15},{10,... | collective-permute-start | bytes 1007624 | tf_op jit(solution)/shard_map/ppermute | solution.py:283
  86.7 6.3 %collective-permute-start.21 = (f32[8,128]{1,0:T(8,128)S(1)}, f32[8,128]{1,0:T(8,128)S(1)}, u32[]{:S(2)}, u32[]{:S(2)}) collective-permute-start(f32[8,128]{1,0:T(8,128)S(1)} %bitcast_reduce_fusion), channel_id=1, source_target_pairs={{0,128},{64,192},{128,0},{192,64},{1,129},{65,193},{129,1},{193,65... | collective-permute-start | bytes 12296 | tf_op jit(solution)/shard_map/ppermute | solution.py:346
  93.0 1.6 %collective-permute-done.21 = f32[8,128]{1,0:T(8,128)S(1)} collective-permute-done((f32[8,128]{1,0:T(8,128)S(1)}, f32[8,128]{1,0:T(8,128)S(1)}, u32[]{:S(2)}, u32[]{:S(2)}) %collective-permute-start.21) | collective-permute-done | bytes 4128 | tf_op jit(solution)/shard_map/ppermute | solution.py:346
  94.6 2.9 %collective-permute-done.22 = f32[656,128]{1,0:T(8,128)S(1)} collective-permute-done((f32[656,128]{1,0:T(8,128)S(1)}, f32[656,128]{1,0:T(8,128)S(1)}, u32[]{:S(2)}, u32[]{:S(2)}) %collective-permute-start.22) | collective-permute-done | bytes 335904 | tf_op jit(solution)/shard_map/ppermute | solution.py:283
  97.5 0.7 collective-permute-done.23
  98.2 3.3 %collective-permute-start.26 = (f32[8,128]{1,0:T(8,128)S(1)}, f32[8,128]{1,0:T(8,128)S(1)}, u32[]{:S(2)}, u32[]{:S(2)}) collective-permute-start(f32[8,128]{1,0:T(8,128)S(1)} %add.77), channel_id=1, source_target_pairs={{0,64},{64,0},{128,192},{192,128},{1,65},{65,1},{129,193},{193,129... | collective-permute-start | bytes 12296 | tf_op jit(solution)/shard_map/ppermute | solution.py:348
  101.6 0.7 pad_maximum_fusion.2
  102.3 0.8 collective-permute-done.26
  103.1 0.1 add_reduce_fusion
  103.2 0.7 divide_bitcast_fusion
  (34 shorter events, 0.8 us)
Async XLA Ops:
  5.2 5.1 %collective-permute-start.1 = (f32[1536,128]{1,0:T(8,128)S(1)}, f32[1536,128]{1,0:T(8,128)S(1)}, u32[]{:S(2)}, u32[]{:S(2)}) collective-permute-start(f32[1536,128]{1,0:T(8,128)S(1)} %get-tuple-element.47), channel_id=1, source_target_pairs={{0,8},{8,0},{16,24},{24,16},{32,40},{40,32},{48,56},{56,48},{1,9},... | collective-permute-start | bytes 2359304 | tf_op jit(solution)/shard_map/ppermute | solution.py:306
  5.3 24.6 %collective-permute-start = (f32[2048,128]{1,0:T(8,128)S(1)}, f32[2048,128]{1,0:T(8,128)S(1)}, u32[]{:S(2)}, u32[]{:S(2)}) collective-permute-start(f32[2048,128]{1,0:T(8,128)S(1)} %get-tuple-element.46), channel_id=1, source_target_pairs={{0,16},{8,56},{16,32},{24,8},{32,48},{40,24},{48,0},{56,40},{1,17}... | collective-permute-start | bytes 3145736 | tf_op jit(solution)/shard_map/ppermute | solution.py:308
  6.8 11.2 %copy-start = (bf16[3584,1024]{1,0:T(8,128)(2,1)S(1)}, bf16[3584,1024]{1,0:T(8,128)(2,1)}, u32[]{:S(2)}) copy-start(bf16[3584,1024]{1,0:T(8,128)(2,1)} %w.1) | copy-start | bytes 22020100
  10.3 25.7 %collective-permute-start.6 = (f32[1536,128]{1,0:T(8,128)S(1)}, f32[1536,128]{1,0:T(8,128)S(1)}, u32[]{:S(2)}, u32[]{:S(2)}) collective-permute-start(f32[1536,128]{1,0:T(8,128)S(1)} %collective-permute-done.1), channel_id=1, source_target_pairs={{0,16},{8,56},{16,32},{24,8},{32,48},{40,24},{48,0},{56,40},{1,17}... | collective-permute-start | bytes 2359304 | tf_op jit(solution)/shard_map/ppermute | solution.py:313
  11.6 15.3 %collective-permute-start.2 = (f32[64,1024]{1,0:T(8,128)S(1)}, f32[64,1024]{1,0:T(8,128)S(1)}, u32[]{:S(2)}, u32[]{:S(2)}) collective-permute-start(f32[64,1024]{1,0:T(8,128)S(1)} %get-tuple-element.54), channel_id=1, source_target_pairs={{0,4},{1,5},{2,6},{3,7},{4,0},{5,1},{6,2},{7,3},{8,12},{9,13},{10,... | collective-permute-start | bytes 786440 | tf_op jit(solution)/shard_map/ppermute | solution.py:283
  14.8 12.6 %collective-permute-start.3 = (f32[64,1024]{1,0:T(8,128)S(1)}, f32[64,1024]{1,0:T(8,128)S(1)}, u32[]{:S(2)}, u32[]{:S(2)}) collective-permute-start(f32[64,1024]{1,0:T(8,128)S(1)} %get-tuple-element.55), channel_id=1, source_target_pairs={{0,2},{1,3},{2,4},{3,5},{4,6},{5,7},{6,0},{7,1},{8,10},{9,11},{10,... | collective-permute-start | bytes 786440 | tf_op jit(solution)/shard_map/ppermute | solution.py:283
  15.5 12.3 %collective-permute-start.4 = (f32[64,1024]{1,0:T(8,128)S(1)}, f32[64,1024]{1,0:T(8,128)S(1)}, u32[]{:S(2)}, u32[]{:S(2)}) collective-permute-start(f32[64,1024]{1,0:T(8,128)S(1)} %get-tuple-element.56), channel_id=1, source_target_pairs={{0,6},{1,7},{2,0},{3,1},{4,2},{5,3},{6,4},{7,5},{8,14},{9,15},{10,... | collective-permute-start | bytes 786440 | tf_op jit(solution)/shard_map/ppermute | solution.py:283
  27.8 8.1 %collective-permute-start.5 = (f32[64,1024]{1,0:T(8,128)S(1)}, f32[64,1024]{1,0:T(8,128)S(1)}, u32[]{:S(2)}, u32[]{:S(2)}) collective-permute-start(f32[64,1024]{1,0:T(8,128)S(1)} %add_add_fusion), channel_id=1, source_target_pairs={{0,1},{1,0},{2,3},{3,2},{4,5},{5,4},{6,7},{7,6},{8,9},{9,8},{10,11... | collective-permute-start | bytes 786440 | tf_op jit(solution)/shard_map/ppermute | solution.py:320
  29.9 23.2 %collective-permute-start.10 = (f32[1536,128]{1,0:T(8,128)S(1)}, f32[1536,128]{1,0:T(8,128)S(1)}, u32[]{:S(2)}, u32[]{:S(2)}) collective-permute-start(f32[1536,128]{1,0:T(8,128)S(1)} %slice.36), channel_id=1, source_target_pairs={{0,16},{8,56},{16,32},{24,8},{32,48},{40,24},{48,0},{56,40},{1,17}... | collective-permute-start | bytes 2359304 | tf_op jit(solution)/shard_map/ppermute | solution.py:324
  36.0 17.1 %collective-permute-start.11 = (f32[4,352,128]{2,1,0:T(8,128)S(1)}, f32[4,352,128]{2,1,0:T(8,128)S(1)}, u32[]{:S(2)}, u32[]{:S(2)}) collective-permute-start(f32[4,352,128]{2,1,0:T(8,128)S(1)} %get-tuple-element.64), channel_id=1, source_target_pairs={{0,1},{1,0},{2,3},{3,2},{4,5},{5,4},{6,7},{7,6},{8,9},{9,8},{10,11... | collective-permute-start | bytes 2162696 | tf_op jit(solution)/shard_map/ppermute | solution.py:323
  37.9 9.3 %collective-permute-start.9 = (f32[64,1024]{1,0:T(8,128)S(1)}, f32[64,1024]{1,0:T(8,128)S(1)}, u32[]{:S(2)}, u32[]{:S(2)}) collective-permute-start(f32[64,1024]{1,0:T(8,128)S(1)} %add.70), channel_id=1, source_target_pairs={{0,2},{1,3},{2,4},{3,5},{4,6},{5,7},{6,0},{7,1},{8,10},{9,11},{10,... | collective-permute-start | bytes 786440 | tf_op jit(solution)/shard_map/ppermute | solution.py:326
  39.4 13.6 %collective-permute-start.8 = (f32[64,1024]{1,0:T(8,128)S(1)}, f32[64,1024]{1,0:T(8,128)S(1)}, u32[]{:S(2)}, u32[]{:S(2)}) collective-permute-start(f32[64,1024]{1,0:T(8,128)S(1)} %add.70), channel_id=1, source_target_pairs={{0,4},{1,5},{2,6},{3,7},{4,0},{5,1},{6,2},{7,3},{8,12},{9,13},{10,... | collective-permute-start | bytes 786440 | tf_op jit(solution)/shard_map/ppermute | solution.py:326
  42.3 10.7 %collective-permute-start.7 = (f32[64,1024]{1,0:T(8,128)S(1)}, f32[64,1024]{1,0:T(8,128)S(1)}, u32[]{:S(2)}, u32[]{:S(2)}) collective-permute-start(f32[64,1024]{1,0:T(8,128)S(1)} %add.70), channel_id=1, source_target_pairs={{0,6},{1,7},{2,0},{3,1},{4,2},{5,3},{6,4},{7,5},{8,14},{9,15},{10,... | collective-permute-start | bytes 786440 | tf_op jit(solution)/shard_map/ppermute | solution.py:326
  53.1 6.4 %collective-permute-start.12 = (f32[4,64,1024]{2,1,0:T(8,128)S(1)}, f32[4,64,1024]{2,1,0:T(8,128)S(1)}, u32[]{:S(2)}, u32[]{:S(2)}) collective-permute-start(f32[4,64,1024]{2,1,0:T(8,128)S(1)} %pad_maximum_fusion.mine), channel_id=1, source_target_pairs={{0,8},{8,0},{16,24},{24,16},{32,40},{40,32},{48,56},{56,48},{1,9},... | collective-permute-start | bytes 3145736 | tf_op jit(solution)/shard_map/ppermute | solution.py:329
  53.2 23.4 %collective-permute-start.19 = (f32[4,304,128]{2,1,0:T(8,128)S(1)}, f32[4,304,128]{2,1,0:T(8,128)S(1)}, u32[]{:S(2)}, u32[]{:S(2)}) collective-permute-start(f32[4,304,128]{2,1,0:T(8,128)S(1)} %get-tuple-element.72), channel_id=1, source_target_pairs={{0,1},{1,0},{2,3},{3,2},{4,5},{5,4},{6,7},{7,6},{8,9},{9,8},{10,11... | collective-permute-start | bytes 1867784 | tf_op jit(solution)/shard_map/ppermute | solution.py:330
  54.8 21.5 %collective-permute-start.18 = (f32[368,256]{1,0:T(8,128)S(1)}, f32[368,256]{1,0:T(8,128)S(1)}, u32[]{:S(2)}, u32[]{:S(2)}) collective-permute-start(f32[368,256]{1,0:T(8,128)S(1)} %get-tuple-element.90), channel_id=1, source_target_pairs={{0,4},{1,5},{2,6},{3,7},{4,0},{5,1},{6,2},{7,3},{8,12},{9,13},{10,... | collective-permute-start | bytes 1130504 | tf_op jit(solution)/shard_map/ppermute | solution.py:283
  57.1 19.5 %collective-permute-start.17 = (f32[368,256]{1,0:T(8,128)S(1)}, f32[368,256]{1,0:T(8,128)S(1)}, u32[]{:S(2)}, u32[]{:S(2)}) collective-permute-start(f32[368,256]{1,0:T(8,128)S(1)} %get-tuple-element.92), channel_id=1, source_target_pairs={{0,6},{1,7},{2,0},{3,1},{4,2},{5,3},{6,4},{7,5},{8,14},{9,15},{10,... | collective-permute-start | bytes 1130504 | tf_op jit(solution)/shard_map/ppermute | solution.py:283
  59.5 17.1 %collective-permute-start.16 = (f32[368,256]{1,0:T(8,128)S(1)}, f32[368,256]{1,0:T(8,128)S(1)}, u32[]{:S(2)}, u32[]{:S(2)}) collective-permute-start(f32[368,256]{1,0:T(8,128)S(1)} %get-tuple-element.93), channel_id=1, source_target_pairs={{0,2},{1,3},{2,4},{3,5},{4,6},{5,7},{6,0},{7,1},{8,10},{9,11},{10,... | collective-permute-start | bytes 1130504 | tf_op jit(solution)/shard_map/ppermute | solution.py:283
  62.2 1.3 %collective-permute-start.13 = (f32[8,1024]{1,0:T(8,128)S(1)}, f32[8,1024]{1,0:T(8,128)S(1)}, u32[]{:S(2)}, u32[]{:S(2)}) collective-permute-start(f32[8,1024]{1,0:T(8,128)S(1)} %get-tuple-element.70), channel_id=1, source_target_pairs={{0,8},{8,0},{16,24},{24,16},{32,40},{40,32},{48,56},{56,48},{1,9},... | collective-permute-start | bytes 98312 | tf_op jit(solution)/shard_map/ppermute | solution.py:334
  63.5 6.9 %collective-permute-start.14 = (f32[8,1024]{1,0:T(8,128)S(1)}, f32[8,1024]{1,0:T(8,128)S(1)}, u32[]{:S(2)}, u32[]{:S(2)}) collective-permute-start(f32[8,1024]{1,0:T(8,128)S(1)} %add.71), channel_id=1, source_target_pairs={{0,1},{1,0},{2,3},{3,2},{4,5},{5,4},{6,7},{7,6},{8,9},{9,8},{10,11... | collective-permute-start | bytes 98312 | tf_op jit(solution)/shard_map/ppermute | solution.py:335
  70.4 5.9 %collective-permute-start.15 = (f32[8,1024]{1,0:T(8,128)S(1)}, f32[8,1024]{1,0:T(8,128)S(1)}, u32[]{:S(2)}, u32[]{:S(2)}) collective-permute-start(f32[8,1024]{1,0:T(8,128)S(1)} %add.72), channel_id=1, source_target_pairs={{0,4},{1,5},{2,6},{3,7},{4,0},{5,1},{6,2},{7,3},{8,12},{9,13},{10,... | collective-permute-start | bytes 98312 | tf_op jit(solution)/shard_map/ppermute | solution.py:336
  76.6 3.9 %collective-permute-start.20 = (f32[8,1024]{1,0:T(8,128)S(1)}, f32[8,1024]{1,0:T(8,128)S(1)}, u32[]{:S(2)}, u32[]{:S(2)}) collective-permute-start(f32[8,1024]{1,0:T(8,128)S(1)} %add.73), channel_id=1, source_target_pairs={{0,2},{1,3},{2,0},{3,1},{4,6},{5,7},{6,4},{7,5},{8,10},{9,11},{10,... | collective-permute-start | bytes 98312 | tf_op jit(solution)/shard_map/ppermute | solution.py:340
  78.8 15.8 %collective-permute-start.25 = (f32[368,128]{1,0:T(8,128)S(1)}, f32[368,128]{1,0:T(8,128)S(1)}, u32[]{:S(2)}, u32[]{:S(2)}) collective-permute-start(f32[368,128]{1,0:T(8,128)S(1)} %get-tuple-element.88), channel_id=1, source_target_pairs={{0,1},{1,0},{2,3},{3,2},{4,5},{5,4},{6,7},{7,6},{8,9},{9,8},{10,11... | collective-permute-start | bytes 565256 | tf_op jit(solution)/shard_map/ppermute | solution.py:339
  80.8 13.8 %collective-permute-start.24 = (f32[656,128]{1,0:T(8,128)S(1)}, f32[656,128]{1,0:T(8,128)S(1)}, u32[]{:S(2)}, u32[]{:S(2)}) collective-permute-start(f32[656,128]{1,0:T(8,128)S(1)} %get-tuple-element.94), channel_id=1, source_target_pairs={{0,4},{1,5},{2,6},{3,7},{4,0},{5,1},{6,2},{7,3},{8,12},{9,13},{10,... | collective-permute-start | bytes 1007624 | tf_op jit(solution)/shard_map/ppermute | solution.py:283
  83.5 14.1 %collective-permute-start.22 = (f32[656,128]{1,0:T(8,128)S(1)}, f32[656,128]{1,0:T(8,128)S(1)}, u32[]{:S(2)}, u32[]{:S(2)}) collective-permute-start(f32[656,128]{1,0:T(8,128)S(1)} %get-tuple-element.95), channel_id=1, source_target_pairs={{0,2},{1,3},{2,4},{3,5},{4,6},{5,7},{6,0},{7,1},{8,10},{9,11},{10,... | collective-permute-start | bytes 1007624 | tf_op jit(solution)/shard_map/ppermute | solution.py:283
  84.9 13.4 %collective-permute-start.23 = (f32[656,128]{1,0:T(8,128)S(1)}, f32[656,128]{1,0:T(8,128)S(1)}, u32[]{:S(2)}, u32[]{:S(2)}) collective-permute-start(f32[656,128]{1,0:T(8,128)S(1)} %get-tuple-element.96), channel_id=1, source_target_pairs={{0,6},{1,7},{2,0},{3,1},{4,2},{5,3},{6,4},{7,5},{8,14},{9,15},{10,... | collective-permute-start | bytes 1007624 | tf_op jit(solution)/shard_map/ppermute | solution.py:283
  86.7 7.9 %collective-permute-start.21 = (f32[8,128]{1,0:T(8,128)S(1)}, f32[8,128]{1,0:T(8,128)S(1)}, u32[]{:S(2)}, u32[]{:S(2)}) collective-permute-start(f32[8,128]{1,0:T(8,128)S(1)} %bitcast_reduce_fusion), channel_id=1, source_target_pairs={{0,128},{64,192},{128,0},{192,64},{1,129},{65,193},{129,1},{193,65... | collective-permute-start | bytes 12296 | tf_op jit(solution)/shard_map/ppermute | solution.py:346
  98.2 4.9 %collective-permute-start.26 = (f32[8,128]{1,0:T(8,128)S(1)}, f32[8,128]{1,0:T(8,128)S(1)}, u32[]{:S(2)}, u32[]{:S(2)}) collective-permute-start(f32[8,128]{1,0:T(8,128)S(1)} %add.77), channel_id=1, source_target_pairs={{0,64},{64,0},{128,192},{192,128},{1,65},{65,1},{129,193},{193,129... | collective-permute-start | bytes 12296 | tf_op jit(solution)/shard_map/ppermute | solution.py:348
